TPU v7x, 768 devices: a whole 4x8x12 slice. The times are simulated.
768 devices in a mesh: sub: 48 (over z, x_hi, core), blk: 16 (over x_lo, y).
Axes of the slice: x: 4 (x_hi: 2, x_lo: 2; x = x_hi * 2 + x_lo), y: 8, z: 12, core: 2. Of those that a mesh axis runs over, the one named last changes fastest.
Arguments:
- stiffness: bfloat16 [48, 2048, 128, 128], P('sub', 'blk')
- dofmap: int32 [48, 2048, 128], P('sub', 'blk'), may hold values from 0 to 16383
- eigvecs: bfloat16 [48, 64, 16384], P('sub', None, 'blk'), may hold values from -6 to 6
- rim_rows: int32 [48, 2, 2048], P('sub'), may hold values from 0 to 16383
- owner_map: int32 [48], replicated, may hold values from 0 to 47, as said below
Outputs:
- coarse_rows: float32 [192, 64, 192], P('sub', 'blk')
Inputs may be any that keep to these rules, and one draw needn't show every extreme that they name: `owner_map`: each solver index names at most 4 subdomains, and one names exactly 4.
All inputs are finite; a program needn't handle non-finite values.
Results may differ from a plain program's by a relative error of at most 0.0003.
Values may be sent and summed in bfloat16 or wider, within the bound.
No kernel may reach another device: no remote copies, remote signals or barrier semaphores. Data moves between devices by JAX's collectives and lax.ppermute only.
A program may use at most 64 MiB of HBM per device.

v0:
```python
import math

import jax
import jax.numpy as jnp
from jax import lax
from jax.sharding import PartitionSpec as P

CAP = 4


def extended(cells, sides, width):
    for axis, dim in sides:
        count = lax.axis_size(axis)
        ends = count - 1
        head = lax.slice_in_dim(cells, 0, width, axis=dim)
        tail = lax.slice_in_dim(cells, cells.shape[dim] - width, cells.shape[dim], axis=dim)
        cells = jnp.concatenate(
            [
                lax.ppermute(tail, axis, [(i, (i + 1) % count) for i in range(ends)]),
                cells,
                lax.ppermute(head, axis, [((i + 1) % count, i) for i in range(ends)]),
            ],
            axis=dim,
        )
    return cells


def inner_rows(left, right):
    return lax.dot_general(
        left,
        right,
        (((1,), (1,)), ((), ())),
        precision=lax.Precision.HIGHEST,
        preferred_element_type=jnp.float32,
    )


def on_device(stiffness, dofmap, eigvecs, rim_rows, owner_map):
    blk_count = lax.axis_size("blk")
    own_rows = eigvecs.shape[2]
    all_modes = lax.all_gather(eigvecs, "blk", axis=2, tiled=True)[0]
    mode_count = all_modes.shape[0]
    total_rows = all_modes.shape[1]
    block_count = stiffness.shape[1]
    block_size = stiffness.shape[2]
    flat_dofs = dofmap[0].reshape(-1)
    picked = jnp.take(all_modes, flat_dofs, axis=1).reshape(mode_count, block_count, block_size)
    products = jnp.einsum("kbe,bef->kbf", picked, stiffness[0], preferred_element_type=jnp.float32)
    partial_value = (
        jnp.zeros((mode_count, total_rows), jnp.float32)
        .at[:, flat_dofs]
        .add(products.reshape(mode_count, -1))
    )
    rim_index = rim_rows[0]
    image_rows = lax.psum_scatter(partial_value, "blk", scatter_dimension=1, tiled=True)
    diagonal_block = inner_rows(eigvecs[0].astype(jnp.float32), image_rows)
    local_rows = rim_index - lax.axis_index("blk") * own_rows
    inside = ((local_rows >= 0) & (local_rows < own_rows)).astype(jnp.float32)
    taken_rows = jnp.take(image_rows, jnp.clip(local_rows, 0, own_rows - 1), axis=1) * inside[None]
    rim_images = jnp.moveaxis(taken_rows, 1, 0)
    beside_all = extended(rim_images, (("sub", 0),), 1)
    left_modes = jnp.take(all_modes, rim_index[0], axis=1).astype(jnp.float32)
    right_modes = jnp.take(all_modes, rim_index[1], axis=1).astype(jnp.float32)
    left_block = inner_rows(left_modes, beside_all[0])
    right_block = inner_rows(right_modes, beside_all[3])
    row_scale = 1.0 / math.sqrt(block_count * blk_count * block_size)
    coarse = jnp.concatenate([left_block, diagonal_block, right_block], axis=1) * row_scale
    row_share = lax.psum_scatter(coarse, "blk", scatter_dimension=0, tiled=True)
    sub_count = lax.axis_size("sub")
    solver_index = lax.axis_index("sub")
    positions = jnp.arange(sub_count, dtype=jnp.int32)
    target = jnp.take(owner_map, solver_index)
    outgoing = jnp.where((positions == target)[:, None, None], row_share[None], 0.0)
    arrived = lax.all_to_all(outgoing, "sub", split_axis=0, concat_axis=0, tiled=True)
    same_owner = owner_map[:, None] == owner_map[None, :]
    earlier = positions[None, :] < positions[:, None]
    slot_rank = jnp.sum((same_owner & earlier).astype(jnp.int32), axis=1)
    slot_ids = jnp.arange(CAP, dtype=jnp.int32)
    selector = (
        (owner_map[None, :] == solver_index) & (slot_rank[None, :] == slot_ids[:, None])
    ).astype(jnp.float32)
    return jnp.einsum("cs,srk->crk", selector, arrived, precision=lax.Precision.HIGHEST)


def solution(mesh):
    return jax.shard_map(
        on_device,
        mesh=mesh,
        in_specs=(
            P("sub", "blk", None, None),
            P("sub", "blk", None),
            P("sub", None, "blk"),
            P("sub", None, None),
            P(),
        ),
        out_specs=P("sub", "blk", None),
        check_vma=False,
    )
```

profile of v0, /device:TPU:1, one launch (start us, length us, event | category | flops | bytes accessed | tf_op | source)
XLA Modules:
  0.0 509.9 jit_solution(13134558226440916640)
XLA Ops:
  6.5 0.0 all-gather.2.cloned.1.call-start
  6.5 1.7 copy.21
  8.3 0.0 all-gather.2.cloned.1.call-update
  8.3 0.0 reduce-scatter.2.cloned.1.call-start
  8.3 0.9 compare_and_fusion
  9.2 0.9 compare_select_fusion
  10.1 80.3 %all-gather.2.cloned.1.call-done = bf16[1,64,16384]{1,2,0:T(8,128)(2,1)} async-done(((bf16[1,64,1024]{1,2,0:T(8,128)(2,1)}), bf16[1,64,16384]{1,2,0:T(8,128)(2,1)}) %all-gather.2.cloned.1.call-update) | async-done | bytes 2097168 | tf_op jit(solution)/shard_map/all_gather | solution.py:41
  90.5 58.0 %gather_fusion = bf16[16384,64]{1,0:T(8,128)(2,1)} fusion(bf16[64,16384]{0,1:T(8,128)(2,1)} %bitcast.63, s32[16384]{0:T(1024)S(1)} %broadcast_clamp_fusion), kind=kCustom, calls=%fused_computation.2 | custom fusion | bytes 4259840 | tf_op jit(solution)/shard_map/jit(_take)/gather | solution.py:47
  148.5 3.7 copy.22
  152.2 3.4 fusion.4
  155.6 2.2 copy.33
  157.8 6.9 %copy.24 = f32[16384,64]{1,0:T(8,128)} copy(f32[16384,64]{0,1:T(8,128)} %bitcast.66) | data formatting | bytes 8388608 | tf_op jit(solution)/shard_map/reshape | solution.py:52
  164.7 91.3 %scatter_custom_fusion = f32[64,16384]{0,1:T(8,128)} fusion(s32[16384]{0:T(1024)S(1)} %bitcast.71, f32[16384,64]{1,0:T(8,128)} %copy.24, f32[]{:T(128)} %constant.52.clone.1), kind=kCustom, calls=%fused_computation.8 | custom fusion | flops 1048576 | bytes 4194816 | tf_op jit(solution)/shard_map/scatter-add | solution.py:52
  256.0 0.0 copy-start.3
  256.0 0.0 copy-start.2
  256.0 0.0 reduce-scatter.2.cloned.1.call-update
  256.0 0.6 copy-done.3
  256.7 0.6 dynamic-slice.2
  257.3 0.0 copy-done.2
  258.1 110.9 %reduce-scatter.2.cloned.1.call-done = f32[64,1024]{0,1:T(8,128)} async-done(((f32[64,16384]{0,1:T(8,128)}), f32[64,1024]{0,1:T(8,128)}) %reduce-scatter.2.cloned.1.call-update) | async-done | bytes 262160 | tf_op jit(solution)/shard_map/reduce_scatter | solution.py:55
  368.9 11.8 %gather_fusion.1 = f32[4096,64]{1,0:T(8,128)S(1)} fusion(f32[64,1024]{0,1:T(8,128)} %reduce-scatter.2.cloned.1.call-done, s32[4096]{0:T(1024)S(1)} %broadcast_clamp_fusion.1), kind=kCustom, calls=%fused_computation.3 | custom fusion | bytes 2113536 | tf_op jit(solution)/shard_map/jit(_take)/gather | solution.py:59
  380.8 0.6 copy.25
  381.4 0.0 copy-start
  381.4 0.0 copy-start.1
  381.4 0.1 multiply_bitcast_fusion
  381.5 0.9 fusion.38
  382.4 4.8 collective-permute-start
  387.3 1.9 collective-permute-start.1
  389.2 1.3 dynamic-slice.3
  391.1 8.3 %gather_fusion.3 = bf16[2048,64]{1,0:T(8,128)(2,1)S(1)} fusion(bf16[64,16384]{0,1:T(8,128)(2,1)} %bitcast.64, s32[2048]{0:T(1024)S(1)} %fusion.29), kind=kCustom, calls=%fused_computation.1.clone | custom fusion | bytes 532480 | tf_op jit(solution)/shard_map/jit(_take)/gather | solution.py:63
  399.5 8.3 %gather_fusion.2 = bf16[2048,64]{1,0:T(8,128)(2,1)S(1)} fusion(bf16[64,16384]{0,1:T(8,128)(2,1)} %bitcast.65, s32[2048]{0:T(1024)S(1)} %fusion.28), kind=kCustom, calls=%fused_computation.clone | custom fusion | bytes 532480 | tf_op jit(solution)/shard_map/jit(_take)/gather | solution.py:62
  407.8 0.0 copy-done
  407.8 0.0 copy-done.1
  407.8 0.3 convolution_bitcast_fusion
  408.1 0.0 collective-permute-done
  408.2 0.9 fusion.13
  409.0 0.0 collective-permute-done.1
  409.0 0.9 fusion.10
  409.9 0.1 maximum_multiply_fusion
  410.0 46.5 %all-reduce = f32[64,192]{1,0:T(8,128)S(1)} all-reduce(f32[64,192]{1,0:T(8,128)S(1)} %maximum_multiply_fusion), channel_id=3, replica_groups=mesh['sub'=48,'blk'=16] {'blk'}, use_global_device_ids=true, to_apply=%region_3.5.clone | all-reduce | flops 12288 | bytes 98304
  456.5 0.8 broadcast_select_fusion
  457.3 28.3 %all-to-all-start = ((f32[48,4,192]{2,1,0:T(4,128)}), f32[48,4,192]{2,1,0:T(4,128)S(1)}, u32[]{:S(2)}, u32[]{:S(2)}) async-start(f32[48,4,192]{2,1,0:T(4,128)} %broadcast_select_fusion), calls=%async_computation.1 | async-start | bytes 393216 | tf_op jit(solution)/shard_map/all_to_all | solution.py:74
  485.6 0.2 convert_reduce_fusion
  485.8 16.4 %all-to-all-done = f32[48,4,192]{2,1,0:T(4,128)S(1)} async-done(((f32[48,4,192]{2,1,0:T(4,128)}), f32[48,4,192]{2,1,0:T(4,128)S(1)}, u32[]{:S(2)}, u32[]{:S(2)}) %all-to-all-start) | async-done | bytes 147488 | tf_op jit(solution)/shard_map/all_to_all | solution.py:74
  502.2 0.2 fusion.22
  502.4 0.6 copy.27
  (14 shorter events, 0.2 us)
Async XLA Ops:
  6.5 83.9 %all-gather.2.cloned.1.call-start = ((), (), s32[]{:S(2)}) async-start(), calls=%async_computation.2 | async-start | bytes 4456448 | tf_op jit(solution)/shard_map/all_gather | solution.py:41
  8.3 360.7 %reduce-scatter.2.cloned.1.call-start = ((), (), s32[]{:S(2)}) async-start(), calls=%async_computation.3 | async-start | bytes 8912896 | tf_op jit(solution)/shard_map/reduce_scatter | solution.py:55
  256.0 0.7 copy-start.3
  256.0 1.2 copy-start.2
  381.4 26.4 %copy-start = (f32[64,1024]{0,1:T(8,128)S(1)}, f32[64,1024]{0,1:T(8,128)}, u32[]{:S(2)}) copy-start(f32[64,1024]{0,1:T(8,128)} %reduce-scatter.2.cloned.1.call-done) | copy-start | bytes 786436
  381.4 26.4 %copy-start.1 = (bf16[1,64,1024]{2,1,0:T(8,128)(2,1)S(1)}, bf16[1,64,1024]{2,1,0:T(8,128)(2,1)}, u32[]{:S(2)}) copy-start(bf16[1,64,1024]{2,1,0:T(8,128)(2,1)} %param.9) | copy-start | bytes 393220
  382.4 25.7 %collective-permute-start = (f32[1,64,2048]{2,1,0:T(8,128)}, f32[1,64,2048]{2,1,0:T(8,128)S(1)}, u32[]{:S(2)}, u32[]{:S(2)}) collective-permute-start(f32[1,64,2048]{2,1,0:T(8,128)} %get-tuple-element.17), channel_id=1, source_target_pairs={{0,16},{16,32},{32,48},{48,64},{64,80},{80,96},{96,112},{112,128},... | collective-permute-start | bytes 1572872 | tf_op jit(solution)/shard_map/ppermute | solution.py:19
  387.3 21.8 %collective-permute-start.1 = (f32[1,64,2048]{2,1,0:T(8,128)S(1)}, f32[1,64,2048]{2,1,0:T(8,128)S(1)}, u32[]{:S(2)}, u32[]{:S(2)}) collective-permute-start(f32[1,64,2048]{2,1,0:T(8,128)S(1)} %get-tuple-element.18), channel_id=1, source_target_pairs={{16,0},{32,16},{48,32},{64,48},{80,64},{96,80},{112,96},{128,112},... | collective-permute-start | bytes 1572872 | tf_op jit(solution)/shard_map/ppermute | solution.py:21
  457.3 44.9 %all-to-all-start = ((f32[48,4,192]{2,1,0:T(4,128)}), f32[48,4,192]{2,1,0:T(4,128)S(1)}, u32[]{:S(2)}, u32[]{:S(2)}) async-start(f32[48,4,192]{2,1,0:T(4,128)} %broadcast_select_fusion), calls=%async_computation.1 | async-start | bytes 393216 | tf_op jit(solution)/shard_map/all_to_all | solution.py:74
Sparse Core Ops, SparseCore 0:
  9.7 80.6 all-gather.1
  256.2 112.7 reduce-scatter.1
where the time goes:
time: 511 us; the launch traced here: 510 us
  waiting for transfers between devices  208 us (41%)
  local copies, waits for them, and re-layouts  106 us (21%)
  other arithmetic  94.4 us (18%)
  blocking collectives  46.5 us (9%)
  starting transfers between devices  35.1 us (7%)
  between operations  14.9 us (3%)
  matrix products  5.66 us (1%)
    reduce_scatter x1, waiting for transfers between devices, on_device(): lax.psum_scatter(partial_value, 'blk', scatter_dimension=1, tiled=True)  111 us
    scatter-add x1, other arithmetic, on_device(): partial_value = jnp.zeros((mode_count, total_rows), jnp.float32).at[:, fl...  91.3 us
    all_gather x1, waiting for transfers between devices, on_device(): all_modes = lax.all_gather(eigvecs, 'blk', axis=2, tiled=True)[0]  80.3 us
    gather x2, local copies, waits for them, and re-layouts, on_device(): jnp.take(all_modes, flat_dofs, axis=1)  61.7 us
    unnamed x1, blocking collectives  46.5 us
    all_to_all x1, starting transfers between devices, on_device(): lax.all_to_all(outgoing, 'sub', split_axis=0, concat_axis=0, tiled=True)  28.3 us
    all_to_all x1, waiting for transfers between devices, on_device(): lax.all_to_all(outgoing, 'sub', split_axis=0, concat_axis=0, tiled=True)  16.4 us
    gather x2, local copies, waits for them, and re-layouts, on_device(): jnp.take(image_rows, jnp.clip(local_rows, 0, own_rows - 1), axis=1)  12.4 us
  transfers between devices with their start and end apart: 5, of which 3 were waited for; matrix products, arithmetic and copies ran while one was open for 4% of the time, Pallas kernels for 0%

commit v1 on v0

v1 whole, which is shorter than its diff:
```python
import functools
import math

import jax
import jax.numpy as jnp
from jax import lax
from jax.experimental import pallas as pl
from jax.experimental.pallas import tpu as pltpu
from jax.sharding import PartitionSpec as P

CAP = 4
LANES = 128
CHUNK = 128
GROUP = 16
TOGETHER = 8
F32 = jnp.float32
BF16 = jnp.bfloat16
VMEM = pl.BlockSpec(memory_space=pltpu.VMEM)
SMEM = pl.BlockSpec(memory_space=pltpu.SMEM)


def low_lanes(rows):
    return lax.broadcasted_iota(jnp.int32, (rows, LANES), 1) < LANES // 2


def pack_kernel(modes_ref, out_ref):
    wide = modes_ref[...].astype(F32)
    half = wide.shape[1] // 2
    stacked = jnp.concatenate([wide[:, :half], wide[:, half:]], axis=0)
    out_ref[...] = stacked.T.astype(BF16)


def pack(modes):
    count, width = modes.shape
    return pl.pallas_call(
        pack_kernel,
        out_shape=jax.ShapeDtypeStruct((width // 2, 2 * count), BF16),
        in_specs=[VMEM],
        out_specs=VMEM,
    )(modes)


def unpack_slices(base_ref, pieces, slice_rows, table, stride=1):
    at = 0
    for piece in pieces:
        for first in range(0, piece.shape[0], slice_rows):
            base = base_ref[at]
            at += 1

            def step(c, _):
                start = pl.multiple_of(c * CHUNK, CHUNK)
                wide = piece[pl.ds(first + start, CHUNK), :].astype(F32)
                low = low_lanes(CHUNK)
                here = pl.multiple_of(base + start, CHUNK)
                there = pl.multiple_of(base + slice_rows + start, CHUNK)
                first_half = jnp.where(low, wide, 0.0)
                second_half = jnp.where(low, pltpu.roll(wide, LANES // 2, 1), 0.0)
                if stride == 1:
                    table[pl.ds(here, CHUNK), :] = first_half
                    table[pl.ds(there, CHUNK), :] = second_half
                else:
                    for at_row, value in ((here, first_half), (there, second_half)):
                        table[pl.ds(2 * at_row, CHUNK, stride=2), :] = value
                        table[pl.ds(2 * at_row + 1, CHUNK, stride=2), :] = jnp.zeros_like(value)
                return 0

            lax.fori_loop(0, slice_rows // CHUNK, step, 0)


def rim_kernel(slice_rows, n_pieces, base_ref, rim_ref, *refs):
    pieces, (left_ref, right_ref), (table, taken) = refs[:n_pieces], refs[n_pieces:n_pieces + 2], refs[n_pieces + 2:]
    unpack_slices(base_ref, pieces, slice_rows, table)
    groups, group = rim_ref.shape[0] // 2, rim_ref.shape[1]
    count = groups * group
    for side, out in ((0, left_ref), (1, right_ref)):

        def gather(g, _):
            to = taken.at[pl.ds(pl.multiple_of(g * group, group), group)]
            for j in range(group):
                to[pl.ds(j, 1), :] = table[pl.ds(rim_ref[side * groups + g, j], 1), :]
            return 0

        lax.fori_loop(0, groups, gather, 0)
        half = count // 2
        out[...] = jnp.where(
            low_lanes(half), taken[:half, :], pltpu.roll(taken[half:, :], LANES // 2, 1)
        ).astype(BF16)


def take_rim(bases, rim, pieces, slice_rows):
    total = 2 * sum(p.shape[0] for p in pieces)
    count = rim.shape[1]
    packed = jax.ShapeDtypeStruct((count // 2, LANES), BF16)
    return pl.pallas_call(
        functools.partial(rim_kernel, slice_rows, len(pieces)),
        out_shape=(packed, packed),
        in_specs=[SMEM, SMEM] + [VMEM] * len(pieces),
        out_specs=(VMEM, VMEM),
        scratch_shapes=[pltpu.VMEM((total, LANES), F32), pltpu.VMEM((count, LANES), F32)],
        compiler_params=pltpu.CompilerParams(vmem_limit_bytes=48 * 2**20),
    )(bases, rim.reshape(-1, LANES), *pieces)


def spread_rim(packed, out, high):
    half = packed.shape[0]

    def step(c, _):
        start = pl.multiple_of(c * CHUNK, CHUNK)
        wide = packed[pl.ds(start, CHUNK), :].astype(F32)
        turned = pltpu.roll(wide, LANES // 2, 1)
        low = low_lanes(CHUNK)
        if high:
            first, second = jnp.where(low, 0.0, turned), jnp.where(low, 0.0, wide)
        else:
            first, second = jnp.where(low, wide, 0.0), jnp.where(low, turned, 0.0)
        out[pl.ds(start, CHUNK), :] = first
        out[pl.ds(half + start, CHUNK), :] = second
        return 0

    lax.fori_loop(0, half // CHUNK, step, 0)


def main_kernel(
    slice_rows, n_pieces, scale, base_ref, rim_ref, clash_ref, dof_ref, stiff_ref, from_left, from_right, *refs
):
    pieces = refs[:n_pieces]
    out_ref = refs[n_pieces]
    table, rim_a, rim_b, got, acc, acc_low = refs[n_pieces + 1:]
    unpack_slices(base_ref, pieces, slice_rows, table, 2)
    spread_rim(from_left, rim_a, True)
    spread_rim(from_right, rim_b, False)
    groups = clash_ref.shape[0]
    group = rim_ref.shape[1]

    def add_rows(g, _):
        first = pl.multiple_of(g * group, group)
        new_a, new_b = rim_a.at[pl.ds(first, group)], rim_b.at[pl.ds(first, group)]

        @pl.when(clash_ref[g] == 0)
        def _():
            at_a = [2 * rim_ref[g, j] for j in range(group)]
            at_b = [2 * rim_ref[groups + g, j] + 1 for j in range(group)]
            sum_a = [table[pl.ds(row, 1), :] + new_a[pl.ds(j, 1), :] for j, row in enumerate(at_a)]
            sum_b = [table[pl.ds(row, 1), :] + new_b[pl.ds(j, 1), :] for j, row in enumerate(at_b)]
            for j in range(group):
                table[pl.ds(at_a[j], 1), :] = sum_a[j]
                table[pl.ds(at_b[j], 1), :] = sum_b[j]

        @pl.when(clash_ref[g] != 0)
        def _():
            def one(j, _):
                table[pl.ds(2 * rim_ref[g, j], 1), :] += new_a[pl.ds(j, 1), :]
                table[pl.ds(2 * rim_ref[groups + g, j] + 1, 1), :] += new_b[pl.ds(j, 1), :]
                return 0

            lax.fori_loop(0, group, one, 0)

        return 0

    lax.fori_loop(0, groups, add_rows, 0)

    n_blocks, size = dof_ref.shape
    modes = LANES // 2

    def gather(e, _):
        to = got.at[pl.ds(pl.multiple_of(2 * e * size, 2 * size), 2 * size)]
        for j in range(size):
            row = dof_ref[e, j]
            to[pl.ds(2 * j, 2), :] = table[pl.ds(2 * row, 2), :]
        return 0

    lax.fori_loop(0, n_blocks, gather, 0)

    acc[...] = jnp.zeros_like(acc)
    acc_low[...] = jnp.zeros_like(acc_low)
    width = TOGETHER * size

    def contract(i, _):
        first = pl.multiple_of(2 * i * width, 2 * width)
        wide_a, wide_b = got[pl.ds(first, width, stride=2), :], got[pl.ds(first + 1, width, stride=2), :]
        high_a, high_b = wide_a.astype(BF16), wide_b.astype(BF16)
        low_ab = ((wide_a - high_a.astype(F32)) + (wide_b - high_b.astype(F32))).astype(BF16)
        picked = high_a.T[:modes, :]
        image = jnp.concatenate(
            [
                jnp.dot(picked[:, e * size:(e + 1) * size], stiff_ref[i * TOGETHER + e], preferred_element_type=F32)
                for e in range(TOGETHER)
            ],
            axis=1,
        )
        image_high = image.astype(BF16)
        image_low = (image - image_high.astype(F32)).astype(BF16)
        both = jnp.concatenate([image_high, image_low], axis=0)
        right = jnp.concatenate([high_a, high_b], axis=1)
        acc[...] += jnp.dot(both, right, preferred_element_type=F32)
        acc_low[...] += jnp.dot(image_high, low_ab, preferred_element_type=F32)
        return 0

    lax.fori_loop(0, n_blocks // TOGETHER, contract, 0)
    summed = acc[:modes, :] + acc[modes:, :]
    first, second = summed[:, :LANES], summed[:, LANES:]
    rest = acc_low[...]
    low = low_lanes(modes)
    first = first + jnp.where(low, 0.0, rest)
    second = second + jnp.where(low, rest, 0.0)
    first_t, second_t = (first * scale).T, (second * scale).T
    own, to_prev, to_next = first_t[:modes], first_t[modes:], second_t[:modes]
    rows = jnp.concatenate([to_next, own, to_prev], axis=1)
    share = out_ref.shape[1]
    for d in range(out_ref.shape[0]):
        out_ref[d] = rows[d * share:(d + 1) * share]


def clashes(rim):
    grouped = rim.reshape(2, -1, GROUP)
    same = grouped[:, :, :, None] == grouped[:, :, None, :]
    places = jnp.arange(GROUP)
    return jnp.any(same & (places[:, None] < places[None, :]), axis=(0, 2, 3)).astype(jnp.int32)


def contract_blocks(bases, rim, dofs, stiffness, from_left, from_right, pieces, slice_rows, parts, scale):
    total = 2 * sum(p.shape[0] for p in pieces)
    count = rim.shape[1]
    modes = LANES // 2
    n_blocks, size = dofs.shape
    wide = lambda n: pltpu.VMEM((n, LANES), F32)
    return pl.pallas_call(
        functools.partial(main_kernel, slice_rows, len(pieces), scale),
        out_shape=jax.ShapeDtypeStruct((parts, modes // parts, 3 * modes), F32),
        in_specs=[SMEM, SMEM, SMEM, SMEM, VMEM, VMEM, VMEM] + [VMEM] * len(pieces),
        out_specs=VMEM,
        scratch_shapes=[
            wide(2 * total), wide(count), wide(count), wide(2 * n_blocks * size),
            pltpu.VMEM((2 * modes, 2 * LANES), F32), pltpu.VMEM((modes, LANES), F32),
        ],
        compiler_params=pltpu.CompilerParams(vmem_limit_bytes=56 * 2**20),
    )(bases, rim.reshape(-1, GROUP), clashes(rim), dofs, stiffness, from_left, from_right, *pieces)


def ring_pieces(packed, index, count):
    ring = count // 2
    move = lambda value, dx, dy: lax.ppermute(
        value, "blk",
        [(i, ((i // ring + dx) % 2) * ring + (i % ring + dy) % ring) for i in range(count)],
    )
    x, y = index // ring, index % ring
    base = lambda flip, dy: ((jnp.remainder(x + flip, 2)) * ring + jnp.remainder(y + dy, ring))
    rows = packed.shape[0]
    both = jnp.concatenate([packed, move(packed, 1, 0)], axis=0)
    pieces, places = [both], [base(0, 0), base(1, 0)]
    up = down = both
    for k in range(1, ring // 2):
        up, down = move(up, 0, 1), move(down, 0, -1)
        pieces += [up, down]
        places += [base(0, -k), base(1, -k), base(0, k), base(1, k)]
    pieces += [move(up[:rows], 0, 1), move(down[rows:], 0, -1)]
    places += [base(0, ring // 2), base(1, ring // 2)]
    return pieces, jnp.stack(places).astype(jnp.int32)


def on_device(stiffness, dofmap, eigvecs, rim_rows, owner_map):
    blk_count, sub_count = lax.axis_size("blk"), lax.axis_size("sub")
    own_rows = eigvecs.shape[2]
    slice_rows = own_rows // 2
    block_count, block_size = dofmap.shape[1:]
    blk, sub = lax.axis_index("blk"), lax.axis_index("sub")
    with jax.named_scope("pack"):
        packed = pack(eigvecs[0])
    with jax.named_scope("gather_modes"):
        pieces, places = ring_pieces(packed, blk, blk_count)
        bases = places * own_rows
    with jax.named_scope("rim"):
        left, right = take_rim(bases, rim_rows[0], pieces, slice_rows)
        from_left = lax.ppermute(right, "sub", [(i, i + 1) for i in range(sub_count - 1)])
        from_right = lax.ppermute(left, "sub", [(i + 1, i) for i in range(sub_count - 1)])
    with jax.named_scope("contract"):
        scale = 1.0 / math.sqrt(block_count * blk_count * block_size)
        share = contract_blocks(
            bases, rim_rows[0], dofmap[0], stiffness[0], from_left, from_right, pieces, slice_rows, blk_count, scale
        )
    with jax.named_scope("sum_over_blk"):
        mine = jnp.sum(lax.all_to_all(share, "blk", 0, 0, tiled=True), axis=0)
    with jax.named_scope("relay"):
        sent = jnp.broadcast_to(mine[None], (sub_count,) + mine.shape)
        arrived = lax.all_to_all(sent, "sub", 0, 0, tiled=True)
    with jax.named_scope("slots"):
        positions = jnp.arange(sub_count, dtype=jnp.int32)
        same_owner = owner_map[:, None] == owner_map[None, :]
        earlier = positions[None, :] < positions[:, None]
        slot_rank = jnp.sum((same_owner & earlier).astype(jnp.int32), axis=1)
        slot_ids = jnp.arange(CAP, dtype=jnp.int32)
        chosen = (owner_map[None, :] == sub) & (slot_rank[None, :] == slot_ids[:, None])
        none = jnp.zeros((CAP, 1), bool)
        from_prev = jnp.concatenate([chosen[:, 1:], none], axis=1)
        from_next = jnp.concatenate([none, chosen[:, :-1]], axis=1)
        modes = LANES // 2
        parts = [
            jnp.sum(jnp.where(pick[:, :, None, None], arrived[None, :, :, p * modes:(p + 1) * modes], 0.0), axis=1)
            for p, pick in enumerate((from_prev, chosen, from_next))
        ]
        return jnp.concatenate(parts, axis=2)


def solution(mesh):
    return jax.shard_map(
        on_device,
        mesh=mesh,
        in_specs=(
            P("sub", "blk", None, None),
            P("sub", "blk", None),
            P("sub", None, "blk"),
            P("sub", None, None),
            P(),
        ),
        out_specs=P("sub", "blk", None),
        check_vma=False,
    )
```

time: 511 us -> 175 us (0.34)
  waiting for transfers between devices: 208 us -> 35.5 us
  local copies, waits for them, and re-layouts: 106 us -> 4.88 us
  other arithmetic: 94.4 us -> 2.92 us
  Pallas kernels: 0 us -> 60 us
  blocking collectives: 46.5 us -> 0 us
  starting transfers between devices: 35.1 us -> 70.6 us
  between operations: 14.9 us -> 0.54 us
  matrix products: 5.66 us -> 0 us
    reduce_scatter x1 -> x0, waiting for transfers between devices: 111 us -> none  [on_device(): lax.psum_scatter(partial_value, 'blk', scatter_dimension=1, tiled=True)]
    scatter-add x1 -> x0, other arithmetic: 91.3 us -> none  [on_device(): partial_value = jnp.zeros((mode_count, total_rows), jnp.float32).at[:, fl...]
    gather x6 -> x0, local copies, waits for them, and re-layouts: 90.8 us -> none  [the longest x2 61.7 us: on_device(): jnp.take(all_modes, flat_dofs, axis=1)]
    all_gather x1 -> x0, waiting for transfers between devices: 80.3 us -> none  [on_device(): all_modes = lax.all_gather(eigvecs, 'blk', axis=2, tiled=True)[0]]
    pallas_call x0 -> x3, Pallas kernels: none -> 60 us  [the longest x1 48.8 us: contract_blocks(): pl.pallas_call(functools.partial(main_kernel, slice_rows, len(pieces), sc...]
    unnamed x1 -> x0, blocking collectives: 46.5 us -> none
    ppermute x2 -> x11, starting transfers between devices: 6.74 us -> 47.6 us  [the longest x9 31.2 us: ring_pieces(): lax.ppermute(value, 'blk', [(i, (i // ring + dx) % 2 * ring + (i % ring +...]
    ppermute x2 -> x11, waiting for transfers between devices: 0.01 us -> 11.7 us  [the longest x9 10.6 us: ring_pieces(): lax.ppermute(value, 'blk', [(i, (i // ring + dx) % 2 * ring + (i % ring +...]
  transfers between devices with their start and end apart: 5 -> 13, of which waited for: 3 -> 8; matrix products, arithmetic and copies ran while one was open for 4% -> 2% of each run, Pallas kernels for 0% -> 0%
where the time goes in v1:
time: 175 us; the launch traced here: 174 us
  starting transfers between devices  70.6 us (40%)
  Pallas kernels  60 us (34%)
  waiting for transfers between devices  35.5 us (20%)
  local copies, waits for them, and re-layouts  4.88 us (3%)
  other arithmetic  2.92 us (2%)
    pallas_call x1, Pallas kernels, contract_blocks(): pl.pallas_call(functools.partial(main_kernel, slice_rows, len(pieces), sc...  48.8 us
    ppermute x9, starting transfers between devices, ring_pieces(): lax.ppermute(value, 'blk', [(i, (i // ring + dx) % 2 * ring + (i % ring +...  31.2 us
    all_to_all x1, waiting for transfers between devices, on_device(): arrived = lax.all_to_all(sent, 'sub', 0, 0, tiled=True)  16.4 us
    all_to_all x1, starting transfers between devices, on_device(): arrived = lax.all_to_all(sent, 'sub', 0, 0, tiled=True)  15.7 us
    ppermute x1, starting transfers between devices, on_device(): lax.ppermute(left, 'sub', [(i + 1, i) for i in range(sub_count - 1)])  14.5 us
    ppermute x9, waiting for transfers between devices, ring_pieces(): lax.ppermute(value, 'blk', [(i, (i // ring + dx) % 2 * ring + (i % ring +...  10.6 us
    pallas_call x1, Pallas kernels, take_rim(): pl.pallas_call(functools.partial(rim_kernel, slice_rows, len(pieces)), ou...  9.5 us
    all_to_all x1, waiting for transfers between devices, on_device(): mine = jnp.sum(lax.all_to_all(share, 'blk', 0, 0, tiled=True), axis=0)  7.37 us
  transfers between devices with their start and end apart: 13, of which 8 were waited for; matrix products, arithmetic and copies ran while one was open for 2% of the time, Pallas kernels for 0%

profile of v1, /device:TPU:1, one launch (start us, length us, event | category | flops | bytes accessed | tf_op | source)
XLA Modules:
  0.0 174.4 jit_solution(8008276167779946586)
XLA Ops:
  0.0 1.7 pack.1
  1.7 3.9 %collective-permute-start = (bf16[512,128]{1,0:T(8,128)(2,1)}, bf16[512,128]{1,0:T(8,128)(2,1)S(1)}, u32[]{:S(2)}, u32[]{:S(2)}) collective-permute-start(bf16[512,128]{1,0:T(8,128)(2,1)} %pack.1), channel_id=1, source_target_pairs={{0,8},{1,9},{2,10},{3,11},{4,12},{5,13},{6,14},{7,15},{8,0},{9,1},... | collective-permute-start | bytes 393224 | tf_op jit(solution)/shard_map/gather_modes/ppermute | solution.py:242
  5.6 2.6 %collective-permute-done = bf16[512,128]{1,0:T(8,128)(2,1)S(1)} collective-permute-done((bf16[512,128]{1,0:T(8,128)(2,1)}, bf16[512,128]{1,0:T(8,128)(2,1)S(1)}, u32[]{:S(2)}, u32[]{:S(2)}) %collective-permute-start) | collective-permute-done | bytes 131104 | tf_op jit(solution)/shard_map/gather_modes/ppermute | solution.py:242
  8.2 0.9 pad_maximum_fusion.refs_0_
  9.1 4.0 %collective-permute-start.1 = (bf16[1024,128]{1,0:T(8,128)(2,1)S(1)}, bf16[1024,128]{1,0:T(8,128)(2,1)S(1)}, u32[]{:S(2)}, u32[]{:S(2)}) collective-permute-start(bf16[1024,128]{1,0:T(8,128)(2,1)S(1)} %pad_maximum_fusion.refs_0_), channel_id=1, source_target_pairs={{0,1},{1,2},{2,3},{3,4},{4,5},{5,6},{6,7},{7,0},{8,9},{9,10},{10,1... | collective-permute-start | bytes 786440 | tf_op jit(solution)/shard_map/gather_modes/ppermute | solution.py:242
  13.1 3.8 %collective-permute-start.2 = (bf16[1024,128]{1,0:T(8,128)(2,1)S(1)}, bf16[1024,128]{1,0:T(8,128)(2,1)S(1)}, u32[]{:S(2)}, u32[]{:S(2)}) collective-permute-start(bf16[1024,128]{1,0:T(8,128)(2,1)S(1)} %pad_maximum_fusion.refs_0_), channel_id=1, source_target_pairs={{0,7},{1,0},{2,1},{3,2},{4,3},{5,4},{6,5},{7,6},{8,15},{9,8},{10,9... | collective-permute-start | bytes 786440 | tf_op jit(solution)/shard_map/gather_modes/ppermute | solution.py:242
  16.9 1.8 %collective-permute-done.1.refs_1_ = bf16[1024,128]{1,0:T(8,128)(2,1)S(1)} collective-permute-done((bf16[1024,128]{1,0:T(8,128)(2,1)S(1)}, bf16[1024,128]{1,0:T(8,128)(2,1)S(1)}, u32[]{:S(2)}, u32[]{:S(2)}) %collective-permute-start.1) | collective-permute-done | bytes 262176 | tf_op jit(solution)/shard_map/gather_modes/ppermute | solution.py:242
  18.7 1.9 %collective-permute-start.3 = (bf16[1024,128]{1,0:T(8,128)(2,1)S(1)}, bf16[1024,128]{1,0:T(8,128)(2,1)S(1)}, u32[]{:S(2)}, u32[]{:S(2)}) collective-permute-start(bf16[1024,128]{1,0:T(8,128)(2,1)S(1)} %collective-permute-done.1.refs_1_), channel_id=1, source_target_pairs={{0,1},{1,2},{2,3},{3,4},{4,5},{5,6},{6,7},{7,0},{8,9},{9,10},{10,1... | collective-permute-start | bytes 786440 | tf_op jit(solution)/shard_map/gather_modes/ppermute | solution.py:242
  20.7 0.0 collective-permute-done.2.refs_2_
  20.7 4.6 %collective-permute-start.4 = (bf16[1024,128]{1,0:T(8,128)(2,1)S(1)}, bf16[1024,128]{1,0:T(8,128)(2,1)S(1)}, u32[]{:S(2)}, u32[]{:S(2)}) collective-permute-start(bf16[1024,128]{1,0:T(8,128)(2,1)S(1)} %collective-permute-done.2.refs_2_), channel_id=1, source_target_pairs={{0,7},{1,0},{2,1},{3,2},{4,3},{5,4},{6,5},{7,6},{8,15},{9,8},{10,9... | collective-permute-start | bytes 786440 | tf_op jit(solution)/shard_map/gather_modes/ppermute | solution.py:242
  25.3 2.9 %collective-permute-done.3.refs_3_ = bf16[1024,128]{1,0:T(8,128)(2,1)S(1)} collective-permute-done((bf16[1024,128]{1,0:T(8,128)(2,1)S(1)}, bf16[1024,128]{1,0:T(8,128)(2,1)S(1)}, u32[]{:S(2)}, u32[]{:S(2)}) %collective-permute-start.3) | collective-permute-done | bytes 262176 | tf_op jit(solution)/shard_map/gather_modes/ppermute | solution.py:242
  28.2 1.9 %collective-permute-start.5 = (bf16[1024,128]{1,0:T(8,128)(2,1)S(1)}, bf16[1024,128]{1,0:T(8,128)(2,1)S(1)}, u32[]{:S(2)}, u32[]{:S(2)}) collective-permute-start(bf16[1024,128]{1,0:T(8,128)(2,1)S(1)} %collective-permute-done.3.refs_3_), channel_id=1, source_target_pairs={{0,1},{1,2},{2,3},{3,4},{4,5},{5,6},{6,7},{7,0},{8,9},{9,10},{10,1... | collective-permute-start | bytes 786440 | tf_op jit(solution)/shard_map/gather_modes/ppermute | solution.py:242
  30.1 0.0 collective-permute-done.4.refs_4_
  30.1 0.0 copy-start.6
  30.1 4.6 %collective-permute-start.6 = (bf16[1024,128]{1,0:T(8,128)(2,1)S(1)}, bf16[1024,128]{1,0:T(8,128)(2,1)S(1)}, u32[]{:S(2)}, u32[]{:S(2)}) collective-permute-start(bf16[1024,128]{1,0:T(8,128)(2,1)S(1)} %collective-permute-done.4.refs_4_), channel_id=1, source_target_pairs={{0,7},{1,0},{2,1},{3,2},{4,3},{5,4},{6,5},{7,6},{8,15},{9,8},{10,9... | collective-permute-start | bytes 786440 | tf_op jit(solution)/shard_map/gather_modes/ppermute | solution.py:242
  34.9 0.1 stack.67
  35.0 1.5 collective-permute-done.5.refs_5_
  36.5 1.9 %collective-permute-start.7 = (bf16[512,128]{1,0:T(8,128)(2,1)S(1)}, bf16[512,128]{1,0:T(8,128)(2,1)S(1)}, u32[]{:S(2)}, u32[]{:S(2)}) collective-permute-start(bf16[512,128]{1,0:T(8,128)(2,1)S(1)} %slice.28), channel_id=1, source_target_pairs={{0,1},{1,2},{2,3},{3,4},{4,5},{5,6},{6,7},{7,0},{8,9},{9,10},{10,1... | collective-permute-start | bytes 393224 | tf_op jit(solution)/shard_map/gather_modes/ppermute | solution.py:242
  38.5 0.0 collective-permute-done.6.refs_6_
  38.5 4.6 %collective-permute-start.8 = (bf16[512,128]{1,0:T(8,128)(2,1)S(1)}, bf16[512,128]{1,0:T(8,128)(2,1)S(1)}, u32[]{:S(2)}, u32[]{:S(2)}) collective-permute-start(bf16[512,128]{1,0:T(8,128)(2,1)S(1)} %slice.29), channel_id=1, source_target_pairs={{0,7},{1,0},{2,1},{3,2},{4,3},{5,4},{6,5},{7,6},{8,15},{9,8},{10,9... | collective-permute-start | bytes 393224 | tf_op jit(solution)/shard_map/gather_modes/ppermute | solution.py:242
  43.1 0.0 copy-start.9
  43.1 0.7 squeeze.20.rim_ref
  43.8 0.8 eq.94
  44.7 0.1 copy.8
  44.7 0.0 collective-permute-done.7.refs_7_
  44.8 1.8 %collective-permute-done.8.refs_8_ = bf16[512,128]{1,0:T(8,128)(2,1)S(1)} collective-permute-done((bf16[512,128]{1,0:T(8,128)(2,1)S(1)}, bf16[512,128]{1,0:T(8,128)(2,1)S(1)}, u32[]{:S(2)}, u32[]{:S(2)}) %collective-permute-start.8) | collective-permute-done | bytes 131104 | tf_op jit(solution)/shard_map/gather_modes/ppermute | solution.py:242
  46.5 9.5 %rim.1 = (bf16[1024,128]{1,0:T(8,128)(2,1)S(1)}, bf16[1024,128]{1,0:T(8,128)(2,1)S(1)}) custom-call(s32[16]{0:T(128)S(1)} %broadcast_multiply_fusion.base_ref, s32[32,128]{1,0:T(8,128)S(1)} %squeeze.20.rim_ref, bf16[1024,128]{1,0:T(8,128)(2,1)S(1)} %pad_maximum_fusion.refs_0_, bf16[1024,128]{1,0:T(8,128)(2,1)S(1)} %collective-permute-done.1.refs_1_, ...), custom_call_target="tpu_custom_call" | custom-call | tf_op jit(solution)/shard_map/rim/pallas_call | solution.py:94
  56.0 14.5 %collective-permute-start.10 = (bf16[1024,128]{1,0:T(8,128)(2,1)S(1)}, bf16[1024,128]{1,0:T(8,128)(2,1)S(1)}, u32[]{:S(2)}, u32[]{:S(2)}) collective-permute-start(bf16[1024,128]{1,0:T(8,128)(2,1)S(1)} %get-tuple-element.8), channel_id=1, source_target_pairs={{16,0},{32,16},{48,32},{64,48},{80,64},{96,80},{112,96},{128,112},... | collective-permute-start | bytes 786440 | tf_op jit(solution)/shard_map/rim/ppermute | solution.py:275
  70.5 1.9 %collective-permute-start.9 = (bf16[1024,128]{1,0:T(8,128)(2,1)S(1)}, bf16[1024,128]{1,0:T(8,128)(2,1)S(1)}, u32[]{:S(2)}, u32[]{:S(2)}) collective-permute-start(bf16[1024,128]{1,0:T(8,128)(2,1)S(1)} %get-tuple-element.7), channel_id=1, source_target_pairs={{0,16},{16,32},{32,48},{48,64},{64,80},{80,96},{96,112},{112,128},... | collective-permute-start | bytes 786440 | tf_op jit(solution)/shard_map/rim/ppermute | solution.py:274
  72.5 0.2 and_reduce_fusion
  72.6 1.5 squeeze.17.rim_ref
  74.1 0.6 convert_element_type.7.clash_ref
  74.7 0.0 collective-permute-done.10.from_right
  74.7 1.1 collective-permute-done.9.from_left
  75.9 0.6 copy-done.11
  76.5 48.8 %contract.1 = f32[16,4,192]{2,1,0:T(4,128)} custom-call(s32[16]{0:T(128)} %copy-done.9, s32[256,16]{1,0:T(8,128)} %squeeze.17.rim_ref, s32[128]{0:T(128)} %convert_element_type.7.clash_ref, s32[128,128]{1,0:T(8,128)} %bitcast.21, bf16[128,128,128]{2,1,0:T(8,128)(2,1)} %bitcast.19, bf16[1024,128]{1,0:T(8,128)(2,1)} %copy-done.11, ...), custom_call_target="tpu_custom_call" | custom-call | tf_op jit(solution)/shard_map/contract/pallas_call | solution.py:227
  125.3 7.3 %all-to-all-start = ((f32[16,4,192]{2,1,0:T(4,128)}), f32[16,4,192]{2,1,0:T(4,128)S(1)}, u32[]{:S(2)}, u32[]{:S(2)}) async-start(f32[16,4,192]{2,1,0:T(4,128)} %contract.1), calls=%async_computation | async-start | bytes 131072 | tf_op jit(solution)/shard_map/sum_over_blk/all_to_all | solution.py:282
  132.6 0.2 convert_reduce_fusion
  132.8 7.4 %all-to-all-done = f32[16,4,192]{2,1,0:T(4,128)S(1)} async-done(((f32[16,4,192]{2,1,0:T(4,128)}), f32[16,4,192]{2,1,0:T(4,128)S(1)}, u32[]{:S(2)}, u32[]{:S(2)}) %all-to-all-start) | async-done | bytes 49184 | tf_op jit(solution)/shard_map/sum_over_blk/all_to_all | solution.py:282
  140.2 0.7 broadcast_in_dim.65
  140.9 15.7 %all-to-all-start.1 = ((f32[48,4,192]{2,1,0:T(4,128)}), f32[48,4,192]{2,1,0:T(4,128)S(1)}, u32[]{:S(2)}, u32[]{:S(2)}) async-start(f32[48,4,192]{2,1,0:T(4,128)} %broadcast_in_dim.65), calls=%async_computation.1 | async-start | bytes 393216 | tf_op jit(solution)/shard_map/relay/all_to_all | solution.py:285
  156.6 0.1 fusion.3
  156.7 0.1 concatenate.14
  156.8 16.4 %all-to-all-done.1 = f32[48,4,192]{2,1,0:T(4,128)S(1)} async-done(((f32[48,4,192]{2,1,0:T(4,128)}), f32[48,4,192]{2,1,0:T(4,128)S(1)}, u32[]{:S(2)}, u32[]{:S(2)}) %all-to-all-start.1) | async-done | bytes 147488 | tf_op jit(solution)/shard_map/relay/all_to_all | solution.py:285
  173.2 0.1 fusion.2
  173.4 0.1 select_reduce_fusion.2
  173.5 0.2 select_reduce_fusion
  173.7 0.7 pad_maximum_fusion.1
  (34 shorter events, 0.2 us)
Async XLA Ops:
  0.0 74.7 %copy-start.12 = (s32[48]{0:T(128)S(1)}, s32[48]{0:T(128)}, u32[]{:S(2)}) copy-start(s32[48]{0:T(128)} %param.9) | copy-start | bytes 580
  1.7 6.5 %collective-permute-start = (bf16[512,128]{1,0:T(8,128)(2,1)}, bf16[512,128]{1,0:T(8,128)(2,1)S(1)}, u32[]{:S(2)}, u32[]{:S(2)}) collective-permute-start(bf16[512,128]{1,0:T(8,128)(2,1)} %pack.1), channel_id=1, source_target_pairs={{0,8},{1,9},{2,10},{3,11},{4,12},{5,13},{6,14},{7,15},{8,0},{9,1},... | collective-permute-start | bytes 393224 | tf_op jit(solution)/shard_map/gather_modes/ppermute | solution.py:242
  9.1 66.7 %copy-start = (bf16[1024,128]{1,0:T(8,128)(2,1)}, bf16[1024,128]{1,0:T(8,128)(2,1)S(1)}, u32[]{:S(2)}) copy-start(bf16[1024,128]{1,0:T(8,128)(2,1)S(1)} %pad_maximum_fusion.refs_0_) | copy-start | bytes 786436
  9.1 9.6 %collective-permute-start.1 = (bf16[1024,128]{1,0:T(8,128)(2,1)S(1)}, bf16[1024,128]{1,0:T(8,128)(2,1)S(1)}, u32[]{:S(2)}, u32[]{:S(2)}) collective-permute-start(bf16[1024,128]{1,0:T(8,128)(2,1)S(1)} %pad_maximum_fusion.refs_0_), channel_id=1, source_target_pairs={{0,1},{1,2},{2,3},{3,4},{4,5},{5,6},{6,7},{7,0},{8,9},{9,10},{10,1... | collective-permute-start | bytes 786440 | tf_op jit(solution)/shard_map/gather_modes/ppermute | solution.py:242
  13.1 7.6 %collective-permute-start.2 = (bf16[1024,128]{1,0:T(8,128)(2,1)S(1)}, bf16[1024,128]{1,0:T(8,128)(2,1)S(1)}, u32[]{:S(2)}, u32[]{:S(2)}) collective-permute-start(bf16[1024,128]{1,0:T(8,128)(2,1)S(1)} %pad_maximum_fusion.refs_0_), channel_id=1, source_target_pairs={{0,7},{1,0},{2,1},{3,2},{4,3},{5,4},{6,5},{7,6},{8,15},{9,8},{10,9... | collective-permute-start | bytes 786440 | tf_op jit(solution)/shard_map/gather_modes/ppermute | solution.py:242
  18.7 57.0 %copy-start.3 = (bf16[1024,128]{1,0:T(8,128)(2,1)}, bf16[1024,128]{1,0:T(8,128)(2,1)S(1)}, u32[]{:S(2)}) copy-start(bf16[1024,128]{1,0:T(8,128)(2,1)S(1)} %collective-permute-done.1.refs_1_) | copy-start | bytes 786436
  18.7 9.4 %collective-permute-start.3 = (bf16[1024,128]{1,0:T(8,128)(2,1)S(1)}, bf16[1024,128]{1,0:T(8,128)(2,1)S(1)}, u32[]{:S(2)}, u32[]{:S(2)}) collective-permute-start(bf16[1024,128]{1,0:T(8,128)(2,1)S(1)} %collective-permute-done.1.refs_1_), channel_id=1, source_target_pairs={{0,1},{1,2},{2,3},{3,4},{4,5},{5,6},{6,7},{7,0},{8,9},{9,10},{10,1... | collective-permute-start | bytes 786440 | tf_op jit(solution)/shard_map/gather_modes/ppermute | solution.py:242
  20.7 55.1 %copy-start.4 = (bf16[1024,128]{1,0:T(8,128)(2,1)}, bf16[1024,128]{1,0:T(8,128)(2,1)S(1)}, u32[]{:S(2)}) copy-start(bf16[1024,128]{1,0:T(8,128)(2,1)S(1)} %collective-permute-done.2.refs_2_) | copy-start | bytes 786436
  20.7 9.4 %collective-permute-start.4 = (bf16[1024,128]{1,0:T(8,128)(2,1)S(1)}, bf16[1024,128]{1,0:T(8,128)(2,1)S(1)}, u32[]{:S(2)}, u32[]{:S(2)}) collective-permute-start(bf16[1024,128]{1,0:T(8,128)(2,1)S(1)} %collective-permute-done.2.refs_2_), channel_id=1, source_target_pairs={{0,7},{1,0},{2,1},{3,2},{4,3},{5,4},{6,5},{7,6},{8,15},{9,8},{10,9... | collective-permute-start | bytes 786440 | tf_op jit(solution)/shard_map/gather_modes/ppermute | solution.py:242
  28.2 47.6 %copy-start.5 = (bf16[1024,128]{1,0:T(8,128)(2,1)}, bf16[1024,128]{1,0:T(8,128)(2,1)S(1)}, u32[]{:S(2)}) copy-start(bf16[1024,128]{1,0:T(8,128)(2,1)S(1)} %collective-permute-done.3.refs_3_) | copy-start | bytes 786436
  28.2 8.3 %collective-permute-start.5 = (bf16[1024,128]{1,0:T(8,128)(2,1)S(1)}, bf16[1024,128]{1,0:T(8,128)(2,1)S(1)}, u32[]{:S(2)}, u32[]{:S(2)}) collective-permute-start(bf16[1024,128]{1,0:T(8,128)(2,1)S(1)} %collective-permute-done.3.refs_3_), channel_id=1, source_target_pairs={{0,1},{1,2},{2,3},{3,4},{4,5},{5,6},{6,7},{7,0},{8,9},{9,10},{10,1... | collective-permute-start | bytes 786440 | tf_op jit(solution)/shard_map/gather_modes/ppermute | solution.py:242
  30.1 45.7 %copy-start.6 = (bf16[1024,128]{1,0:T(8,128)(2,1)}, bf16[1024,128]{1,0:T(8,128)(2,1)S(1)}, u32[]{:S(2)}) copy-start(bf16[1024,128]{1,0:T(8,128)(2,1)S(1)} %collective-permute-done.4.refs_4_) | copy-start | bytes 786436
  30.1 8.3 %collective-permute-start.6 = (bf16[1024,128]{1,0:T(8,128)(2,1)S(1)}, bf16[1024,128]{1,0:T(8,128)(2,1)S(1)}, u32[]{:S(2)}, u32[]{:S(2)}) collective-permute-start(bf16[1024,128]{1,0:T(8,128)(2,1)S(1)} %collective-permute-done.4.refs_4_), channel_id=1, source_target_pairs={{0,7},{1,0},{2,1},{3,2},{4,3},{5,4},{6,5},{7,6},{8,15},{9,8},{10,9... | collective-permute-start | bytes 786440 | tf_op jit(solution)/shard_map/gather_modes/ppermute | solution.py:242
  36.5 39.3 %copy-start.1 = (bf16[1024,128]{1,0:T(8,128)(2,1)}, bf16[1024,128]{1,0:T(8,128)(2,1)S(1)}, u32[]{:S(2)}) copy-start(bf16[1024,128]{1,0:T(8,128)(2,1)S(1)} %collective-permute-done.5.refs_5_) | copy-start | bytes 786436
  36.5 8.2 %collective-permute-start.7 = (bf16[512,128]{1,0:T(8,128)(2,1)S(1)}, bf16[512,128]{1,0:T(8,128)(2,1)S(1)}, u32[]{:S(2)}, u32[]{:S(2)}) collective-permute-start(bf16[512,128]{1,0:T(8,128)(2,1)S(1)} %slice.28), channel_id=1, source_target_pairs={{0,1},{1,2},{2,3},{3,4},{4,5},{5,6},{6,7},{7,0},{8,9},{9,10},{10,1... | collective-permute-start | bytes 393224 | tf_op jit(solution)/shard_map/gather_modes/ppermute | solution.py:242
  38.5 37.4 %copy-start.2 = (bf16[1024,128]{1,0:T(8,128)(2,1)}, bf16[1024,128]{1,0:T(8,128)(2,1)S(1)}, u32[]{:S(2)}) copy-start(bf16[1024,128]{1,0:T(8,128)(2,1)S(1)} %collective-permute-done.6.refs_6_) | copy-start | bytes 786436
  38.5 8.0 %collective-permute-start.8 = (bf16[512,128]{1,0:T(8,128)(2,1)S(1)}, bf16[512,128]{1,0:T(8,128)(2,1)S(1)}, u32[]{:S(2)}, u32[]{:S(2)}) collective-permute-start(bf16[512,128]{1,0:T(8,128)(2,1)S(1)} %slice.29), channel_id=1, source_target_pairs={{0,7},{1,0},{2,1},{3,2},{4,3},{5,4},{6,5},{7,6},{8,15},{9,8},{10,9... | collective-permute-start | bytes 393224 | tf_op jit(solution)/shard_map/gather_modes/ppermute | solution.py:242
  43.1 32.7 %copy-start.9 = (s32[16]{0:T(128)}, s32[16]{0:T(128)S(1)}, u32[]{:S(2)}) copy-start(s32[16]{0:T(128)S(1)} %broadcast_multiply_fusion.base_ref) | copy-start | bytes 196
  44.7 31.1 %copy-start.7 = (bf16[512,128]{1,0:T(8,128)(2,1)}, bf16[512,128]{1,0:T(8,128)(2,1)S(1)}, u32[]{:S(2)}) copy-start(bf16[512,128]{1,0:T(8,128)(2,1)S(1)} %collective-permute-done.7.refs_7_) | copy-start | bytes 393220
  46.5 29.3 %copy-start.8 = (bf16[512,128]{1,0:T(8,128)(2,1)}, bf16[512,128]{1,0:T(8,128)(2,1)S(1)}, u32[]{:S(2)}) copy-start(bf16[512,128]{1,0:T(8,128)(2,1)S(1)} %collective-permute-done.8.refs_8_) | copy-start | bytes 393220
  56.0 18.7 %collective-permute-start.10 = (bf16[1024,128]{1,0:T(8,128)(2,1)S(1)}, bf16[1024,128]{1,0:T(8,128)(2,1)S(1)}, u32[]{:S(2)}, u32[]{:S(2)}) collective-permute-start(bf16[1024,128]{1,0:T(8,128)(2,1)S(1)} %get-tuple-element.8), channel_id=1, source_target_pairs={{16,0},{32,16},{48,32},{64,48},{80,64},{96,80},{112,96},{128,112},... | collective-permute-start | bytes 786440 | tf_op jit(solution)/shard_map/rim/ppermute | solution.py:275
  70.5 5.2 %collective-permute-start.9 = (bf16[1024,128]{1,0:T(8,128)(2,1)S(1)}, bf16[1024,128]{1,0:T(8,128)(2,1)S(1)}, u32[]{:S(2)}, u32[]{:S(2)}) collective-permute-start(bf16[1024,128]{1,0:T(8,128)(2,1)S(1)} %get-tuple-element.7), channel_id=1, source_target_pairs={{0,16},{16,32},{32,48},{48,64},{64,80},{80,96},{96,112},{112,128},... | collective-permute-start | bytes 786440 | tf_op jit(solution)/shard_map/rim/ppermute | solution.py:274
  74.7 1.1 copy-start.10
  75.8 0.7 copy-start.11
  125.3 14.8 %all-to-all-start = ((f32[16,4,192]{2,1,0:T(4,128)}), f32[16,4,192]{2,1,0:T(4,128)S(1)}, u32[]{:S(2)}, u32[]{:S(2)}) async-start(f32[16,4,192]{2,1,0:T(4,128)} %contract.1), calls=%async_computation | async-start | bytes 131072 | tf_op jit(solution)/shard_map/sum_over_blk/all_to_all | solution.py:282
  140.9 32.3 %all-to-all-start.1 = ((f32[48,4,192]{2,1,0:T(4,128)}), f32[48,4,192]{2,1,0:T(4,128)S(1)}, u32[]{:S(2)}, u32[]{:S(2)}) async-start(f32[48,4,192]{2,1,0:T(4,128)} %broadcast_in_dim.65), calls=%async_computation.1 | async-start | bytes 393216 | tf_op jit(solution)/shard_map/relay/all_to_all | solution.py:285

commit v2 on v1

--- a/solution.py
+++ b/solution.py
@@ -10,7 +10,7 @@
 
 CAP = 4
 LANES = 128
-CHUNK = 128
+CHUNK = 256
 GROUP = 16
 TOGETHER = 8
 F32 = jnp.float32
@@ -40,7 +40,40 @@
     )(modes)
 
 
-def unpack_slices(base_ref, pieces, slice_rows, table, stride=1):
+def index_kernel(dof_ref, rim_ref, dof_words, rim_words, clash_ref):
+    size = dof_ref.shape[1]
+    dofs = dof_ref[...]
+    dof_words[...] = 2 * dofs + (pltpu.roll(dofs, size // 2, 1) << 17)
+    rows = rim_words.shape[0]
+    sides = [
+        jnp.concatenate([rim_ref[side:side + 1, r * LANES:(r + 1) * LANES] for r in range(rows)], axis=0)
+        for side in range(2)
+    ]
+    rim_words[...] = 2 * sides[0] + (sides[1] << 17)
+    place = lax.broadcasted_iota(jnp.int32, (rows, LANES), 1) % GROUP
+    clash = jnp.zeros((rows, LANES), jnp.int32)
+    for d in range(1, GROUP):
+        for side in sides:
+            clash = jnp.where((pltpu.roll(side, d, 1) == side) & (place >= d), 1, clash)
+    step = 1
+    while step < GROUP:
+        clash = jnp.maximum(clash, pltpu.roll(clash, step, 1))
+        step *= 2
+    clash_ref[...] = clash
+
+
+def index_words(dofs, rim):
+    rows = rim.shape[1] // LANES
+    word = lambda r, c: jax.ShapeDtypeStruct((r, c), jnp.int32)
+    return pl.pallas_call(
+        index_kernel,
+        out_shape=(word(*dofs.shape), word(rows, LANES), word(rows, LANES)),
+        in_specs=[VMEM, VMEM],
+        out_specs=(VMEM, VMEM, VMEM),
+    )(dofs, rim)
+
+
+def unpack_slices(base_ref, pieces, slice_rows, table, clear):
     at = 0
     for piece in pieces:
         for first in range(0, piece.shape[0], slice_rows):
@@ -53,15 +86,12 @@
                 low = low_lanes(CHUNK)
                 here = pl.multiple_of(base + start, CHUNK)
                 there = pl.multiple_of(base + slice_rows + start, CHUNK)
-                first_half = jnp.where(low, wide, 0.0)
-                second_half = jnp.where(low, pltpu.roll(wide, LANES // 2, 1), 0.0)
-                if stride == 1:
-                    table[pl.ds(here, CHUNK), :] = first_half
-                    table[pl.ds(there, CHUNK), :] = second_half
-                else:
-                    for at_row, value in ((here, first_half), (there, second_half)):
-                        table[pl.ds(2 * at_row, CHUNK, stride=2), :] = value
+                turned = pltpu.roll(wide, LANES // 2, 1)
+                for at_row, value in ((here, wide), (there, turned)):
+                    if clear:
+                        value = jnp.where(low, value, 0.0)
                         table[pl.ds(2 * at_row + 1, CHUNK, stride=2), :] = jnp.zeros_like(value)
+                    table[pl.ds(2 * at_row, CHUNK, stride=2), :] = value
                 return 0
 
             lax.fori_loop(0, slice_rows // CHUNK, step, 0)
@@ -69,36 +99,38 @@
 
 def rim_kernel(slice_rows, n_pieces, base_ref, rim_ref, *refs):
     pieces, (left_ref, right_ref), (table, taken) = refs[:n_pieces], refs[n_pieces:n_pieces + 2], refs[n_pieces + 2:]
-    unpack_slices(base_ref, pieces, slice_rows, table)
-    groups, group = rim_ref.shape[0] // 2, rim_ref.shape[1]
+    unpack_slices(base_ref, pieces, slice_rows, table, False)
+    groups, group = rim_ref.shape
     count = groups * group
-    for side, out in ((0, left_ref), (1, right_ref)):
-
-        def gather(g, _):
-            to = taken.at[pl.ds(pl.multiple_of(g * group, group), group)]
-            for j in range(group):
-                to[pl.ds(j, 1), :] = table[pl.ds(rim_ref[side * groups + g, j], 1), :]
-            return 0
-
-        lax.fori_loop(0, groups, gather, 0)
-        half = count // 2
-        out[...] = jnp.where(
-            low_lanes(half), taken[:half, :], pltpu.roll(taken[half:, :], LANES // 2, 1)
-        ).astype(BF16)
+
+    def gather(g, _):
+        first = pl.multiple_of(g * group, group)
+        to_left, to_right = taken.at[pl.ds(first, group)], taken.at[pl.ds(count + first, group)]
+        for j in range(group):
+            word = rim_ref[g, j]
+            to_left[pl.ds(j, 1), :] = table[pl.ds(word & 0xFFFF, 1), :]
+            to_right[pl.ds(j, 1), :] = table[pl.ds(word >> 16, 1), :]
+        return 0
+
+    lax.fori_loop(0, groups, gather, 0)
+    half = count // 2
+    for at, out in ((0, left_ref), (count, right_ref)):
+        first, second = taken[at:at + half, :], taken[at + half:at + count, :]
+        out[...] = jnp.where(low_lanes(half), first, pltpu.roll(second, LANES // 2, 1)).astype(BF16)
 
 
 def take_rim(bases, rim, pieces, slice_rows):
     total = 2 * sum(p.shape[0] for p in pieces)
-    count = rim.shape[1]
+    count = rim.size
     packed = jax.ShapeDtypeStruct((count // 2, LANES), BF16)
     return pl.pallas_call(
         functools.partial(rim_kernel, slice_rows, len(pieces)),
         out_shape=(packed, packed),
         in_specs=[SMEM, SMEM] + [VMEM] * len(pieces),
         out_specs=(VMEM, VMEM),
-        scratch_shapes=[pltpu.VMEM((total, LANES), F32), pltpu.VMEM((count, LANES), F32)],
+        scratch_shapes=[pltpu.VMEM((2 * total, LANES), F32), pltpu.VMEM((2 * count, LANES), F32)],
         compiler_params=pltpu.CompilerParams(vmem_limit_bytes=48 * 2**20),
-    )(bases, rim.reshape(-1, LANES), *pieces)
+    )(bases, rim, *pieces)
 
 
 def spread_rim(packed, out, high):
@@ -126,47 +158,51 @@
     pieces = refs[:n_pieces]
     out_ref = refs[n_pieces]
     table, rim_a, rim_b, got, acc, acc_low = refs[n_pieces + 1:]
-    unpack_slices(base_ref, pieces, slice_rows, table, 2)
+    unpack_slices(base_ref, pieces, slice_rows, table, True)
     spread_rim(from_left, rim_a, True)
     spread_rim(from_right, rim_b, False)
-    groups = clash_ref.shape[0]
-    group = rim_ref.shape[1]
+    rim_groups, group_rows = rim_ref.shape
 
     def add_rows(g, _):
-        first = pl.multiple_of(g * group, group)
-        new_a, new_b = rim_a.at[pl.ds(first, group)], rim_b.at[pl.ds(first, group)]
-
-        @pl.when(clash_ref[g] == 0)
-        def _():
-            at_a = [2 * rim_ref[g, j] for j in range(group)]
-            at_b = [2 * rim_ref[groups + g, j] + 1 for j in range(group)]
-            sum_a = [table[pl.ds(row, 1), :] + new_a[pl.ds(j, 1), :] for j, row in enumerate(at_a)]
-            sum_b = [table[pl.ds(row, 1), :] + new_b[pl.ds(j, 1), :] for j, row in enumerate(at_b)]
-            for j in range(group):
-                table[pl.ds(at_a[j], 1), :] = sum_a[j]
-                table[pl.ds(at_b[j], 1), :] = sum_b[j]
-
-        @pl.when(clash_ref[g] != 0)
-        def _():
-            def one(j, _):
-                table[pl.ds(2 * rim_ref[g, j], 1), :] += new_a[pl.ds(j, 1), :]
-                table[pl.ds(2 * rim_ref[groups + g, j] + 1, 1), :] += new_b[pl.ds(j, 1), :]
-                return 0
-
-            lax.fori_loop(0, group, one, 0)
-
-        return 0
-
-    lax.fori_loop(0, groups, add_rows, 0)
+        first = pl.multiple_of(g * group_rows, group_rows)
+        for k in range(0, group_rows, GROUP):
+            new_a, new_b = rim_a.at[pl.ds(first + k, GROUP)], rim_b.at[pl.ds(first + k, GROUP)]
+
+            @pl.when(clash_ref[g, k + GROUP - 1] == 0)
+            def _(k=k, new_a=new_a, new_b=new_b):
+                words = [rim_ref[g, k + j] for j in range(GROUP)]
+                at = [(word & 0xFFFF, (word >> 16) + 1) for word in words]
+                sums = [
+                    (table[pl.ds(a, 1), :] + new_a[pl.ds(j, 1), :], table[pl.ds(b, 1), :] + new_b[pl.ds(j, 1), :])
+                    for j, (a, b) in enumerate(at)
+                ]
+                for (a, b), (sum_a, sum_b) in zip(at, sums):
+                    table[pl.ds(a, 1), :] = sum_a
+                    table[pl.ds(b, 1), :] = sum_b
+
+            @pl.when(clash_ref[g, k + GROUP - 1] != 0)
+            def _(k=k, new_a=new_a, new_b=new_b):
+                def one(j, _):
+                    word = rim_ref[g, k + j]
+                    table[pl.ds(word & 0xFFFF, 1), :] += new_a[pl.ds(j, 1), :]
+                    table[pl.ds((word >> 16) + 1, 1), :] += new_b[pl.ds(j, 1), :]
+                    return 0
+
+                lax.fori_loop(0, GROUP, one, 0)
+
+        return 0
+
+    lax.fori_loop(0, rim_groups, add_rows, 0)
 
     n_blocks, size = dof_ref.shape
     modes = LANES // 2
 
     def gather(e, _):
         to = got.at[pl.ds(pl.multiple_of(2 * e * size, 2 * size), 2 * size)]
-        for j in range(size):
-            row = dof_ref[e, j]
-            to[pl.ds(2 * j, 2), :] = table[pl.ds(2 * row, 2), :]
+        for j in range(size // 2):
+            word = dof_ref[e, j]
+            to[pl.ds(2 * j, 2), :] = table[pl.ds(word & 0xFFFF, 2), :]
+            to[pl.ds(size + 2 * j, 2), :] = table[pl.ds(word >> 16, 2), :]
         return 0
 
     lax.fori_loop(0, n_blocks, gather, 0)
@@ -211,16 +247,9 @@
         out_ref[d] = rows[d * share:(d + 1) * share]
 
 
-def clashes(rim):
-    grouped = rim.reshape(2, -1, GROUP)
-    same = grouped[:, :, :, None] == grouped[:, :, None, :]
-    places = jnp.arange(GROUP)
-    return jnp.any(same & (places[:, None] < places[None, :]), axis=(0, 2, 3)).astype(jnp.int32)
-
-
-def contract_blocks(bases, rim, dofs, stiffness, from_left, from_right, pieces, slice_rows, parts, scale):
+def contract_blocks(bases, rim, clash, dofs, stiffness, from_left, from_right, pieces, slice_rows, parts, scale):
     total = 2 * sum(p.shape[0] for p in pieces)
-    count = rim.shape[1]
+    count = rim.size
     modes = LANES // 2
     n_blocks, size = dofs.shape
     wide = lambda n: pltpu.VMEM((n, LANES), F32)
@@ -234,7 +263,7 @@
             pltpu.VMEM((2 * modes, 2 * LANES), F32), pltpu.VMEM((modes, LANES), F32),
         ],
         compiler_params=pltpu.CompilerParams(vmem_limit_bytes=56 * 2**20),
-    )(bases, rim.reshape(-1, GROUP), clashes(rim), dofs, stiffness, from_left, from_right, *pieces)
+    )(bases, rim, clash, dofs, stiffness, from_left, from_right, *pieces)
 
 
 def ring_pieces(packed, index, count):
@@ -245,17 +274,24 @@
     )
     x, y = index // ring, index % ring
     base = lambda flip, dy: ((jnp.remainder(x + flip, 2)) * ring + jnp.remainder(y + dy, ring))
-    rows = packed.shape[0]
-    both = jnp.concatenate([packed, move(packed, 1, 0)], axis=0)
-    pieces, places = [both], [base(0, 0), base(1, 0)]
-    up = down = both
-    for k in range(1, ring // 2):
-        up, down = move(up, 0, 1), move(down, 0, -1)
-        pieces += [up, down]
-        places += [base(0, -k), base(1, -k), base(0, k), base(1, k)]
-    pieces += [move(up[:rows], 0, 1), move(down[rows:], 0, -1)]
-    places += [base(0, ring // 2), base(1, ring // 2)]
-    return pieces, jnp.stack(places).astype(jnp.int32)
+    own, steps, parts, split = [packed], [0], [], ring // 4
+    up = down = packed
+    sent = 0
+    for k in range(1, ring // 2 + 1):
+        up = move(up, 0, 1)
+        own.append(up)
+        steps.append(-k)
+        if k < ring // 2:
+            down = move(down, 0, -1)
+            own.append(down)
+            steps.append(k)
+        if k == split or k == ring // 2:
+            parts.append((move(jnp.concatenate(own[sent:], axis=0), 1, 0), steps[sent:]))
+            sent = len(own)
+    places = [base(0, dy) for dy in steps]
+    for _, dys in parts:
+        places += [base(1, dy) for dy in dys]
+    return own + [part for part, _ in parts], jnp.stack(places).astype(jnp.int32)
 
 
 def on_device(stiffness, dofmap, eigvecs, rim_rows, owner_map):
@@ -266,17 +302,19 @@
     blk, sub = lax.axis_index("blk"), lax.axis_index("sub")
     with jax.named_scope("pack"):
         packed = pack(eigvecs[0])
+    with jax.named_scope("index_words"):
+        dofs, rim, clash = index_words(dofmap[0], rim_rows[0])
     with jax.named_scope("gather_modes"):
         pieces, places = ring_pieces(packed, blk, blk_count)
         bases = places * own_rows
     with jax.named_scope("rim"):
-        left, right = take_rim(bases, rim_rows[0], pieces, slice_rows)
+        left, right = take_rim(bases, rim, pieces, slice_rows)
         from_left = lax.ppermute(right, "sub", [(i, i + 1) for i in range(sub_count - 1)])
         from_right = lax.ppermute(left, "sub", [(i + 1, i) for i in range(sub_count - 1)])
     with jax.named_scope("contract"):
         scale = 1.0 / math.sqrt(block_count * blk_count * block_size)
         share = contract_blocks(
-            bases, rim_rows[0], dofmap[0], stiffness[0], from_left, from_right, pieces, slice_rows, blk_count, scale
+            bases, rim, clash, dofs, stiffness[0], from_left, from_right, pieces, slice_rows, blk_count, scale
         )
     with jax.named_scope("sum_over_blk"):
         mine = jnp.sum(lax.all_to_all(share, "blk", 0, 0, tiled=True), axis=0)

time: 175 us -> 167 us (0.954)
  Pallas kernels: 60 us -> 46.6 us
  starting transfers between devices: 70.6 us -> 75.5 us
  waiting for transfers between devices: 35.5 us -> 38.1 us
    ppermute x1, starting transfers between devices: 1.92 us -> 16.1 us  [on_device(): lax.ppermute(right, 'sub', [(i, i + 1) for i in range(sub_count - 1)])]
    pallas_call x1, Pallas kernels: 48.8 us -> 36.1 us  [contract_blocks(): pl.pallas_call(functools.partial(main_kernel, slice_rows, len(pieces), sc...]
    ppermute x1, starting transfers between devices: 14.5 us -> 1.92 us  [on_device(): lax.ppermute(left, 'sub', [(i + 1, i) for i in range(sub_count - 1)])]
    ppermute x1, waiting for transfers between devices: 0.01 us -> 5.9 us  [on_device(): lax.ppermute(left, 'sub', [(i + 1, i) for i in range(sub_count - 1)])]
    all_to_all x1, starting transfers between devices: 15.7 us -> 20.1 us  [on_device(): arrived = lax.all_to_all(sent, 'sub', 0, 0, tiled=True)]
    ppermute x9, waiting for transfers between devices: 10.6 us -> 7.21 us  [ring_pieces(): lax.ppermute(value, 'blk', [(i, (i // ring + dx) % 2 * ring + (i % ring +...]
    unnamed x26 -> x34, local copies, waits for them, and re-layouts: 0.67 us -> 3.35 us
    pallas_call x1, Pallas kernels: 9.5 us -> 6.98 us  [take_rim(): pl.pallas_call(functools.partial(rim_kernel, slice_rows, len(pieces)), ou...]
  transfers between devices with their start and end apart: 13 -> 13, of which waited for: 8 -> 8; matrix products, arithmetic and copies ran while one was open for 2% -> 1% of each run, Pallas kernels for 0% -> 1%
where the time goes in v2:
time: 167 us
  starting transfers between devices  75.5 us (45%)
  Pallas kernels  46.6 us (28%)
  waiting for transfers between devices  38.1 us (23%)
  local copies, waits for them, and re-layouts  4.45 us (3%)
    pallas_call x1, Pallas kernels, contract_blocks(): pl.pallas_call(functools.partial(main_kernel, slice_rows, len(pieces), sc...  36.1 us
    ppermute x9, starting transfers between devices, ring_pieces(): lax.ppermute(value, 'blk', [(i, (i // ring + dx) % 2 * ring + (i % ring +...  31 us
    all_to_all x1, starting transfers between devices, on_device(): arrived = lax.all_to_all(sent, 'sub', 0, 0, tiled=True)  20.1 us
    all_to_all x1, waiting for transfers between devices, on_device(): arrived = lax.all_to_all(sent, 'sub', 0, 0, tiled=True)  16.4 us
    ppermute x1, starting transfers between devices, on_device(): lax.ppermute(right, 'sub', [(i, i + 1) for i in range(sub_count - 1)])  16.1 us
    ppermute x9, waiting for transfers between devices, ring_pieces(): lax.ppermute(value, 'blk', [(i, (i // ring + dx) % 2 * ring + (i % ring +...  7.21 us
    all_to_all x1, waiting for transfers between devices, on_device(): mine = jnp.sum(lax.all_to_all(share, 'blk', 0, 0, tiled=True), axis=0)  7.2 us
    pallas_call x1, Pallas kernels, take_rim(): pl.pallas_call(functools.partial(rim_kernel, slice_rows, len(pieces)), ou...  6.98 us
  transfers between devices with their start and end apart: 13, of which 8 were waited for; matrix products, arithmetic and copies ran while one was open for 1% of the time, Pallas kernels for 1%

profile of v2, /device:TPU:1, one launch (start us, length us, event | category | flops | bytes accessed | tf_op | source)
XLA Modules:
  0.0 166.5 jit_solution(12061007168950472114)
XLA Ops:
  0.0 1.7 %pack.1.refs_0_ = bf16[512,128]{1,0:T(8,128)(2,1)} custom-call(bf16[64,1024]{1,0:T(8,128)(2,1)} %bitcast.21), custom_call_target="tpu_custom_call" | custom-call | tf_op jit(solution)/shard_map/pack/pallas_call | solution.py:35
  1.7 4.0 %collective-permute-start = (bf16[512,128]{1,0:T(8,128)(2,1)}, bf16[512,128]{1,0:T(8,128)(2,1)S(1)}, u32[]{:S(2)}, u32[]{:S(2)}) collective-permute-start(bf16[512,128]{1,0:T(8,128)(2,1)} %pack.1.refs_0_), channel_id=1, source_target_pairs={{0,1},{1,2},{2,3},{3,4},{4,5},{5,6},{6,7},{7,0},{8,9},{9,10},{10,1... | collective-permute-start | bytes 393224 | tf_op jit(solution)/shard_map/gather_modes/ppermute | solution.py:271
  5.7 3.8 %collective-permute-start.1 = (bf16[512,128]{1,0:T(8,128)(2,1)}, bf16[512,128]{1,0:T(8,128)(2,1)S(1)}, u32[]{:S(2)}, u32[]{:S(2)}) collective-permute-start(bf16[512,128]{1,0:T(8,128)(2,1)} %pack.1.refs_0_), channel_id=1, source_target_pairs={{0,7},{1,0},{2,1},{3,2},{4,3},{5,4},{6,5},{7,6},{8,15},{9,8},{10,9... | collective-permute-start | bytes 393224 | tf_op jit(solution)/shard_map/gather_modes/ppermute | solution.py:271
  9.5 0.6 collective-permute-done.refs_1_
  10.2 1.9 %collective-permute-start.2 = (bf16[512,128]{1,0:T(8,128)(2,1)S(1)}, bf16[512,128]{1,0:T(8,128)(2,1)S(1)}, u32[]{:S(2)}, u32[]{:S(2)}) collective-permute-start(bf16[512,128]{1,0:T(8,128)(2,1)S(1)} %collective-permute-done.refs_1_), channel_id=1, source_target_pairs={{0,1},{1,2},{2,3},{3,4},{4,5},{5,6},{6,7},{7,0},{8,9},{9,10},{10,1... | collective-permute-start | bytes 393224 | tf_op jit(solution)/shard_map/gather_modes/ppermute | solution.py:271
  12.1 0.9 constant_dynamic-update-slice_fusion.4
  13.0 0.0 collective-permute-done.1.refs_2_
  13.0 0.0 copy-start.4
  13.0 4.6 %collective-permute-start.3 = (bf16[512,128]{1,0:T(8,128)(2,1)S(1)}, bf16[512,128]{1,0:T(8,128)(2,1)S(1)}, u32[]{:S(2)}, u32[]{:S(2)}) collective-permute-start(bf16[512,128]{1,0:T(8,128)(2,1)S(1)} %collective-permute-done.1.refs_2_), channel_id=1, source_target_pairs={{0,7},{1,0},{2,1},{3,2},{4,3},{5,4},{6,5},{7,6},{8,15},{9,8},{10,9... | collective-permute-start | bytes 393224 | tf_op jit(solution)/shard_map/gather_modes/ppermute | solution.py:271
  17.6 0.0 collective-permute-done.2.refs_3_
  17.6 0.0 copy-start.5
  17.6 1.9 %collective-permute-start.4 = (bf16[512,128]{1,0:T(8,128)(2,1)S(1)}, bf16[512,128]{1,0:T(8,128)(2,1)S(1)}, u32[]{:S(2)}, u32[]{:S(2)}) collective-permute-start(bf16[512,128]{1,0:T(8,128)(2,1)S(1)} %collective-permute-done.2.refs_3_), channel_id=1, source_target_pairs={{0,1},{1,2},{2,3},{3,4},{4,5},{5,6},{6,7},{7,0},{8,9},{9,10},{10,1... | collective-permute-start | bytes 393224 | tf_op jit(solution)/shard_map/gather_modes/ppermute | solution.py:271
  19.6 0.0 collective-permute-done.3.refs_4_
  19.6 0.0 copy-start.6
  19.6 4.9 %collective-permute-start.5 = (bf16[512,128]{1,0:T(8,128)(2,1)S(1)}, bf16[512,128]{1,0:T(8,128)(2,1)S(1)}, u32[]{:S(2)}, u32[]{:S(2)}) collective-permute-start(bf16[512,128]{1,0:T(8,128)(2,1)S(1)} %collective-permute-done.3.refs_4_), channel_id=1, source_target_pairs={{0,7},{1,0},{2,1},{3,2},{4,3},{5,4},{6,5},{7,6},{8,15},{9,8},{10,9... | collective-permute-start | bytes 393224 | tf_op jit(solution)/shard_map/gather_modes/ppermute | solution.py:271
  24.5 0.0 collective-permute-done.4.refs_5_
  24.6 1.9 %collective-permute-start.6 = (bf16[512,128]{1,0:T(8,128)(2,1)S(1)}, bf16[512,128]{1,0:T(8,128)(2,1)S(1)}, u32[]{:S(2)}, u32[]{:S(2)}) collective-permute-start(bf16[512,128]{1,0:T(8,128)(2,1)S(1)} %collective-permute-done.4.refs_5_), channel_id=1, source_target_pairs={{0,1},{1,2},{2,3},{3,4},{4,5},{5,6},{6,7},{7,0},{8,9},{9,10},{10,1... | collective-permute-start | bytes 393224 | tf_op jit(solution)/shard_map/gather_modes/ppermute | solution.py:271
  26.5 4.0 %collective-permute-start.7 = (bf16[2560,128]{1,0:T(8,128)(2,1)S(1)}, bf16[2560,128]{1,0:T(8,128)(2,1)S(1)}, u32[]{:S(2)}, u32[]{:S(2)}) collective-permute-start(bf16[2560,128]{1,0:T(8,128)(2,1)S(1)} %constant_dynamic-update-slice_fusion), channel_id=1, source_target_pairs={{0,8},{1,9},{2,10},{3,11},{4,12},{5,13},{6,14},{7,15},{8,0},{9,1},... | collective-permute-start | bytes 1966088 | tf_op jit(solution)/shard_map/gather_modes/ppermute | solution.py:271
  30.5 0.0 collective-permute-done.5.refs_6_
  30.5 0.0 copy-start.8
  30.5 1.0 collective-permute-done.6.refs_7_
  31.5 4.0 %collective-permute-start.8 = (bf16[1536,128]{1,0:T(8,128)(2,1)S(1)}, bf16[1536,128]{1,0:T(8,128)(2,1)S(1)}, u32[]{:S(2)}, u32[]{:S(2)}) collective-permute-start(bf16[1536,128]{1,0:T(8,128)(2,1)S(1)} %pad_maximum_fusion), channel_id=1, source_target_pairs={{0,8},{1,9},{2,10},{3,11},{4,12},{5,13},{6,14},{7,15},{8,0},{9,1},... | collective-permute-start | bytes 1179656 | tf_op jit(solution)/shard_map/gather_modes/ppermute | solution.py:271
  35.7 1.8 %index_words.1 = (s32[128,128]{1,0:T(8,128)}, s32[16,128]{1,0:T(8,128)}, s32[16,128]{1,0:T(8,128)}) custom-call(s32[128,128]{1,0:T(8,128)} %bitcast.22, s32[2,2048]{1,0:T(2,128)} %bitcast.23), custom_call_target="tpu_custom_call" | custom-call | tf_op jit(solution)/shard_map/index_words/pallas_call | solution.py:68
  37.5 0.1 stack.67
  37.7 0.0 copy-start.11
  37.7 0.8 collective-permute-done.7.refs_8_
  38.5 4.8 %collective-permute-done.8.refs_9_ = bf16[1536,128]{1,0:T(8,128)(2,1)S(1)} collective-permute-done((bf16[1536,128]{1,0:T(8,128)(2,1)S(1)}, bf16[1536,128]{1,0:T(8,128)(2,1)S(1)}, u32[]{:S(2)}, u32[]{:S(2)}) %collective-permute-start.8) | collective-permute-done | bytes 393248 | tf_op jit(solution)/shard_map/gather_modes/ppermute | solution.py:271
  43.3 1.0 copy-done.1
  44.3 0.7 copy-done.10
  45.0 7.0 %rim.1 = (bf16[1024,128]{1,0:T(8,128)(2,1)S(1)}, bf16[1024,128]{1,0:T(8,128)(2,1)S(1)}) custom-call(s32[16]{0:T(128)S(1)} %broadcast_multiply_fusion.base_ref, s32[16,128]{1,0:T(8,128)S(1)} %copy-done.10, bf16[512,128]{1,0:T(8,128)(2,1)S(1)} %copy-done.1, bf16[512,128]{1,0:T(8,128)(2,1)S(1)} %collective-permute-done.refs_1_, ...), custom_call_target="tpu_custom_call" | custom-call | tf_op jit(solution)/shard_map/rim/pallas_call | solution.py:126
  52.0 16.1 %collective-permute-start.9 = (bf16[1024,128]{1,0:T(8,128)(2,1)S(1)}, bf16[1024,128]{1,0:T(8,128)(2,1)S(1)}, u32[]{:S(2)}, u32[]{:S(2)}) collective-permute-start(bf16[1024,128]{1,0:T(8,128)(2,1)S(1)} %get-tuple-element.13), channel_id=1, source_target_pairs={{0,16},{16,32},{32,48},{48,64},{64,80},{80,96},{96,112},{112,128},... | collective-permute-start | bytes 786440 | tf_op jit(solution)/shard_map/rim/ppermute | solution.py:312
  68.1 1.9 %collective-permute-start.10 = (bf16[1024,128]{1,0:T(8,128)(2,1)S(1)}, bf16[1024,128]{1,0:T(8,128)(2,1)S(1)}, u32[]{:S(2)}, u32[]{:S(2)}) collective-permute-start(bf16[1024,128]{1,0:T(8,128)(2,1)S(1)} %get-tuple-element.14), channel_id=1, source_target_pairs={{16,0},{32,16},{48,32},{64,48},{80,64},{96,80},{112,96},{128,112},... | collective-permute-start | bytes 786440 | tf_op jit(solution)/shard_map/rim/ppermute | solution.py:313
  70.1 1.3 collective-permute-done.9.from_left
  71.4 5.9 %collective-permute-done.10.from_right = bf16[1024,128]{1,0:T(8,128)(2,1)S(1)} collective-permute-done((bf16[1024,128]{1,0:T(8,128)(2,1)S(1)}, bf16[1024,128]{1,0:T(8,128)(2,1)S(1)}, u32[]{:S(2)}, u32[]{:S(2)}) %collective-permute-start.10) | collective-permute-done | bytes 262176 | tf_op jit(solution)/shard_map/rim/ppermute | solution.py:313
  77.4 0.6 copy-done.13
  78.0 36.1 %contract.1 = f32[16,4,192]{2,1,0:T(4,128)} custom-call(s32[16]{0:T(128)} %copy-done.11, s32[16,128]{1,0:T(8,128)} %get-tuple-element.10.rim_ref, s32[16,128]{1,0:T(8,128)} %get-tuple-element.11.clash_ref, s32[128,128]{1,0:T(8,128)} %get-tuple-element.12.dof_ref, bf16[128,128,128]{2,1,0:T(8,128)(2,1)} %bitcast.20, bf16[1024,128]{1,0:T(8,128)(2,1)} %copy-done.12, ...), custom_call_target="tpu_custom_call" | custom-call | tf_op jit(solution)/shard_map/contract/pallas_call | solution.py:256
  114.1 6.4 %all-to-all-start = ((f32[16,4,192]{2,1,0:T(4,128)}), f32[16,4,192]{2,1,0:T(4,128)S(1)}, u32[]{:S(2)}, u32[]{:S(2)}) async-start(f32[16,4,192]{2,1,0:T(4,128)} %contract.1), calls=%async_computation | async-start | bytes 131072 | tf_op jit(solution)/shard_map/sum_over_blk/all_to_all | solution.py:320
  120.5 0.2 convert_reduce_fusion
  120.7 7.2 %all-to-all-done = f32[16,4,192]{2,1,0:T(4,128)S(1)} async-done(((f32[16,4,192]{2,1,0:T(4,128)}), f32[16,4,192]{2,1,0:T(4,128)S(1)}, u32[]{:S(2)}, u32[]{:S(2)}) %all-to-all-start) | async-done | bytes 49184 | tf_op jit(solution)/shard_map/sum_over_blk/all_to_all | solution.py:320
  127.9 0.7 broadcast_in_dim.62
  128.6 20.1 %all-to-all-start.1 = ((f32[48,4,192]{2,1,0:T(4,128)}), f32[48,4,192]{2,1,0:T(4,128)S(1)}, u32[]{:S(2)}, u32[]{:S(2)}) async-start(f32[48,4,192]{2,1,0:T(4,128)} %broadcast_in_dim.62), calls=%async_computation.1 | async-start | bytes 393216 | tf_op jit(solution)/shard_map/relay/all_to_all | solution.py:323
  148.7 0.1 fusion.3
  148.8 0.1 concatenate.18
  148.9 16.4 %all-to-all-done.1 = f32[48,4,192]{2,1,0:T(4,128)S(1)} async-done(((f32[48,4,192]{2,1,0:T(4,128)}), f32[48,4,192]{2,1,0:T(4,128)S(1)}, u32[]{:S(2)}, u32[]{:S(2)}) %all-to-all-start.1) | async-done | bytes 147488 | tf_op jit(solution)/shard_map/relay/all_to_all | solution.py:323
  165.3 0.1 fusion.2
  165.5 0.1 select_reduce_fusion.2
  165.6 0.2 select_reduce_fusion
  165.8 0.7 pad_maximum_fusion.1
  (35 shorter events, 0.2 us)
Async XLA Ops:
  0.0 70.0 %copy-start.14 = (s32[48]{0:T(128)S(1)}, s32[48]{0:T(128)}, u32[]{:S(2)}) copy-start(s32[48]{0:T(128)} %param.9) | copy-start | bytes 580
  1.7 8.5 %collective-permute-start = (bf16[512,128]{1,0:T(8,128)(2,1)}, bf16[512,128]{1,0:T(8,128)(2,1)S(1)}, u32[]{:S(2)}, u32[]{:S(2)}) collective-permute-start(bf16[512,128]{1,0:T(8,128)(2,1)} %pack.1.refs_0_), channel_id=1, source_target_pairs={{0,1},{1,2},{2,3},{3,4},{4,5},{5,6},{6,7},{7,0},{8,9},{9,10},{10,1... | collective-permute-start | bytes 393224 | tf_op jit(solution)/shard_map/gather_modes/ppermute | solution.py:271
  5.7 7.3 %collective-permute-start.1 = (bf16[512,128]{1,0:T(8,128)(2,1)}, bf16[512,128]{1,0:T(8,128)(2,1)S(1)}, u32[]{:S(2)}, u32[]{:S(2)}) collective-permute-start(bf16[512,128]{1,0:T(8,128)(2,1)} %pack.1.refs_0_), channel_id=1, source_target_pairs={{0,7},{1,0},{2,1},{3,2},{4,3},{5,4},{6,5},{7,6},{8,15},{9,8},{10,9... | collective-permute-start | bytes 393224 | tf_op jit(solution)/shard_map/gather_modes/ppermute | solution.py:271
  10.2 67.1 %copy-start.3 = (bf16[512,128]{1,0:T(8,128)(2,1)}, bf16[512,128]{1,0:T(8,128)(2,1)S(1)}, u32[]{:S(2)}) copy-start(bf16[512,128]{1,0:T(8,128)(2,1)S(1)} %collective-permute-done.refs_1_) | copy-start | bytes 393220
  10.2 7.5 %collective-permute-start.2 = (bf16[512,128]{1,0:T(8,128)(2,1)S(1)}, bf16[512,128]{1,0:T(8,128)(2,1)S(1)}, u32[]{:S(2)}, u32[]{:S(2)}) collective-permute-start(bf16[512,128]{1,0:T(8,128)(2,1)S(1)} %collective-permute-done.refs_1_), channel_id=1, source_target_pairs={{0,1},{1,2},{2,3},{3,4},{4,5},{5,6},{6,7},{7,0},{8,9},{9,10},{10,1... | collective-permute-start | bytes 393224 | tf_op jit(solution)/shard_map/gather_modes/ppermute | solution.py:271
  13.0 64.3 %copy-start.4 = (bf16[512,128]{1,0:T(8,128)(2,1)}, bf16[512,128]{1,0:T(8,128)(2,1)S(1)}, u32[]{:S(2)}) copy-start(bf16[512,128]{1,0:T(8,128)(2,1)S(1)} %collective-permute-done.1.refs_2_) | copy-start | bytes 393220
  13.0 6.6 %collective-permute-start.3 = (bf16[512,128]{1,0:T(8,128)(2,1)S(1)}, bf16[512,128]{1,0:T(8,128)(2,1)S(1)}, u32[]{:S(2)}, u32[]{:S(2)}) collective-permute-start(bf16[512,128]{1,0:T(8,128)(2,1)S(1)} %collective-permute-done.1.refs_2_), channel_id=1, source_target_pairs={{0,7},{1,0},{2,1},{3,2},{4,3},{5,4},{6,5},{7,6},{8,15},{9,8},{10,9... | collective-permute-start | bytes 393224 | tf_op jit(solution)/shard_map/gather_modes/ppermute | solution.py:271
  17.6 59.7 %copy-start.5 = (bf16[512,128]{1,0:T(8,128)(2,1)}, bf16[512,128]{1,0:T(8,128)(2,1)S(1)}, u32[]{:S(2)}) copy-start(bf16[512,128]{1,0:T(8,128)(2,1)S(1)} %collective-permute-done.2.refs_3_) | copy-start | bytes 393220
  17.6 6.9 %collective-permute-start.4 = (bf16[512,128]{1,0:T(8,128)(2,1)S(1)}, bf16[512,128]{1,0:T(8,128)(2,1)S(1)}, u32[]{:S(2)}, u32[]{:S(2)}) collective-permute-start(bf16[512,128]{1,0:T(8,128)(2,1)S(1)} %collective-permute-done.2.refs_3_), channel_id=1, source_target_pairs={{0,1},{1,2},{2,3},{3,4},{4,5},{5,6},{6,7},{7,0},{8,9},{9,10},{10,1... | collective-permute-start | bytes 393224 | tf_op jit(solution)/shard_map/gather_modes/ppermute | solution.py:271
  19.6 57.7 %copy-start.6 = (bf16[512,128]{1,0:T(8,128)(2,1)}, bf16[512,128]{1,0:T(8,128)(2,1)S(1)}, u32[]{:S(2)}) copy-start(bf16[512,128]{1,0:T(8,128)(2,1)S(1)} %collective-permute-done.3.refs_4_) | copy-start | bytes 393220
  19.6 10.9 %collective-permute-start.5 = (bf16[512,128]{1,0:T(8,128)(2,1)S(1)}, bf16[512,128]{1,0:T(8,128)(2,1)S(1)}, u32[]{:S(2)}, u32[]{:S(2)}) collective-permute-start(bf16[512,128]{1,0:T(8,128)(2,1)S(1)} %collective-permute-done.3.refs_4_), channel_id=1, source_target_pairs={{0,7},{1,0},{2,1},{3,2},{4,3},{5,4},{6,5},{7,6},{8,15},{9,8},{10,9... | collective-permute-start | bytes 393224 | tf_op jit(solution)/shard_map/gather_modes/ppermute | solution.py:271
  24.6 52.8 %copy-start.7 = (bf16[512,128]{1,0:T(8,128)(2,1)}, bf16[512,128]{1,0:T(8,128)(2,1)S(1)}, u32[]{:S(2)}) copy-start(bf16[512,128]{1,0:T(8,128)(2,1)S(1)} %collective-permute-done.4.refs_5_) | copy-start | bytes 393220
  24.6 6.9 %collective-permute-start.6 = (bf16[512,128]{1,0:T(8,128)(2,1)S(1)}, bf16[512,128]{1,0:T(8,128)(2,1)S(1)}, u32[]{:S(2)}, u32[]{:S(2)}) collective-permute-start(bf16[512,128]{1,0:T(8,128)(2,1)S(1)} %collective-permute-done.4.refs_5_), channel_id=1, source_target_pairs={{0,1},{1,2},{2,3},{3,4},{4,5},{5,6},{6,7},{7,0},{8,9},{9,10},{10,1... | collective-permute-start | bytes 393224 | tf_op jit(solution)/shard_map/gather_modes/ppermute | solution.py:271
  26.5 12.0 %collective-permute-start.7 = (bf16[2560,128]{1,0:T(8,128)(2,1)S(1)}, bf16[2560,128]{1,0:T(8,128)(2,1)S(1)}, u32[]{:S(2)}, u32[]{:S(2)}) collective-permute-start(bf16[2560,128]{1,0:T(8,128)(2,1)S(1)} %constant_dynamic-update-slice_fusion), channel_id=1, source_target_pairs={{0,8},{1,9},{2,10},{3,11},{4,12},{5,13},{6,14},{7,15},{8,0},{9,1},... | collective-permute-start | bytes 1966088 | tf_op jit(solution)/shard_map/gather_modes/ppermute | solution.py:271
  30.5 46.8 %copy-start.8 = (bf16[512,128]{1,0:T(8,128)(2,1)}, bf16[512,128]{1,0:T(8,128)(2,1)S(1)}, u32[]{:S(2)}) copy-start(bf16[512,128]{1,0:T(8,128)(2,1)S(1)} %collective-permute-done.5.refs_6_) | copy-start | bytes 393220
  31.5 45.9 %copy-start.9 = (bf16[512,128]{1,0:T(8,128)(2,1)}, bf16[512,128]{1,0:T(8,128)(2,1)S(1)}, u32[]{:S(2)}) copy-start(bf16[512,128]{1,0:T(8,128)(2,1)S(1)} %collective-permute-done.6.refs_7_) | copy-start | bytes 393220
  31.5 11.7 %collective-permute-start.8 = (bf16[1536,128]{1,0:T(8,128)(2,1)S(1)}, bf16[1536,128]{1,0:T(8,128)(2,1)S(1)}, u32[]{:S(2)}, u32[]{:S(2)}) collective-permute-start(bf16[1536,128]{1,0:T(8,128)(2,1)S(1)} %pad_maximum_fusion), channel_id=1, source_target_pairs={{0,8},{1,9},{2,10},{3,11},{4,12},{5,13},{6,14},{7,15},{8,0},{9,1},... | collective-permute-start | bytes 1179656 | tf_op jit(solution)/shard_map/gather_modes/ppermute | solution.py:271
  37.7 39.7 %copy-start.11 = (s32[16]{0:T(128)}, s32[16]{0:T(128)S(1)}, u32[]{:S(2)}) copy-start(s32[16]{0:T(128)S(1)} %broadcast_multiply_fusion.base_ref) | copy-start | bytes 196
  38.5 38.9 %copy-start = (bf16[2560,128]{1,0:T(8,128)(2,1)}, bf16[2560,128]{1,0:T(8,128)(2,1)S(1)}, u32[]{:S(2)}) copy-start(bf16[2560,128]{1,0:T(8,128)(2,1)S(1)} %collective-permute-done.7.refs_8_) | copy-start | bytes 1966084
  43.3 34.1 %copy-start.2 = (bf16[1536,128]{1,0:T(8,128)(2,1)}, bf16[1536,128]{1,0:T(8,128)(2,1)S(1)}, u32[]{:S(2)}) copy-start(bf16[1536,128]{1,0:T(8,128)(2,1)S(1)} %collective-permute-done.8.refs_9_) | copy-start | bytes 1179652
  43.3 1.0 copy-start.1
  44.3 0.7 copy-start.10
  52.0 19.4 %collective-permute-start.9 = (bf16[1024,128]{1,0:T(8,128)(2,1)S(1)}, bf16[1024,128]{1,0:T(8,128)(2,1)S(1)}, u32[]{:S(2)}, u32[]{:S(2)}) collective-permute-start(bf16[1024,128]{1,0:T(8,128)(2,1)S(1)} %get-tuple-element.13), channel_id=1, source_target_pairs={{0,16},{16,32},{32,48},{48,64},{64,80},{80,96},{96,112},{112,128},... | collective-permute-start | bytes 786440 | tf_op jit(solution)/shard_map/rim/ppermute | solution.py:312
  68.1 9.2 %collective-permute-start.10 = (bf16[1024,128]{1,0:T(8,128)(2,1)S(1)}, bf16[1024,128]{1,0:T(8,128)(2,1)S(1)}, u32[]{:S(2)}, u32[]{:S(2)}) collective-permute-start(bf16[1024,128]{1,0:T(8,128)(2,1)S(1)} %get-tuple-element.14), channel_id=1, source_target_pairs={{16,0},{32,16},{48,32},{64,48},{80,64},{96,80},{112,96},{128,112},... | collective-permute-start | bytes 786440 | tf_op jit(solution)/shard_map/rim/ppermute | solution.py:313
  71.4 6.0 %copy-start.12 = (bf16[1024,128]{1,0:T(8,128)(2,1)}, bf16[1024,128]{1,0:T(8,128)(2,1)S(1)}, u32[]{:S(2)}) copy-start(bf16[1024,128]{1,0:T(8,128)(2,1)S(1)} %collective-permute-done.9.from_left) | copy-start | bytes 786436
  77.3 0.7 copy-start.13
  114.1 13.8 %all-to-all-start = ((f32[16,4,192]{2,1,0:T(4,128)}), f32[16,4,192]{2,1,0:T(4,128)S(1)}, u32[]{:S(2)}, u32[]{:S(2)}) async-start(f32[16,4,192]{2,1,0:T(4,128)} %contract.1), calls=%async_computation | async-start | bytes 131072 | tf_op jit(solution)/shard_map/sum_over_blk/all_to_all | solution.py:320
  128.6 36.7 %all-to-all-start.1 = ((f32[48,4,192]{2,1,0:T(4,128)}), f32[48,4,192]{2,1,0:T(4,128)S(1)}, u32[]{:S(2)}, u32[]{:S(2)}) async-start(f32[48,4,192]{2,1,0:T(4,128)} %broadcast_in_dim.62), calls=%async_computation.1 | async-start | bytes 393216 | tf_op jit(solution)/shard_map/relay/all_to_all | solution.py:323

commit v3 on v2

--- a/solution.py
+++ b/solution.py
@@ -12,7 +12,7 @@
 LANES = 128
 CHUNK = 256
 GROUP = 16
-TOGETHER = 8
+TOGETHER = 16
 F32 = jnp.float32
 BF16 = jnp.bfloat16
 VMEM = pl.BlockSpec(memory_space=pltpu.VMEM)
@@ -37,6 +37,7 @@
         out_shape=jax.ShapeDtypeStruct((width // 2, 2 * count), BF16),
         in_specs=[VMEM],
         out_specs=VMEM,
+        compiler_params=pltpu.CompilerParams(vmem_limit_bytes=8 * 2**20),
     )(modes)
 
 
@@ -70,6 +71,7 @@
         out_shape=(word(*dofs.shape), word(rows, LANES), word(rows, LANES)),
         in_specs=[VMEM, VMEM],
         out_specs=(VMEM, VMEM, VMEM),
+        compiler_params=pltpu.CompilerParams(vmem_limit_bytes=8 * 2**20),
     )(dofs, rim)
 
 
@@ -129,7 +131,7 @@
         in_specs=[SMEM, SMEM] + [VMEM] * len(pieces),
         out_specs=(VMEM, VMEM),
         scratch_shapes=[pltpu.VMEM((2 * total, LANES), F32), pltpu.VMEM((2 * count, LANES), F32)],
-        compiler_params=pltpu.CompilerParams(vmem_limit_bytes=48 * 2**20),
+        compiler_params=pltpu.CompilerParams(vmem_limit_bytes=28 * 2**20),
     )(bases, rim, *pieces)
 
 
@@ -262,11 +264,42 @@
             wide(2 * total), wide(count), wide(count), wide(2 * n_blocks * size),
             pltpu.VMEM((2 * modes, 2 * LANES), F32), pltpu.VMEM((modes, LANES), F32),
         ],
-        compiler_params=pltpu.CompilerParams(vmem_limit_bytes=56 * 2**20),
+        compiler_params=pltpu.CompilerParams(vmem_limit_bytes=44 * 2**20),
     )(bases, rim, clash, dofs, stiffness, from_left, from_right, *pieces)
 
 
-def ring_pieces(packed, index, count):
+def slots_kernel(me_ref, owner_ref, arrived_ref, out_ref):
+    count = arrived_ref.shape[0]
+    shape = arrived_ref.shape[1:]
+    part = lax.broadcasted_iota(jnp.int32, shape, 1) // (LANES // 2)
+    out_ref[...] = jnp.zeros_like(out_ref)
+
+    def step(t, slot):
+        mine = owner_ref[t] == me_ref[0]
+
+        @pl.when(mine)
+        def _():
+            before = jnp.where(t > 0, arrived_ref[jnp.maximum(t - 1, 0)], 0.0)
+            after = jnp.where(t < count - 1, arrived_ref[jnp.minimum(t + 1, count - 1)], 0.0)
+            row = jnp.where(part == 0, before, jnp.where(part == 1, arrived_ref[t], after))
+            out_ref[jnp.minimum(slot, CAP - 1)] = row
+
+        return slot + mine.astype(jnp.int32)
+
+    lax.fori_loop(0, count, step, 0)
+
+
+def fill_slots(me, owner_map, arrived):
+    return pl.pallas_call(
+        slots_kernel,
+        out_shape=jax.ShapeDtypeStruct((CAP,) + arrived.shape[1:], F32),
+        in_specs=[SMEM, SMEM, VMEM],
+        out_specs=VMEM,
+        compiler_params=pltpu.CompilerParams(vmem_limit_bytes=8 * 2**20),
+    )(me.astype(jnp.int32), owner_map, arrived)
+
+
+def ring_pieces(packed, index, count, beside):
     ring = count // 2
     move = lambda value, dx, dy: lax.ppermute(
         value, "blk",
@@ -274,24 +307,18 @@
     )
     x, y = index // ring, index % ring
     base = lambda flip, dy: ((jnp.remainder(x + flip, 2)) * ring + jnp.remainder(y + dy, ring))
-    own, steps, parts, split = [packed], [0], [], ring // 4
-    up = down = packed
-    sent = 0
-    for k in range(1, ring // 2 + 1):
-        up = move(up, 0, 1)
-        own.append(up)
-        steps.append(-k)
-        if k < ring // 2:
-            down = move(down, 0, -1)
-            own.append(down)
-            steps.append(k)
-        if k == split or k == ring // 2:
-            parts.append((move(jnp.concatenate(own[sent:], axis=0), 1, 0), steps[sent:]))
-            sent = len(own)
-    places = [base(0, dy) for dy in steps]
-    for _, dys in parts:
-        places += [base(1, dy) for dy in dys]
-    return own + [part for part, _ in parts], jnp.stack(places).astype(jnp.int32)
+    rows = packed.shape[0]
+    both = jnp.concatenate([packed, move(packed, 1, 0)], axis=0)
+    both, beside = lax.optimization_barrier((both, beside))
+    pieces, places = [both], [base(0, 0), base(1, 0)]
+    up = down = both
+    for k in range(1, ring // 2):
+        up, down = move(up, 0, 1), move(down, 0, -1)
+        pieces += [up, down]
+        places += [base(0, -k), base(1, -k), base(0, k), base(1, k)]
+    pieces += [move(up[:rows], 0, 1), move(down[rows:], 0, -1)]
+    places += [base(0, ring // 2), base(1, ring // 2)]
+    return pieces, jnp.stack(places).astype(jnp.int32), beside
 
 
 def on_device(stiffness, dofmap, eigvecs, rim_rows, owner_map):
@@ -303,9 +330,9 @@
     with jax.named_scope("pack"):
         packed = pack(eigvecs[0])
     with jax.named_scope("index_words"):
-        dofs, rim, clash = index_words(dofmap[0], rim_rows[0])
+        dofs, rim, clash = index_words(dofmap[0], lax.optimization_barrier((rim_rows[0], packed))[0])
     with jax.named_scope("gather_modes"):
-        pieces, places = ring_pieces(packed, blk, blk_count)
+        pieces, places, (dofs, rim, clash) = ring_pieces(packed, blk, blk_count, (dofs, rim, clash))
         bases = places * own_rows
     with jax.named_scope("rim"):
         left, right = take_rim(bases, rim, pieces, slice_rows)
@@ -322,21 +349,7 @@
         sent = jnp.broadcast_to(mine[None], (sub_count,) + mine.shape)
         arrived = lax.all_to_all(sent, "sub", 0, 0, tiled=True)
     with jax.named_scope("slots"):
-        positions = jnp.arange(sub_count, dtype=jnp.int32)
-        same_owner = owner_map[:, None] == owner_map[None, :]
-        earlier = positions[None, :] < positions[:, None]
-        slot_rank = jnp.sum((same_owner & earlier).astype(jnp.int32), axis=1)
-        slot_ids = jnp.arange(CAP, dtype=jnp.int32)
-        chosen = (owner_map[None, :] == sub) & (slot_rank[None, :] == slot_ids[:, None])
-        none = jnp.zeros((CAP, 1), bool)
-        from_prev = jnp.concatenate([chosen[:, 1:], none], axis=1)
-        from_next = jnp.concatenate([none, chosen[:, :-1]], axis=1)
-        modes = LANES // 2
-        parts = [
-            jnp.sum(jnp.where(pick[:, :, None, None], arrived[None, :, :, p * modes:(p + 1) * modes], 0.0), axis=1)
-            for p, pick in enumerate((from_prev, chosen, from_next))
-        ]
-        return jnp.concatenate(parts, axis=2)
+        return fill_slots(jnp.reshape(sub, (1,)), owner_map, arrived)
 
 
 def solution(mesh):

time: 167 us -> 160 us (0.958)
  blocking collectives: 0 us -> 11.2 us
  starting transfers between devices: 75.5 us -> 67.6 us
  waiting for transfers between devices: 38.1 us -> 31.9 us
  Pallas kernels: 46.6 us -> 42.9 us
    all_to_all x0 -> x1, blocking collectives: none -> 11.2 us  [on_device(): mine = jnp.sum(lax.all_to_all(share, 'blk', 0, 0, tiled=True), axis=0)]
    ppermute x1, starting transfers between devices: 16.1 us -> 6.49 us  [on_device(): lax.ppermute(right, 'sub', [(i, i + 1) for i in range(sub_count - 1)])]
    all_to_all x1 -> x0, waiting for transfers between devices: 7.2 us -> none  [on_device(): mine = jnp.sum(lax.all_to_all(share, 'blk', 0, 0, tiled=True), axis=0)]
    ppermute x9, waiting for transfers between devices: 7.21 us -> 14.2 us  [ring_pieces(): lax.ppermute(value, 'blk', [(i, (i // ring + dx) % 2 * ring + (i % ring +...]
    all_to_all x1 -> x0, starting transfers between devices: 6.38 us -> none  [on_device(): mine = jnp.sum(lax.all_to_all(share, 'blk', 0, 0, tiled=True), axis=0)]
    ppermute x1, starting transfers between devices: 1.92 us -> 8.08 us  [on_device(): lax.ppermute(left, 'sub', [(i + 1, i) for i in range(sub_count - 1)])]
    ppermute x1, waiting for transfers between devices: 5.9 us -> 1.13 us  [on_device(): lax.ppermute(left, 'sub', [(i + 1, i) for i in range(sub_count - 1)])]
    pallas_call x1, Pallas kernels: 36.1 us -> 33.5 us  [contract_blocks(): pl.pallas_call(functools.partial(main_kernel, slice_rows, len(pieces), sc...]
  transfers between devices with their start and end apart: 13 -> 12, of which waited for: 8 -> 9; matrix products, arithmetic and copies ran while one was open for 1% -> 0% of each run, Pallas kernels for 1% -> 0%
where the time goes in v3:
time: 160 us; the launch traced here: 159 us
  starting transfers between devices  67.6 us (42%)
  Pallas kernels  42.9 us (27%)
  waiting for transfers between devices  31.9 us (20%)
  blocking collectives  11.2 us (7%)
  local copies, waits for them, and re-layouts  5.46 us (3%)
    pallas_call x1, Pallas kernels, contract_blocks(): pl.pallas_call(functools.partial(main_kernel, slice_rows, len(pieces), sc...  33.5 us
    ppermute x9, starting transfers between devices, ring_pieces(): lax.ppermute(value, 'blk', [(i, (i // ring + dx) % 2 * ring + (i % ring +...  32.8 us
    all_to_all x1, starting transfers between devices, on_device(): arrived = lax.all_to_all(sent, 'sub', 0, 0, tiled=True)  20.2 us
    all_to_all x1, waiting for transfers between devices, on_device(): arrived = lax.all_to_all(sent, 'sub', 0, 0, tiled=True)  16.6 us
    ppermute x9, waiting for transfers between devices, ring_pieces(): lax.ppermute(value, 'blk', [(i, (i // ring + dx) % 2 * ring + (i % ring +...  14.2 us
    all_to_all x1, blocking collectives, on_device(): mine = jnp.sum(lax.all_to_all(share, 'blk', 0, 0, tiled=True), axis=0)  11.2 us
    ppermute x1, starting transfers between devices, on_device(): lax.ppermute(left, 'sub', [(i + 1, i) for i in range(sub_count - 1)])  8.08 us
    pallas_call x1, Pallas kernels, take_rim(): pl.pallas_call(functools.partial(rim_kernel, slice_rows, len(pieces)), ou...  6.98 us
  transfers between devices with their start and end apart: 12, of which 9 were waited for; matrix products, arithmetic and copies ran while one was open for 0% of the time, Pallas kernels for 0%

profile of v3, /device:TPU:1, one launch (start us, length us, event | category | flops | bytes accessed | tf_op | source)
XLA Modules:
  0.0 159.4 jit_solution(1644111856408988788)
XLA Ops:
  0.0 0.0 copy-start.1
  0.0 0.9 copy-done.1
  0.9 0.1 pack.1
  1.0 3.9 %collective-permute-start = (bf16[512,128]{1,0:T(8,128)(2,1)S(1)}, bf16[512,128]{1,0:T(8,128)(2,1)S(1)}, u32[]{:S(2)}, u32[]{:S(2)}) collective-permute-start(bf16[512,128]{1,0:T(8,128)(2,1)S(1)} %pack.1), channel_id=1, source_target_pairs={{0,8},{1,9},{2,10},{3,11},{4,12},{5,13},{6,14},{7,15},{8,0},{9,1},... | collective-permute-start | bytes 393224 | tf_op jit(solution)/shard_map/gather_modes/ppermute | solution.py:304
  5.0 0.0 copy-start.2
  5.0 0.8 copy-done.2
  5.8 0.0 copy-start.3
  5.8 0.7 copy-done.3
  6.5 0.4 index_words.1
  6.9 0.4 collective-permute-done
  7.3 5.9 %collective-permute-start.2 = (bf16[1024,128]{1,0:T(8,128)(2,1)S(1)}, bf16[1024,128]{1,0:T(8,128)(2,1)S(1)}, u32[]{:S(2)}, u32[]{:S(2)}) collective-permute-start(bf16[1024,128]{1,0:T(8,128)(2,1)S(1)} %pad_maximum_fusion.refs_0_), channel_id=1, source_target_pairs={{0,7},{1,0},{2,1},{3,2},{4,3},{5,4},{6,5},{7,6},{8,15},{9,8},{10,9... | collective-permute-start | bytes 786440 | tf_op jit(solution)/shard_map/gather_modes/ppermute | solution.py:304
  13.2 1.9 %collective-permute-start.1 = (bf16[1024,128]{1,0:T(8,128)(2,1)S(1)}, bf16[1024,128]{1,0:T(8,128)(2,1)S(1)}, u32[]{:S(2)}, u32[]{:S(2)}) collective-permute-start(bf16[1024,128]{1,0:T(8,128)(2,1)S(1)} %pad_maximum_fusion.refs_0_), channel_id=1, source_target_pairs={{0,1},{1,2},{2,3},{3,4},{4,5},{5,6},{6,7},{7,0},{8,9},{9,10},{10,1... | collective-permute-start | bytes 786440 | tf_op jit(solution)/shard_map/gather_modes/ppermute | solution.py:304
  15.2 1.4 collective-permute-done.2.refs_2_
  16.5 5.0 %collective-permute-start.4 = (bf16[1024,128]{1,0:T(8,128)(2,1)S(1)}, bf16[1024,128]{1,0:T(8,128)(2,1)S(1)}, u32[]{:S(2)}, u32[]{:S(2)}) collective-permute-start(bf16[1024,128]{1,0:T(8,128)(2,1)S(1)} %collective-permute-done.2.refs_2_), channel_id=1, source_target_pairs={{0,7},{1,0},{2,1},{3,2},{4,3},{5,4},{6,5},{7,6},{8,15},{9,8},{10,9... | collective-permute-start | bytes 786440 | tf_op jit(solution)/shard_map/gather_modes/ppermute | solution.py:304
  21.5 0.0 collective-permute-done.1.refs_1_
  21.6 1.9 %collective-permute-start.3 = (bf16[1024,128]{1,0:T(8,128)(2,1)S(1)}, bf16[1024,128]{1,0:T(8,128)(2,1)S(1)}, u32[]{:S(2)}, u32[]{:S(2)}) collective-permute-start(bf16[1024,128]{1,0:T(8,128)(2,1)S(1)} %collective-permute-done.1.refs_1_), channel_id=1, source_target_pairs={{0,1},{1,2},{2,3},{3,4},{4,5},{5,6},{6,7},{7,0},{8,9},{9,10},{10,1... | collective-permute-start | bytes 786440 | tf_op jit(solution)/shard_map/gather_modes/ppermute | solution.py:304
  23.5 3.1 %collective-permute-done.4.refs_4_ = bf16[1024,128]{1,0:T(8,128)(2,1)S(1)} collective-permute-done((bf16[1024,128]{1,0:T(8,128)(2,1)S(1)}, bf16[1024,128]{1,0:T(8,128)(2,1)S(1)}, u32[]{:S(2)}, u32[]{:S(2)}) %collective-permute-start.4) | collective-permute-done | bytes 262176 | tf_op jit(solution)/shard_map/gather_modes/ppermute | solution.py:304
  26.6 5.0 %collective-permute-start.6 = (bf16[1024,128]{1,0:T(8,128)(2,1)S(1)}, bf16[1024,128]{1,0:T(8,128)(2,1)S(1)}, u32[]{:S(2)}, u32[]{:S(2)}) collective-permute-start(bf16[1024,128]{1,0:T(8,128)(2,1)S(1)} %collective-permute-done.4.refs_4_), channel_id=1, source_target_pairs={{0,7},{1,0},{2,1},{3,2},{4,3},{5,4},{6,5},{7,6},{8,15},{9,8},{10,9... | collective-permute-start | bytes 786440 | tf_op jit(solution)/shard_map/gather_modes/ppermute | solution.py:304
  31.6 0.3 collective-permute-done.3.refs_3_
  31.9 1.9 %collective-permute-start.5 = (bf16[1024,128]{1,0:T(8,128)(2,1)S(1)}, bf16[1024,128]{1,0:T(8,128)(2,1)S(1)}, u32[]{:S(2)}, u32[]{:S(2)}) collective-permute-start(bf16[1024,128]{1,0:T(8,128)(2,1)S(1)} %collective-permute-done.3.refs_3_), channel_id=1, source_target_pairs={{0,1},{1,2},{2,3},{3,4},{4,5},{5,6},{6,7},{7,0},{8,9},{9,10},{10,1... | collective-permute-start | bytes 786440 | tf_op jit(solution)/shard_map/gather_modes/ppermute | solution.py:304
  34.0 0.1 stack.67
  34.1 3.5 %collective-permute-done.6.refs_6_ = bf16[1024,128]{1,0:T(8,128)(2,1)S(1)} collective-permute-done((bf16[1024,128]{1,0:T(8,128)(2,1)S(1)}, bf16[1024,128]{1,0:T(8,128)(2,1)S(1)}, u32[]{:S(2)}, u32[]{:S(2)}) %collective-permute-start.6) | collective-permute-done | bytes 262176 | tf_op jit(solution)/shard_map/gather_modes/ppermute | solution.py:304
  37.6 5.3 %collective-permute-start.8 = (bf16[512,128]{1,0:T(8,128)(2,1)S(1)}, bf16[512,128]{1,0:T(8,128)(2,1)S(1)}, u32[]{:S(2)}, u32[]{:S(2)}) collective-permute-start(bf16[512,128]{1,0:T(8,128)(2,1)S(1)} %slice.9), channel_id=1, source_target_pairs={{0,7},{1,0},{2,1},{3,2},{4,3},{5,4},{6,5},{7,6},{8,15},{9,8},{10,9... | collective-permute-start | bytes 393224 | tf_op jit(solution)/shard_map/gather_modes/ppermute | solution.py:304
  43.0 0.0 collective-permute-done.5.refs_5_
  43.0 1.9 %collective-permute-start.7 = (bf16[512,128]{1,0:T(8,128)(2,1)S(1)}, bf16[512,128]{1,0:T(8,128)(2,1)S(1)}, u32[]{:S(2)}, u32[]{:S(2)}) collective-permute-start(bf16[512,128]{1,0:T(8,128)(2,1)S(1)} %slice.8), channel_id=1, source_target_pairs={{0,1},{1,2},{2,3},{3,4},{4,5},{5,6},{6,7},{7,0},{8,9},{9,10},{10,1... | collective-permute-start | bytes 393224 | tf_op jit(solution)/shard_map/gather_modes/ppermute | solution.py:304
  45.0 0.4 collective-permute-done.8.refs_8_
  45.3 5.1 %collective-permute-done.7.refs_7_ = bf16[512,128]{1,0:T(8,128)(2,1)S(1)} collective-permute-done((bf16[512,128]{1,0:T(8,128)(2,1)S(1)}, bf16[512,128]{1,0:T(8,128)(2,1)S(1)}, u32[]{:S(2)}, u32[]{:S(2)}) %collective-permute-start.7) | collective-permute-done | bytes 131104 | tf_op jit(solution)/shard_map/gather_modes/ppermute | solution.py:304
  50.4 7.0 %rim.1 = (bf16[1024,128]{1,0:T(8,128)(2,1)S(1)}, bf16[1024,128]{1,0:T(8,128)(2,1)S(1)}) custom-call(s32[16]{0:T(128)S(1)} %broadcast_multiply_fusion.base_ref, s32[16,128]{1,0:T(8,128)S(1)} %get-tuple-element.19.rim_ref, bf16[1024,128]{1,0:T(8,128)(2,1)S(1)} %pad_maximum_fusion.refs_0_, bf16[1024,128]{1,0:T(8,128)(2,1)S(1)} %collective-permute-done.1.refs_1_, ...), custom_call_target="tpu_custom_call" | custom-call | tf_op jit(solution)/shard_map/rim/pallas_call | solution.py:128
  57.4 0.0 copy-start.4
  57.4 6.5 %collective-permute-start.9 = (bf16[1024,128]{1,0:T(8,128)(2,1)S(1)}, bf16[1024,128]{1,0:T(8,128)(2,1)S(1)}, u32[]{:S(2)}, u32[]{:S(2)}) collective-permute-start(bf16[1024,128]{1,0:T(8,128)(2,1)S(1)} %get-tuple-element.23), channel_id=1, source_target_pairs={{0,16},{16,32},{32,48},{48,64},{64,80},{80,96},{96,112},{112,128},... | collective-permute-start | bytes 786440 | tf_op jit(solution)/shard_map/rim/ppermute | solution.py:339
  63.9 8.1 %collective-permute-start.10 = (bf16[1024,128]{1,0:T(8,128)(2,1)S(1)}, bf16[1024,128]{1,0:T(8,128)(2,1)S(1)}, u32[]{:S(2)}, u32[]{:S(2)}) collective-permute-start(bf16[1024,128]{1,0:T(8,128)(2,1)S(1)} %get-tuple-element.24), channel_id=1, source_target_pairs={{16,0},{32,16},{48,32},{64,48},{80,64},{96,80},{112,96},{128,112},... | collective-permute-start | bytes 786440 | tf_op jit(solution)/shard_map/rim/ppermute | solution.py:340
  72.0 0.0 collective-permute-done.9.from_left
  72.0 1.1 collective-permute-done.10.from_right
  73.1 0.0 copy-start
  73.1 2.2 %copy-done = bf16[1,128,128,128]{3,2,1,0:T(8,128)(2,1)S(1)} copy-done((bf16[1,128,128,128]{3,2,1,0:T(8,128)(2,1)S(1)}, bf16[1,128,128,128]{3,2,1,0:T(8,128)(2,1)}, u32[]{:S(2)}) %copy-start) | copy-done | bytes 4194328
  75.3 33.5 %contract.1 = f32[16,4,192]{2,1,0:T(4,128)S(1)} custom-call(s32[16]{0:T(128)S(1)} %broadcast_multiply_fusion.base_ref, s32[16,128]{1,0:T(8,128)S(1)} %get-tuple-element.19.rim_ref, s32[16,128]{1,0:T(8,128)S(1)} %get-tuple-element.20.clash_ref, s32[128,128]{1,0:T(8,128)S(1)} %get-tuple-element.21.dof_ref, bf16[128,128,128]{2,1,0:T(8,128)(2,1)S(1)} %bitcast.21, ...), custom_call_target="tpu_custom_call" | custom-call | tf_op jit(solution)/shard_map/contract/pallas_call | solution.py:258
  108.8 11.2 %all_to_all.10 = f32[16,4,192]{2,1,0:T(4,128)S(1)} all-to-all(f32[16,4,192]{2,1,0:T(4,128)S(1)} %contract.1), channel_id=1, replica_groups=mesh['sub'=48,'blk'=16] {'blk'}, dimensions={0} | all-to-all | bytes 98304 | tf_op jit(solution)/shard_map/sum_over_blk/all_to_all | solution.py:347
  120.0 0.7 broadcast_in_dim.2
  120.7 20.2 %all-to-all-start.1 = ((f32[48,4,192]{2,1,0:T(4,128)}), f32[48,4,192]{2,1,0:T(4,128)S(1)}, u32[]{:S(2)}, u32[]{:S(2)}) async-start(f32[48,4,192]{2,1,0:T(4,128)} %broadcast_in_dim.2), calls=%async_computation.1 | async-start | bytes 393216 | tf_op jit(solution)/shard_map/relay/all_to_all | solution.py:350
  140.9 16.6 %all-to-all-done.1.arrived_ref = f32[48,4,192]{2,1,0:T(4,128)S(1)} async-done(((f32[48,4,192]{2,1,0:T(4,128)}), f32[48,4,192]{2,1,0:T(4,128)S(1)}, u32[]{:S(2)}, u32[]{:S(2)}) %all-to-all-start.1) | async-done | bytes 147488 | tf_op jit(solution)/shard_map/relay/all_to_all | solution.py:350
  157.5 0.0 copy-done.4
  157.5 1.9 %slots.1 = f32[4,4,192]{2,1,0:T(4,128)} custom-call(s32[1]{0:T(128)} %bitcast.me_ref, s32[48]{0:T(128)S(1)} %copy-done.4, f32[48,4,192]{2,1,0:T(4,128)S(1)} %all-to-all-done.1.arrived_ref), custom_call_target="tpu_custom_call" | custom-call | tf_op jit(solution)/shard_map/slots/pallas_call | solution.py:293
  (5 shorter events, 0.1 us)
Async XLA Ops:
  0.0 0.9 copy-start.1
  1.0 6.3 %collective-permute-start = (bf16[512,128]{1,0:T(8,128)(2,1)S(1)}, bf16[512,128]{1,0:T(8,128)(2,1)S(1)}, u32[]{:S(2)}, u32[]{:S(2)}) collective-permute-start(bf16[512,128]{1,0:T(8,128)(2,1)S(1)} %pack.1), channel_id=1, source_target_pairs={{0,8},{1,9},{2,10},{3,11},{4,12},{5,13},{6,14},{7,15},{8,0},{9,1},... | collective-permute-start | bytes 393224 | tf_op jit(solution)/shard_map/gather_modes/ppermute | solution.py:304
  5.0 0.8 copy-start.2
  5.8 0.7 copy-start.3
  7.3 9.2 %collective-permute-start.2 = (bf16[1024,128]{1,0:T(8,128)(2,1)S(1)}, bf16[1024,128]{1,0:T(8,128)(2,1)S(1)}, u32[]{:S(2)}, u32[]{:S(2)}) collective-permute-start(bf16[1024,128]{1,0:T(8,128)(2,1)S(1)} %pad_maximum_fusion.refs_0_), channel_id=1, source_target_pairs={{0,7},{1,0},{2,1},{3,2},{4,3},{5,4},{6,5},{7,6},{8,15},{9,8},{10,9... | collective-permute-start | bytes 786440 | tf_op jit(solution)/shard_map/gather_modes/ppermute | solution.py:304
  13.2 8.3 %collective-permute-start.1 = (bf16[1024,128]{1,0:T(8,128)(2,1)S(1)}, bf16[1024,128]{1,0:T(8,128)(2,1)S(1)}, u32[]{:S(2)}, u32[]{:S(2)}) collective-permute-start(bf16[1024,128]{1,0:T(8,128)(2,1)S(1)} %pad_maximum_fusion.refs_0_), channel_id=1, source_target_pairs={{0,1},{1,2},{2,3},{3,4},{4,5},{5,6},{6,7},{7,0},{8,9},{9,10},{10,1... | collective-permute-start | bytes 786440 | tf_op jit(solution)/shard_map/gather_modes/ppermute | solution.py:304
  16.5 10.1 %collective-permute-start.4 = (bf16[1024,128]{1,0:T(8,128)(2,1)S(1)}, bf16[1024,128]{1,0:T(8,128)(2,1)S(1)}, u32[]{:S(2)}, u32[]{:S(2)}) collective-permute-start(bf16[1024,128]{1,0:T(8,128)(2,1)S(1)} %collective-permute-done.2.refs_2_), channel_id=1, source_target_pairs={{0,7},{1,0},{2,1},{3,2},{4,3},{5,4},{6,5},{7,6},{8,15},{9,8},{10,9... | collective-permute-start | bytes 786440 | tf_op jit(solution)/shard_map/gather_modes/ppermute | solution.py:304
  21.6 10.4 %collective-permute-start.3 = (bf16[1024,128]{1,0:T(8,128)(2,1)S(1)}, bf16[1024,128]{1,0:T(8,128)(2,1)S(1)}, u32[]{:S(2)}, u32[]{:S(2)}) collective-permute-start(bf16[1024,128]{1,0:T(8,128)(2,1)S(1)} %collective-permute-done.1.refs_1_), channel_id=1, source_target_pairs={{0,1},{1,2},{2,3},{3,4},{4,5},{5,6},{6,7},{7,0},{8,9},{9,10},{10,1... | collective-permute-start | bytes 786440 | tf_op jit(solution)/shard_map/gather_modes/ppermute | solution.py:304
  26.6 11.0 %collective-permute-start.6 = (bf16[1024,128]{1,0:T(8,128)(2,1)S(1)}, bf16[1024,128]{1,0:T(8,128)(2,1)S(1)}, u32[]{:S(2)}, u32[]{:S(2)}) collective-permute-start(bf16[1024,128]{1,0:T(8,128)(2,1)S(1)} %collective-permute-done.4.refs_4_), channel_id=1, source_target_pairs={{0,7},{1,0},{2,1},{3,2},{4,3},{5,4},{6,5},{7,6},{8,15},{9,8},{10,9... | collective-permute-start | bytes 786440 | tf_op jit(solution)/shard_map/gather_modes/ppermute | solution.py:304
  31.9 11.1 %collective-permute-start.5 = (bf16[1024,128]{1,0:T(8,128)(2,1)S(1)}, bf16[1024,128]{1,0:T(8,128)(2,1)S(1)}, u32[]{:S(2)}, u32[]{:S(2)}) collective-permute-start(bf16[1024,128]{1,0:T(8,128)(2,1)S(1)} %collective-permute-done.3.refs_3_), channel_id=1, source_target_pairs={{0,1},{1,2},{2,3},{3,4},{4,5},{5,6},{6,7},{7,0},{8,9},{9,10},{10,1... | collective-permute-start | bytes 786440 | tf_op jit(solution)/shard_map/gather_modes/ppermute | solution.py:304
  37.6 7.7 %collective-permute-start.8 = (bf16[512,128]{1,0:T(8,128)(2,1)S(1)}, bf16[512,128]{1,0:T(8,128)(2,1)S(1)}, u32[]{:S(2)}, u32[]{:S(2)}) collective-permute-start(bf16[512,128]{1,0:T(8,128)(2,1)S(1)} %slice.9), channel_id=1, source_target_pairs={{0,7},{1,0},{2,1},{3,2},{4,3},{5,4},{6,5},{7,6},{8,15},{9,8},{10,9... | collective-permute-start | bytes 393224 | tf_op jit(solution)/shard_map/gather_modes/ppermute | solution.py:304
  43.0 7.4 %collective-permute-start.7 = (bf16[512,128]{1,0:T(8,128)(2,1)S(1)}, bf16[512,128]{1,0:T(8,128)(2,1)S(1)}, u32[]{:S(2)}, u32[]{:S(2)}) collective-permute-start(bf16[512,128]{1,0:T(8,128)(2,1)S(1)} %slice.8), channel_id=1, source_target_pairs={{0,1},{1,2},{2,3},{3,4},{4,5},{5,6},{6,7},{7,0},{8,9},{9,10},{10,1... | collective-permute-start | bytes 393224 | tf_op jit(solution)/shard_map/gather_modes/ppermute | solution.py:304
  57.4 100.1 %copy-start.4 = (s32[48]{0:T(128)S(1)}, s32[48]{0:T(128)}, u32[]{:S(2)}) copy-start(s32[48]{0:T(128)} %owner_ref.1) | copy-start | bytes 580
  57.4 14.6 %collective-permute-start.9 = (bf16[1024,128]{1,0:T(8,128)(2,1)S(1)}, bf16[1024,128]{1,0:T(8,128)(2,1)S(1)}, u32[]{:S(2)}, u32[]{:S(2)}) collective-permute-start(bf16[1024,128]{1,0:T(8,128)(2,1)S(1)} %get-tuple-element.23), channel_id=1, source_target_pairs={{0,16},{16,32},{32,48},{48,64},{64,80},{80,96},{96,112},{112,128},... | collective-permute-start | bytes 786440 | tf_op jit(solution)/shard_map/rim/ppermute | solution.py:339
  63.9 9.2 %collective-permute-start.10 = (bf16[1024,128]{1,0:T(8,128)(2,1)S(1)}, bf16[1024,128]{1,0:T(8,128)(2,1)S(1)}, u32[]{:S(2)}, u32[]{:S(2)}) collective-permute-start(bf16[1024,128]{1,0:T(8,128)(2,1)S(1)} %get-tuple-element.24), channel_id=1, source_target_pairs={{16,0},{32,16},{48,32},{64,48},{80,64},{96,80},{112,96},{128,112},... | collective-permute-start | bytes 786440 | tf_op jit(solution)/shard_map/rim/ppermute | solution.py:340
  73.1 2.2 %copy-start = (bf16[1,128,128,128]{3,2,1,0:T(8,128)(2,1)S(1)}, bf16[1,128,128,128]{3,2,1,0:T(8,128)(2,1)}, u32[]{:S(2)}) copy-start(bf16[1,128,128,128]{3,2,1,0:T(8,128)(2,1)} %param.5) | copy-start | bytes 12582916
  120.7 36.8 %all-to-all-start.1 = ((f32[48,4,192]{2,1,0:T(4,128)}), f32[48,4,192]{2,1,0:T(4,128)S(1)}, u32[]{:S(2)}, u32[]{:S(2)}) async-start(f32[48,4,192]{2,1,0:T(4,128)} %broadcast_in_dim.2), calls=%async_computation.1 | async-start | bytes 393216 | tf_op jit(solution)/shard_map/relay/all_to_all | solution.py:350

commit v4 on v3

--- a/solution.py
+++ b/solution.py
@@ -155,11 +155,13 @@
 
 
 def main_kernel(
-    slice_rows, n_pieces, scale, base_ref, rim_ref, clash_ref, dof_ref, stiff_ref, from_left, from_right, *refs
+    slice_rows, n_pieces, scale, base_ref, rim_ref, clash_ref, dof_ref, stiff_hbm, from_left, from_right, *refs
 ):
     pieces = refs[:n_pieces]
     out_ref = refs[n_pieces]
-    table, rim_a, rim_b, got, acc, acc_low = refs[n_pieces + 1:]
+    table, rim_a, rim_b, got, acc, acc_low, stiff_ref, arrived = refs[n_pieces + 1:]
+    fetch = pltpu.make_async_copy(stiff_hbm, stiff_ref, arrived)
+    fetch.start()
     unpack_slices(base_ref, pieces, slice_rows, table, True)
     spread_rim(from_left, rim_a, True)
     spread_rim(from_right, rim_b, False)
@@ -209,6 +211,7 @@
 
     lax.fori_loop(0, n_blocks, gather, 0)
 
+    fetch.wait()
     acc[...] = jnp.zeros_like(acc)
     acc_low[...] = jnp.zeros_like(acc_low)
     width = TOGETHER * size
@@ -258,13 +261,14 @@
     return pl.pallas_call(
         functools.partial(main_kernel, slice_rows, len(pieces), scale),
         out_shape=jax.ShapeDtypeStruct((parts, modes // parts, 3 * modes), F32),
-        in_specs=[SMEM, SMEM, SMEM, SMEM, VMEM, VMEM, VMEM] + [VMEM] * len(pieces),
+        in_specs=[SMEM] * 4 + [pl.BlockSpec(memory_space=pltpu.HBM)] + [VMEM] * (2 + len(pieces)),
         out_specs=VMEM,
         scratch_shapes=[
             wide(2 * total), wide(count), wide(count), wide(2 * n_blocks * size),
             pltpu.VMEM((2 * modes, 2 * LANES), F32), pltpu.VMEM((modes, LANES), F32),
+            pltpu.VMEM(stiffness.shape, BF16), pltpu.SemaphoreType.DMA,
         ],
-        compiler_params=pltpu.CompilerParams(vmem_limit_bytes=44 * 2**20),
+        compiler_params=pltpu.CompilerParams(vmem_limit_bytes=50 * 2**20),
     )(bases, rim, clash, dofs, stiffness, from_left, from_right, *pieces)
 
 
@@ -307,7 +311,6 @@
     )
     x, y = index // ring, index % ring
     base = lambda flip, dy: ((jnp.remainder(x + flip, 2)) * ring + jnp.remainder(y + dy, ring))
-    rows = packed.shape[0]
     both = jnp.concatenate([packed, move(packed, 1, 0)], axis=0)
     both, beside = lax.optimization_barrier((both, beside))
     pieces, places = [both], [base(0, 0), base(1, 0)]
@@ -316,8 +319,8 @@
         up, down = move(up, 0, 1), move(down, 0, -1)
         pieces += [up, down]
         places += [base(0, -k), base(1, -k), base(0, k), base(1, k)]
-    pieces += [move(up[:rows], 0, 1), move(down[rows:], 0, -1)]
-    places += [base(0, ring // 2), base(1, ring // 2)]
+    pieces.append(move(up, 0, 1))
+    places += [base(0, -(ring // 2)), base(1, -(ring // 2))]
     return pieces, jnp.stack(places).astype(jnp.int32), beside
 
 

time: 160 us -> 156 us (0.975)
  starting transfers between devices: 67.6 us -> 63.9 us
  blocking collectives: 11.2 us -> 13.4 us
  local copies, waits for them, and re-layouts: 5.46 us -> 3.26 us
    ppermute x9 -> x8, starting transfers between devices: 32.8 us -> 26.6 us  [ring_pieces(): lax.ppermute(value, 'blk', [(i, (i // ring + dx) % 2 * ring + (i % ring +...]
    ppermute x1, starting transfers between devices: 6.49 us -> 10.5 us  [on_device(): lax.ppermute(right, 'sub', [(i, i + 1) for i in range(sub_count - 1)])]
    all_to_all x1, blocking collectives: 11.2 us -> 13.4 us  [on_device(): mine = jnp.sum(lax.all_to_all(share, 'blk', 0, 0, tiled=True), axis=0)]
    unnamed x10 -> x8, local copies, waits for them, and re-layouts: 4.65 us -> 2.46 us
    ppermute x9 -> x8, waiting for transfers between devices: 14.2 us -> 13 us  [ring_pieces(): lax.ppermute(value, 'blk', [(i, (i // ring + dx) % 2 * ring + (i % ring +...]
  transfers between devices with their start and end apart: 12 -> 11, of which waited for: 9 -> 7; matrix products, arithmetic and copies ran while one was open for 0% -> 0% of each run, Pallas kernels for 0% -> 0%
where the time goes in v4:
time: 156 us; the launch traced here: 155 us
  starting transfers between devices  63.9 us (41%)
  Pallas kernels  42.3 us (27%)
  waiting for transfers between devices  32 us (21%)
  blocking collectives  13.4 us (9%)
  local copies, waits for them, and re-layouts  3.26 us (2%)
    pallas_call x1, Pallas kernels, contract_blocks(): pl.pallas_call(functools.partial(main_kernel, slice_rows, len(pieces), sc...  33 us
    ppermute x8, starting transfers between devices, ring_pieces(): lax.ppermute(value, 'blk', [(i, (i // ring + dx) % 2 * ring + (i % ring +...  26.6 us
    all_to_all x1, starting transfers between devices, on_device(): arrived = lax.all_to_all(sent, 'sub', 0, 0, tiled=True)  19.9 us
    all_to_all x1, waiting for transfers between devices, on_device(): arrived = lax.all_to_all(sent, 'sub', 0, 0, tiled=True)  16.6 us
    all_to_all x1, blocking collectives, on_device(): mine = jnp.sum(lax.all_to_all(share, 'blk', 0, 0, tiled=True), axis=0)  13.4 us
    ppermute x8, waiting for transfers between devices, ring_pieces(): lax.ppermute(value, 'blk', [(i, (i // ring + dx) % 2 * ring + (i % ring +...  13 us
    ppermute x1, starting transfers between devices, on_device(): lax.ppermute(right, 'sub', [(i, i + 1) for i in range(sub_count - 1)])  10.5 us
    pallas_call x1, Pallas kernels, take_rim(): pl.pallas_call(functools.partial(rim_kernel, slice_rows, len(pieces)), ou...  6.98 us
  transfers between devices with their start and end apart: 11, of which 7 were waited for; matrix products, arithmetic and copies ran while one was open for 0% of the time, Pallas kernels for 0%

profile of v4, /device:TPU:1, one launch (start us, length us, event | category | flops | bytes accessed | tf_op | source)
XLA Modules:
  0.0 155.3 jit_solution(8202083900903068702)
XLA Ops:
  0.0 0.0 copy-start
  0.0 0.9 copy-done
  0.9 0.1 pack.1
  1.0 3.9 %collective-permute-start = (bf16[512,128]{1,0:T(8,128)(2,1)S(1)}, bf16[512,128]{1,0:T(8,128)(2,1)S(1)}, u32[]{:S(2)}, u32[]{:S(2)}) collective-permute-start(bf16[512,128]{1,0:T(8,128)(2,1)S(1)} %pack.1), channel_id=1, source_target_pairs={{0,8},{1,9},{2,10},{3,11},{4,12},{5,13},{6,14},{7,15},{8,0},{9,1},... | collective-permute-start | bytes 393224 | tf_op jit(solution)/shard_map/gather_modes/ppermute | solution.py:308
  5.0 0.0 copy-start.1
  5.0 0.8 copy-done.1
  5.8 0.0 copy-start.2
  5.8 0.7 copy-done.2
  6.5 0.4 index_words.1
  6.9 0.4 collective-permute-done
  7.3 4.0 %collective-permute-start.1 = (bf16[1024,128]{1,0:T(8,128)(2,1)S(1)}, bf16[1024,128]{1,0:T(8,128)(2,1)S(1)}, u32[]{:S(2)}, u32[]{:S(2)}) collective-permute-start(bf16[1024,128]{1,0:T(8,128)(2,1)S(1)} %pad_maximum_fusion.refs_0_), channel_id=1, source_target_pairs={{0,1},{1,2},{2,3},{3,4},{4,5},{5,6},{6,7},{7,0},{8,9},{9,10},{10,1... | collective-permute-start | bytes 786440 | tf_op jit(solution)/shard_map/gather_modes/ppermute | solution.py:308
  11.3 3.8 %collective-permute-start.2 = (bf16[1024,128]{1,0:T(8,128)(2,1)S(1)}, bf16[1024,128]{1,0:T(8,128)(2,1)S(1)}, u32[]{:S(2)}, u32[]{:S(2)}) collective-permute-start(bf16[1024,128]{1,0:T(8,128)(2,1)S(1)} %pad_maximum_fusion.refs_0_), channel_id=1, source_target_pairs={{0,7},{1,0},{2,1},{3,2},{4,3},{5,4},{6,5},{7,6},{8,15},{9,8},{10,9... | collective-permute-start | bytes 786440 | tf_op jit(solution)/shard_map/gather_modes/ppermute | solution.py:308
  15.2 1.8 %collective-permute-done.1.refs_1_ = bf16[1024,128]{1,0:T(8,128)(2,1)S(1)} collective-permute-done((bf16[1024,128]{1,0:T(8,128)(2,1)S(1)}, bf16[1024,128]{1,0:T(8,128)(2,1)S(1)}, u32[]{:S(2)}, u32[]{:S(2)}) %collective-permute-start.1) | collective-permute-done | bytes 262176 | tf_op jit(solution)/shard_map/gather_modes/ppermute | solution.py:308
  17.0 1.9 %collective-permute-start.3 = (bf16[1024,128]{1,0:T(8,128)(2,1)S(1)}, bf16[1024,128]{1,0:T(8,128)(2,1)S(1)}, u32[]{:S(2)}, u32[]{:S(2)}) collective-permute-start(bf16[1024,128]{1,0:T(8,128)(2,1)S(1)} %collective-permute-done.1.refs_1_), channel_id=1, source_target_pairs={{0,1},{1,2},{2,3},{3,4},{4,5},{5,6},{6,7},{7,0},{8,9},{9,10},{10,1... | collective-permute-start | bytes 786440 | tf_op jit(solution)/shard_map/gather_modes/ppermute | solution.py:308
  18.9 0.0 collective-permute-done.2.refs_2_
  18.9 4.6 %collective-permute-start.4 = (bf16[1024,128]{1,0:T(8,128)(2,1)S(1)}, bf16[1024,128]{1,0:T(8,128)(2,1)S(1)}, u32[]{:S(2)}, u32[]{:S(2)}) collective-permute-start(bf16[1024,128]{1,0:T(8,128)(2,1)S(1)} %collective-permute-done.2.refs_2_), channel_id=1, source_target_pairs={{0,7},{1,0},{2,1},{3,2},{4,3},{5,4},{6,5},{7,6},{8,15},{9,8},{10,9... | collective-permute-start | bytes 786440 | tf_op jit(solution)/shard_map/gather_modes/ppermute | solution.py:308
  23.5 2.9 %collective-permute-done.3.refs_3_ = bf16[1024,128]{1,0:T(8,128)(2,1)S(1)} collective-permute-done((bf16[1024,128]{1,0:T(8,128)(2,1)S(1)}, bf16[1024,128]{1,0:T(8,128)(2,1)S(1)}, u32[]{:S(2)}, u32[]{:S(2)}) %collective-permute-start.3) | collective-permute-done | bytes 262176 | tf_op jit(solution)/shard_map/gather_modes/ppermute | solution.py:308
  26.4 1.9 %collective-permute-start.5 = (bf16[1024,128]{1,0:T(8,128)(2,1)S(1)}, bf16[1024,128]{1,0:T(8,128)(2,1)S(1)}, u32[]{:S(2)}, u32[]{:S(2)}) collective-permute-start(bf16[1024,128]{1,0:T(8,128)(2,1)S(1)} %collective-permute-done.3.refs_3_), channel_id=1, source_target_pairs={{0,1},{1,2},{2,3},{3,4},{4,5},{5,6},{6,7},{7,0},{8,9},{9,10},{10,1... | collective-permute-start | bytes 786440 | tf_op jit(solution)/shard_map/gather_modes/ppermute | solution.py:308
  28.3 0.0 collective-permute-done.4.refs_4_
  28.3 4.6 %collective-permute-start.6 = (bf16[1024,128]{1,0:T(8,128)(2,1)S(1)}, bf16[1024,128]{1,0:T(8,128)(2,1)S(1)}, u32[]{:S(2)}, u32[]{:S(2)}) collective-permute-start(bf16[1024,128]{1,0:T(8,128)(2,1)S(1)} %collective-permute-done.4.refs_4_), channel_id=1, source_target_pairs={{0,7},{1,0},{2,1},{3,2},{4,3},{5,4},{6,5},{7,6},{8,15},{9,8},{10,9... | collective-permute-start | bytes 786440 | tf_op jit(solution)/shard_map/gather_modes/ppermute | solution.py:308
  32.9 1.8 %collective-permute-done.5.refs_5_ = bf16[1024,128]{1,0:T(8,128)(2,1)S(1)} collective-permute-done((bf16[1024,128]{1,0:T(8,128)(2,1)S(1)}, bf16[1024,128]{1,0:T(8,128)(2,1)S(1)}, u32[]{:S(2)}, u32[]{:S(2)}) %collective-permute-start.5) | collective-permute-done | bytes 262176 | tf_op jit(solution)/shard_map/gather_modes/ppermute | solution.py:308
  34.7 1.9 %collective-permute-start.7 = (bf16[1024,128]{1,0:T(8,128)(2,1)S(1)}, bf16[1024,128]{1,0:T(8,128)(2,1)S(1)}, u32[]{:S(2)}, u32[]{:S(2)}) collective-permute-start(bf16[1024,128]{1,0:T(8,128)(2,1)S(1)} %collective-permute-done.5.refs_5_), channel_id=1, source_target_pairs={{0,1},{1,2},{2,3},{3,4},{4,5},{5,6},{6,7},{7,0},{8,9},{9,10},{10,1... | collective-permute-start | bytes 786440 | tf_op jit(solution)/shard_map/gather_modes/ppermute | solution.py:308
  36.8 0.1 stack.67
  37.0 0.0 collective-permute-done.6.refs_6_
  37.0 6.1 %collective-permute-done.7.refs_7_ = bf16[1024,128]{1,0:T(8,128)(2,1)S(1)} collective-permute-done((bf16[1024,128]{1,0:T(8,128)(2,1)S(1)}, bf16[1024,128]{1,0:T(8,128)(2,1)S(1)}, u32[]{:S(2)}, u32[]{:S(2)}) %collective-permute-start.7) | collective-permute-done | bytes 262176 | tf_op jit(solution)/shard_map/gather_modes/ppermute | solution.py:308
  43.0 7.0 %rim.1 = (bf16[1024,128]{1,0:T(8,128)(2,1)S(1)}, bf16[1024,128]{1,0:T(8,128)(2,1)S(1)}) custom-call(s32[16]{0:T(128)S(1)} %broadcast_multiply_fusion.base_ref, s32[16,128]{1,0:T(8,128)S(1)} %get-tuple-element.19.rim_ref, bf16[1024,128]{1,0:T(8,128)(2,1)S(1)} %pad_maximum_fusion.refs_0_, bf16[1024,128]{1,0:T(8,128)(2,1)S(1)} %collective-permute-done.1.refs_1_, ...), custom_call_target="tpu_custom_call" | custom-call | tf_op jit(solution)/shard_map/rim/pallas_call | solution.py:128
  50.0 0.0 copy-start.3
  50.0 10.5 %collective-permute-start.8 = (bf16[1024,128]{1,0:T(8,128)(2,1)S(1)}, bf16[1024,128]{1,0:T(8,128)(2,1)S(1)}, u32[]{:S(2)}, u32[]{:S(2)}) collective-permute-start(bf16[1024,128]{1,0:T(8,128)(2,1)S(1)} %get-tuple-element.23), channel_id=1, source_target_pairs={{0,16},{16,32},{32,48},{48,64},{64,80},{80,96},{96,112},{112,128},... | collective-permute-start | bytes 786440 | tf_op jit(solution)/shard_map/rim/ppermute | solution.py:342
  60.6 6.8 %collective-permute-start.9 = (bf16[1024,128]{1,0:T(8,128)(2,1)S(1)}, bf16[1024,128]{1,0:T(8,128)(2,1)S(1)}, u32[]{:S(2)}, u32[]{:S(2)}) collective-permute-start(bf16[1024,128]{1,0:T(8,128)(2,1)S(1)} %get-tuple-element.24), channel_id=1, source_target_pairs={{16,0},{32,16},{48,32},{64,48},{80,64},{96,80},{112,96},{128,112},... | collective-permute-start | bytes 786440 | tf_op jit(solution)/shard_map/rim/ppermute | solution.py:343
  67.4 0.0 collective-permute-done.8.from_left
  67.4 2.3 %collective-permute-done.9.from_right = bf16[1024,128]{1,0:T(8,128)(2,1)S(1)} collective-permute-done((bf16[1024,128]{1,0:T(8,128)(2,1)S(1)}, bf16[1024,128]{1,0:T(8,128)(2,1)S(1)}, u32[]{:S(2)}, u32[]{:S(2)}) %collective-permute-start.9) | collective-permute-done | bytes 262176 | tf_op jit(solution)/shard_map/rim/ppermute | solution.py:343
  69.8 33.0 %contract.1 = f32[16,4,192]{2,1,0:T(4,128)S(1)} custom-call(s32[16]{0:T(128)S(1)} %broadcast_multiply_fusion.base_ref, s32[16,128]{1,0:T(8,128)S(1)} %get-tuple-element.19.rim_ref, s32[16,128]{1,0:T(8,128)S(1)} %get-tuple-element.20.clash_ref, s32[128,128]{1,0:T(8,128)S(1)} %get-tuple-element.21.dof_ref, bf16[128,128,128]{2,1,0:T(8,128)(2,1)} %bitcast.24, ...), custom_call_target="tpu_custom_call" | custom-call | tf_op jit(solution)/shard_map/contract/pallas_call | solution.py:261
  102.7 13.4 %all_to_all.10 = f32[16,4,192]{2,1,0:T(4,128)S(1)} all-to-all(f32[16,4,192]{2,1,0:T(4,128)S(1)} %contract.1), channel_id=1, replica_groups=mesh['sub'=48,'blk'=16] {'blk'}, dimensions={0} | all-to-all | bytes 98304 | tf_op jit(solution)/shard_map/sum_over_blk/all_to_all | solution.py:350
  116.2 0.7 broadcast_in_dim.2
  116.9 19.9 %all-to-all-start.1 = ((f32[48,4,192]{2,1,0:T(4,128)}), f32[48,4,192]{2,1,0:T(4,128)S(1)}, u32[]{:S(2)}, u32[]{:S(2)}) async-start(f32[48,4,192]{2,1,0:T(4,128)} %broadcast_in_dim.2), calls=%async_computation.1 | async-start | bytes 393216 | tf_op jit(solution)/shard_map/relay/all_to_all | solution.py:353
  136.8 16.6 %all-to-all-done.1.arrived_ref = f32[48,4,192]{2,1,0:T(4,128)S(1)} async-done(((f32[48,4,192]{2,1,0:T(4,128)}), f32[48,4,192]{2,1,0:T(4,128)S(1)}, u32[]{:S(2)}, u32[]{:S(2)}) %all-to-all-start.1) | async-done | bytes 147488 | tf_op jit(solution)/shard_map/relay/all_to_all | solution.py:353
  153.4 0.0 copy-done.3
  153.4 1.9 %slots.1 = f32[4,4,192]{2,1,0:T(4,128)} custom-call(s32[1]{0:T(128)} %bitcast.me_ref, s32[48]{0:T(128)S(1)} %copy-done.3, f32[48,4,192]{2,1,0:T(4,128)S(1)} %all-to-all-done.1.arrived_ref), custom_call_target="tpu_custom_call" | custom-call | tf_op jit(solution)/shard_map/slots/pallas_call | solution.py:297
  (3 shorter events, 0.1 us)
Async XLA Ops:
  0.0 0.9 copy-start
  1.0 6.3 %collective-permute-start = (bf16[512,128]{1,0:T(8,128)(2,1)S(1)}, bf16[512,128]{1,0:T(8,128)(2,1)S(1)}, u32[]{:S(2)}, u32[]{:S(2)}) collective-permute-start(bf16[512,128]{1,0:T(8,128)(2,1)S(1)} %pack.1), channel_id=1, source_target_pairs={{0,8},{1,9},{2,10},{3,11},{4,12},{5,13},{6,14},{7,15},{8,0},{9,1},... | collective-permute-start | bytes 393224 | tf_op jit(solution)/shard_map/gather_modes/ppermute | solution.py:308
  5.0 0.8 copy-start.1
  5.8 0.7 copy-start.2
  7.3 9.6 %collective-permute-start.1 = (bf16[1024,128]{1,0:T(8,128)(2,1)S(1)}, bf16[1024,128]{1,0:T(8,128)(2,1)S(1)}, u32[]{:S(2)}, u32[]{:S(2)}) collective-permute-start(bf16[1024,128]{1,0:T(8,128)(2,1)S(1)} %pad_maximum_fusion.refs_0_), channel_id=1, source_target_pairs={{0,1},{1,2},{2,3},{3,4},{4,5},{5,6},{6,7},{7,0},{8,9},{9,10},{10,1... | collective-permute-start | bytes 786440 | tf_op jit(solution)/shard_map/gather_modes/ppermute | solution.py:308
  11.3 7.6 %collective-permute-start.2 = (bf16[1024,128]{1,0:T(8,128)(2,1)S(1)}, bf16[1024,128]{1,0:T(8,128)(2,1)S(1)}, u32[]{:S(2)}, u32[]{:S(2)}) collective-permute-start(bf16[1024,128]{1,0:T(8,128)(2,1)S(1)} %pad_maximum_fusion.refs_0_), channel_id=1, source_target_pairs={{0,7},{1,0},{2,1},{3,2},{4,3},{5,4},{6,5},{7,6},{8,15},{9,8},{10,9... | collective-permute-start | bytes 786440 | tf_op jit(solution)/shard_map/gather_modes/ppermute | solution.py:308
  17.0 9.4 %collective-permute-start.3 = (bf16[1024,128]{1,0:T(8,128)(2,1)S(1)}, bf16[1024,128]{1,0:T(8,128)(2,1)S(1)}, u32[]{:S(2)}, u32[]{:S(2)}) collective-permute-start(bf16[1024,128]{1,0:T(8,128)(2,1)S(1)} %collective-permute-done.1.refs_1_), channel_id=1, source_target_pairs={{0,1},{1,2},{2,3},{3,4},{4,5},{5,6},{6,7},{7,0},{8,9},{9,10},{10,1... | collective-permute-start | bytes 786440 | tf_op jit(solution)/shard_map/gather_modes/ppermute | solution.py:308
  18.9 9.4 %collective-permute-start.4 = (bf16[1024,128]{1,0:T(8,128)(2,1)S(1)}, bf16[1024,128]{1,0:T(8,128)(2,1)S(1)}, u32[]{:S(2)}, u32[]{:S(2)}) collective-permute-start(bf16[1024,128]{1,0:T(8,128)(2,1)S(1)} %collective-permute-done.2.refs_2_), channel_id=1, source_target_pairs={{0,7},{1,0},{2,1},{3,2},{4,3},{5,4},{6,5},{7,6},{8,15},{9,8},{10,9... | collective-permute-start | bytes 786440 | tf_op jit(solution)/shard_map/gather_modes/ppermute | solution.py:308
  26.4 8.3 %collective-permute-start.5 = (bf16[1024,128]{1,0:T(8,128)(2,1)S(1)}, bf16[1024,128]{1,0:T(8,128)(2,1)S(1)}, u32[]{:S(2)}, u32[]{:S(2)}) collective-permute-start(bf16[1024,128]{1,0:T(8,128)(2,1)S(1)} %collective-permute-done.3.refs_3_), channel_id=1, source_target_pairs={{0,1},{1,2},{2,3},{3,4},{4,5},{5,6},{6,7},{7,0},{8,9},{9,10},{10,1... | collective-permute-start | bytes 786440 | tf_op jit(solution)/shard_map/gather_modes/ppermute | solution.py:308
  28.3 8.6 %collective-permute-start.6 = (bf16[1024,128]{1,0:T(8,128)(2,1)S(1)}, bf16[1024,128]{1,0:T(8,128)(2,1)S(1)}, u32[]{:S(2)}, u32[]{:S(2)}) collective-permute-start(bf16[1024,128]{1,0:T(8,128)(2,1)S(1)} %collective-permute-done.4.refs_4_), channel_id=1, source_target_pairs={{0,7},{1,0},{2,1},{3,2},{4,3},{5,4},{6,5},{7,6},{8,15},{9,8},{10,9... | collective-permute-start | bytes 786440 | tf_op jit(solution)/shard_map/gather_modes/ppermute | solution.py:308
  34.7 8.3 %collective-permute-start.7 = (bf16[1024,128]{1,0:T(8,128)(2,1)S(1)}, bf16[1024,128]{1,0:T(8,128)(2,1)S(1)}, u32[]{:S(2)}, u32[]{:S(2)}) collective-permute-start(bf16[1024,128]{1,0:T(8,128)(2,1)S(1)} %collective-permute-done.5.refs_5_), channel_id=1, source_target_pairs={{0,1},{1,2},{2,3},{3,4},{4,5},{5,6},{6,7},{7,0},{8,9},{9,10},{10,1... | collective-permute-start | bytes 786440 | tf_op jit(solution)/shard_map/gather_modes/ppermute | solution.py:308
  50.0 103.4 %copy-start.3 = (s32[48]{0:T(128)S(1)}, s32[48]{0:T(128)}, u32[]{:S(2)}) copy-start(s32[48]{0:T(128)} %owner_ref.1) | copy-start | bytes 580
  50.0 17.4 %collective-permute-start.8 = (bf16[1024,128]{1,0:T(8,128)(2,1)S(1)}, bf16[1024,128]{1,0:T(8,128)(2,1)S(1)}, u32[]{:S(2)}, u32[]{:S(2)}) collective-permute-start(bf16[1024,128]{1,0:T(8,128)(2,1)S(1)} %get-tuple-element.23), channel_id=1, source_target_pairs={{0,16},{16,32},{32,48},{48,64},{64,80},{80,96},{96,112},{112,128},... | collective-permute-start | bytes 786440 | tf_op jit(solution)/shard_map/rim/ppermute | solution.py:342
  60.6 9.2 %collective-permute-start.9 = (bf16[1024,128]{1,0:T(8,128)(2,1)S(1)}, bf16[1024,128]{1,0:T(8,128)(2,1)S(1)}, u32[]{:S(2)}, u32[]{:S(2)}) collective-permute-start(bf16[1024,128]{1,0:T(8,128)(2,1)S(1)} %get-tuple-element.24), channel_id=1, source_target_pairs={{16,0},{32,16},{48,32},{64,48},{80,64},{96,80},{112,96},{128,112},... | collective-permute-start | bytes 786440 | tf_op jit(solution)/shard_map/rim/ppermute | solution.py:343
  116.9 36.5 %all-to-all-start.1 = ((f32[48,4,192]{2,1,0:T(4,128)}), f32[48,4,192]{2,1,0:T(4,128)S(1)}, u32[]{:S(2)}, u32[]{:S(2)}) async-start(f32[48,4,192]{2,1,0:T(4,128)} %broadcast_in_dim.2), calls=%async_computation.1 | async-start | bytes 393216 | tf_op jit(solution)/shard_map/relay/all_to_all | solution.py:353

commit v5 on v4

--- a/solution.py
+++ b/solution.py
@@ -167,32 +167,44 @@
     spread_rim(from_right, rim_b, False)
     rim_groups, group_rows = rim_ref.shape
 
+    def add_group(g, first, k):
+        new_a, new_b = rim_a.at[pl.ds(first + k, GROUP)], rim_b.at[pl.ds(first + k, GROUP)]
+        words = [rim_ref[g, k + j] for j in range(GROUP)]
+        at = [(word & 0xFFFF, (word >> 16) + 1) for word in words]
+        sums = [
+            (table[pl.ds(a, 1), :] + new_a[pl.ds(j, 1), :], table[pl.ds(b, 1), :] + new_b[pl.ds(j, 1), :])
+            for j, (a, b) in enumerate(at)
+        ]
+        for (a, b), (sum_a, sum_b) in zip(at, sums):
+            table[pl.ds(a, 1), :] = sum_a
+            table[pl.ds(b, 1), :] = sum_b
+
+    def add_one_by_one(g, first, k):
+        def one(j, _):
+            word = rim_ref[g, k + j]
+            table[pl.ds(word & 0xFFFF, 1), :] += rim_a[pl.ds(first + k + j, 1), :]
+            table[pl.ds((word >> 16) + 1, 1), :] += rim_b[pl.ds(first + k + j, 1), :]
+            return 0
+
+        lax.fori_loop(0, GROUP, one, 0)
+
     def add_rows(g, _):
         first = pl.multiple_of(g * group_rows, group_rows)
-        for k in range(0, group_rows, GROUP):
-            new_a, new_b = rim_a.at[pl.ds(first + k, GROUP)], rim_b.at[pl.ds(first + k, GROUP)]
-
-            @pl.when(clash_ref[g, k + GROUP - 1] == 0)
-            def _(k=k, new_a=new_a, new_b=new_b):
-                words = [rim_ref[g, k + j] for j in range(GROUP)]
-                at = [(word & 0xFFFF, (word >> 16) + 1) for word in words]
-                sums = [
-                    (table[pl.ds(a, 1), :] + new_a[pl.ds(j, 1), :], table[pl.ds(b, 1), :] + new_b[pl.ds(j, 1), :])
-                    for j, (a, b) in enumerate(at)
-                ]
-                for (a, b), (sum_a, sum_b) in zip(at, sums):
-                    table[pl.ds(a, 1), :] = sum_a
-                    table[pl.ds(b, 1), :] = sum_b
-
-            @pl.when(clash_ref[g, k + GROUP - 1] != 0)
-            def _(k=k, new_a=new_a, new_b=new_b):
-                def one(j, _):
-                    word = rim_ref[g, k + j]
-                    table[pl.ds(word & 0xFFFF, 1), :] += new_a[pl.ds(j, 1), :]
-                    table[pl.ds((word >> 16) + 1, 1), :] += new_b[pl.ds(j, 1), :]
-                    return 0
-
-                lax.fori_loop(0, GROUP, one, 0)
+        ends = [k + GROUP - 1 for k in range(0, group_rows, GROUP)]
+        worst = clash_ref[g, ends[0]]
+        for end in ends[1:]:
+            worst = worst | clash_ref[g, end]
+
+        @pl.when(worst == 0)
+        def _():
+            for k in range(0, group_rows, GROUP):
+                add_group(g, first, k)
+
+        @pl.when(worst != 0)
+        def _():
+            for k in range(0, group_rows, GROUP):
+                pl.when(clash_ref[g, k + GROUP - 1] == 0)(functools.partial(add_group, g, first, k))
+                pl.when(clash_ref[g, k + GROUP - 1] != 0)(functools.partial(add_one_by_one, g, first, k))
 
         return 0
 
@@ -272,25 +284,40 @@
     )(bases, rim, clash, dofs, stiffness, from_left, from_right, *pieces)
 
 
+def sum_kernel(parts_ref, out_ref):
+    total = parts_ref[0]
+    for i in range(1, parts_ref.shape[0]):
+        total = total + parts_ref[i]
+    for i in range(out_ref.shape[0]):
+        out_ref[i] = total
+
+
+def sum_for_all(parts, receivers):
+    return pl.pallas_call(
+        sum_kernel,
+        out_shape=jax.ShapeDtypeStruct((receivers,) + parts.shape[1:], F32),
+        in_specs=[VMEM],
+        out_specs=VMEM,
+        compiler_params=pltpu.CompilerParams(vmem_limit_bytes=8 * 2**20),
+    )(parts)
+
+
 def slots_kernel(me_ref, owner_ref, arrived_ref, out_ref):
     count = arrived_ref.shape[0]
     shape = arrived_ref.shape[1:]
     part = lax.broadcasted_iota(jnp.int32, shape, 1) // (LANES // 2)
-    out_ref[...] = jnp.zeros_like(out_ref)
-
-    def step(t, slot):
-        mine = owner_ref[t] == me_ref[0]
-
-        @pl.when(mine)
-        def _():
-            before = jnp.where(t > 0, arrived_ref[jnp.maximum(t - 1, 0)], 0.0)
-            after = jnp.where(t < count - 1, arrived_ref[jnp.minimum(t + 1, count - 1)], 0.0)
-            row = jnp.where(part == 0, before, jnp.where(part == 1, arrived_ref[t], after))
-            out_ref[jnp.minimum(slot, CAP - 1)] = row
-
-        return slot + mine.astype(jnp.int32)
-
-    lax.fori_loop(0, count, step, 0)
+    me = me_ref[0]
+    filled = jnp.int32(0)
+    held = [jnp.int32(-1)] * CAP
+    for t in range(count):
+        mine = owner_ref[t] == me
+        held = [jnp.where(mine & (filled == slot), t, old) for slot, old in enumerate(held)]
+        filled = filled + mine.astype(jnp.int32)
+    for slot, t in enumerate(held):
+        before = jnp.where(t > 0, arrived_ref[jnp.maximum(t - 1, 0)], 0.0)
+        after = jnp.where((t >= 0) & (t < count - 1), arrived_ref[jnp.minimum(t + 1, count - 1)], 0.0)
+        own = jnp.where(t >= 0, arrived_ref[jnp.maximum(t, 0)], 0.0)
+        out_ref[slot] = jnp.where(part == 0, before, jnp.where(part == 1, own, after))
 
 
 def fill_slots(me, owner_map, arrived):
@@ -347,9 +374,8 @@
             bases, rim, clash, dofs, stiffness[0], from_left, from_right, pieces, slice_rows, blk_count, scale
         )
     with jax.named_scope("sum_over_blk"):
-        mine = jnp.sum(lax.all_to_all(share, "blk", 0, 0, tiled=True), axis=0)
+        sent = sum_for_all(lax.all_to_all(share, "blk", 0, 0, tiled=True), sub_count)
     with jax.named_scope("relay"):
-        sent = jnp.broadcast_to(mine[None], (sub_count,) + mine.shape)
         arrived = lax.all_to_all(sent, "sub", 0, 0, tiled=True)
     with jax.named_scope("slots"):
         return fill_slots(jnp.reshape(sub, (1,)), owner_map, arrived)

time: 156 us -> 153 us (0.981)
  Pallas kernels: 42.3 us -> 39.8 us
    pallas_call x1, Pallas kernels: 33 us -> 30 us  [contract_blocks(): pl.pallas_call(functools.partial(main_kernel, slice_rows, len(pieces), sc...]
where the time goes in v5:
time: 153 us; the launch traced here: 152 us
  starting transfers between devices  64 us (42%)
  Pallas kernels  39.8 us (26%)
  waiting for transfers between devices  32 us (21%)
  blocking collectives  13.4 us (9%)
  local copies, waits for them, and re-layouts  2.55 us (2%)
    pallas_call x1, Pallas kernels, contract_blocks(): pl.pallas_call(functools.partial(main_kernel, slice_rows, len(pieces), sc...  30 us
    ppermute x8, starting transfers between devices, ring_pieces(): lax.ppermute(value, 'blk', [(i, (i // ring + dx) % 2 * ring + (i % ring +...  26.6 us
    all_to_all x1, starting transfers between devices, on_device(): arrived = lax.all_to_all(sent, 'sub', 0, 0, tiled=True)  20.1 us
    all_to_all x1, waiting for transfers between devices, on_device(): arrived = lax.all_to_all(sent, 'sub', 0, 0, tiled=True)  16.6 us
    all_to_all x1, blocking collectives, on_device(): lax.all_to_all(share, 'blk', 0, 0, tiled=True)  13.4 us
    ppermute x8, waiting for transfers between devices, ring_pieces(): lax.ppermute(value, 'blk', [(i, (i // ring + dx) % 2 * ring + (i % ring +...  13 us
    ppermute x1, starting transfers between devices, on_device(): lax.ppermute(right, 'sub', [(i, i + 1) for i in range(sub_count - 1)])  10.5 us
    pallas_call x1, Pallas kernels, take_rim(): pl.pallas_call(functools.partial(rim_kernel, slice_rows, len(pieces)), ou...  6.98 us
  transfers between devices with their start and end apart: 11, of which 7 were waited for; matrix products, arithmetic and copies ran while one was open for 0% of the time, Pallas kernels for 0%

profile of v5, /device:TPU:1, one launch (start us, length us, event | category | flops | bytes accessed | tf_op | source)
XLA Modules:
  0.0 152.2 jit_solution(9100639570235023133)
XLA Ops:
  0.0 0.0 copy-start
  0.0 0.9 copy-done
  0.9 0.1 pack.1
  1.0 3.9 %collective-permute-start = (bf16[512,128]{1,0:T(8,128)(2,1)S(1)}, bf16[512,128]{1,0:T(8,128)(2,1)S(1)}, u32[]{:S(2)}, u32[]{:S(2)}) collective-permute-start(bf16[512,128]{1,0:T(8,128)(2,1)S(1)} %pack.1), channel_id=1, source_target_pairs={{0,8},{1,9},{2,10},{3,11},{4,12},{5,13},{6,14},{7,15},{8,0},{9,1},... | collective-permute-start | bytes 393224 | tf_op jit(solution)/shard_map/gather_modes/ppermute | solution.py:335
  5.0 0.0 copy-start.1
  5.0 0.8 copy-done.1
  5.8 0.0 copy-start.2
  5.8 0.7 copy-done.2
  6.5 0.4 index_words.1
  6.9 0.4 collective-permute-done
  7.3 4.0 %collective-permute-start.1 = (bf16[1024,128]{1,0:T(8,128)(2,1)S(1)}, bf16[1024,128]{1,0:T(8,128)(2,1)S(1)}, u32[]{:S(2)}, u32[]{:S(2)}) collective-permute-start(bf16[1024,128]{1,0:T(8,128)(2,1)S(1)} %pad_maximum_fusion.refs_0_), channel_id=1, source_target_pairs={{0,1},{1,2},{2,3},{3,4},{4,5},{5,6},{6,7},{7,0},{8,9},{9,10},{10,1... | collective-permute-start | bytes 786440 | tf_op jit(solution)/shard_map/gather_modes/ppermute | solution.py:335
  11.3 3.8 %collective-permute-start.2 = (bf16[1024,128]{1,0:T(8,128)(2,1)S(1)}, bf16[1024,128]{1,0:T(8,128)(2,1)S(1)}, u32[]{:S(2)}, u32[]{:S(2)}) collective-permute-start(bf16[1024,128]{1,0:T(8,128)(2,1)S(1)} %pad_maximum_fusion.refs_0_), channel_id=1, source_target_pairs={{0,7},{1,0},{2,1},{3,2},{4,3},{5,4},{6,5},{7,6},{8,15},{9,8},{10,9... | collective-permute-start | bytes 786440 | tf_op jit(solution)/shard_map/gather_modes/ppermute | solution.py:335
  15.2 1.8 %collective-permute-done.1.refs_1_ = bf16[1024,128]{1,0:T(8,128)(2,1)S(1)} collective-permute-done((bf16[1024,128]{1,0:T(8,128)(2,1)S(1)}, bf16[1024,128]{1,0:T(8,128)(2,1)S(1)}, u32[]{:S(2)}, u32[]{:S(2)}) %collective-permute-start.1) | collective-permute-done | bytes 262176 | tf_op jit(solution)/shard_map/gather_modes/ppermute | solution.py:335
  17.0 1.9 %collective-permute-start.3 = (bf16[1024,128]{1,0:T(8,128)(2,1)S(1)}, bf16[1024,128]{1,0:T(8,128)(2,1)S(1)}, u32[]{:S(2)}, u32[]{:S(2)}) collective-permute-start(bf16[1024,128]{1,0:T(8,128)(2,1)S(1)} %collective-permute-done.1.refs_1_), channel_id=1, source_target_pairs={{0,1},{1,2},{2,3},{3,4},{4,5},{5,6},{6,7},{7,0},{8,9},{9,10},{10,1... | collective-permute-start | bytes 786440 | tf_op jit(solution)/shard_map/gather_modes/ppermute | solution.py:335
  18.9 0.0 collective-permute-done.2.refs_2_
  18.9 4.6 %collective-permute-start.4 = (bf16[1024,128]{1,0:T(8,128)(2,1)S(1)}, bf16[1024,128]{1,0:T(8,128)(2,1)S(1)}, u32[]{:S(2)}, u32[]{:S(2)}) collective-permute-start(bf16[1024,128]{1,0:T(8,128)(2,1)S(1)} %collective-permute-done.2.refs_2_), channel_id=1, source_target_pairs={{0,7},{1,0},{2,1},{3,2},{4,3},{5,4},{6,5},{7,6},{8,15},{9,8},{10,9... | collective-permute-start | bytes 786440 | tf_op jit(solution)/shard_map/gather_modes/ppermute | solution.py:335
  23.5 2.9 %collective-permute-done.3.refs_3_ = bf16[1024,128]{1,0:T(8,128)(2,1)S(1)} collective-permute-done((bf16[1024,128]{1,0:T(8,128)(2,1)S(1)}, bf16[1024,128]{1,0:T(8,128)(2,1)S(1)}, u32[]{:S(2)}, u32[]{:S(2)}) %collective-permute-start.3) | collective-permute-done | bytes 262176 | tf_op jit(solution)/shard_map/gather_modes/ppermute | solution.py:335
  26.4 1.9 %collective-permute-start.5 = (bf16[1024,128]{1,0:T(8,128)(2,1)S(1)}, bf16[1024,128]{1,0:T(8,128)(2,1)S(1)}, u32[]{:S(2)}, u32[]{:S(2)}) collective-permute-start(bf16[1024,128]{1,0:T(8,128)(2,1)S(1)} %collective-permute-done.3.refs_3_), channel_id=1, source_target_pairs={{0,1},{1,2},{2,3},{3,4},{4,5},{5,6},{6,7},{7,0},{8,9},{9,10},{10,1... | collective-permute-start | bytes 786440 | tf_op jit(solution)/shard_map/gather_modes/ppermute | solution.py:335
  28.3 0.0 collective-permute-done.4.refs_4_
  28.3 4.6 %collective-permute-start.6 = (bf16[1024,128]{1,0:T(8,128)(2,1)S(1)}, bf16[1024,128]{1,0:T(8,128)(2,1)S(1)}, u32[]{:S(2)}, u32[]{:S(2)}) collective-permute-start(bf16[1024,128]{1,0:T(8,128)(2,1)S(1)} %collective-permute-done.4.refs_4_), channel_id=1, source_target_pairs={{0,7},{1,0},{2,1},{3,2},{4,3},{5,4},{6,5},{7,6},{8,15},{9,8},{10,9... | collective-permute-start | bytes 786440 | tf_op jit(solution)/shard_map/gather_modes/ppermute | solution.py:335
  32.9 1.8 %collective-permute-done.5.refs_5_ = bf16[1024,128]{1,0:T(8,128)(2,1)S(1)} collective-permute-done((bf16[1024,128]{1,0:T(8,128)(2,1)S(1)}, bf16[1024,128]{1,0:T(8,128)(2,1)S(1)}, u32[]{:S(2)}, u32[]{:S(2)}) %collective-permute-start.5) | collective-permute-done | bytes 262176 | tf_op jit(solution)/shard_map/gather_modes/ppermute | solution.py:335
  34.7 1.9 %collective-permute-start.7 = (bf16[1024,128]{1,0:T(8,128)(2,1)S(1)}, bf16[1024,128]{1,0:T(8,128)(2,1)S(1)}, u32[]{:S(2)}, u32[]{:S(2)}) collective-permute-start(bf16[1024,128]{1,0:T(8,128)(2,1)S(1)} %collective-permute-done.5.refs_5_), channel_id=1, source_target_pairs={{0,1},{1,2},{2,3},{3,4},{4,5},{5,6},{6,7},{7,0},{8,9},{9,10},{10,1... | collective-permute-start | bytes 786440 | tf_op jit(solution)/shard_map/gather_modes/ppermute | solution.py:335
  36.8 0.1 stack.67
  37.0 0.0 collective-permute-done.6.refs_6_
  37.0 6.1 %collective-permute-done.7.refs_7_ = bf16[1024,128]{1,0:T(8,128)(2,1)S(1)} collective-permute-done((bf16[1024,128]{1,0:T(8,128)(2,1)S(1)}, bf16[1024,128]{1,0:T(8,128)(2,1)S(1)}, u32[]{:S(2)}, u32[]{:S(2)}) %collective-permute-start.7) | collective-permute-done | bytes 262176 | tf_op jit(solution)/shard_map/gather_modes/ppermute | solution.py:335
  43.0 7.0 %rim.1 = (bf16[1024,128]{1,0:T(8,128)(2,1)S(1)}, bf16[1024,128]{1,0:T(8,128)(2,1)S(1)}) custom-call(s32[16]{0:T(128)S(1)} %broadcast_multiply_fusion.base_ref, s32[16,128]{1,0:T(8,128)S(1)} %get-tuple-element.19.rim_ref, bf16[1024,128]{1,0:T(8,128)(2,1)S(1)} %pad_maximum_fusion.refs_0_, bf16[1024,128]{1,0:T(8,128)(2,1)S(1)} %collective-permute-done.1.refs_1_, ...), custom_call_target="tpu_custom_call" | custom-call | tf_op jit(solution)/shard_map/rim/pallas_call | solution.py:128
  50.0 0.0 copy-start.3
  50.0 10.5 %collective-permute-start.8 = (bf16[1024,128]{1,0:T(8,128)(2,1)S(1)}, bf16[1024,128]{1,0:T(8,128)(2,1)S(1)}, u32[]{:S(2)}, u32[]{:S(2)}) collective-permute-start(bf16[1024,128]{1,0:T(8,128)(2,1)S(1)} %get-tuple-element.23), channel_id=1, source_target_pairs={{0,16},{16,32},{32,48},{48,64},{64,80},{80,96},{96,112},{112,128},... | collective-permute-start | bytes 786440 | tf_op jit(solution)/shard_map/rim/ppermute | solution.py:369
  60.6 6.8 %collective-permute-start.9 = (bf16[1024,128]{1,0:T(8,128)(2,1)S(1)}, bf16[1024,128]{1,0:T(8,128)(2,1)S(1)}, u32[]{:S(2)}, u32[]{:S(2)}) collective-permute-start(bf16[1024,128]{1,0:T(8,128)(2,1)S(1)} %get-tuple-element.24), channel_id=1, source_target_pairs={{16,0},{32,16},{48,32},{64,48},{80,64},{96,80},{112,96},{128,112},... | collective-permute-start | bytes 786440 | tf_op jit(solution)/shard_map/rim/ppermute | solution.py:370
  67.4 0.0 collective-permute-done.8.from_left
  67.4 2.3 %collective-permute-done.9.from_right = bf16[1024,128]{1,0:T(8,128)(2,1)S(1)} collective-permute-done((bf16[1024,128]{1,0:T(8,128)(2,1)S(1)}, bf16[1024,128]{1,0:T(8,128)(2,1)S(1)}, u32[]{:S(2)}, u32[]{:S(2)}) %collective-permute-start.9) | collective-permute-done | bytes 262176 | tf_op jit(solution)/shard_map/rim/ppermute | solution.py:370
  69.8 30.0 %contract.1 = f32[16,4,192]{2,1,0:T(4,128)S(1)} custom-call(s32[16]{0:T(128)S(1)} %broadcast_multiply_fusion.base_ref, s32[16,128]{1,0:T(8,128)S(1)} %get-tuple-element.19.rim_ref, s32[16,128]{1,0:T(8,128)S(1)} %get-tuple-element.20.clash_ref, s32[128,128]{1,0:T(8,128)S(1)} %get-tuple-element.21.dof_ref, bf16[128,128,128]{2,1,0:T(8,128)(2,1)} %bitcast.24, ...), custom_call_target="tpu_custom_call" | custom-call | tf_op jit(solution)/shard_map/contract/pallas_call | solution.py:273
  99.8 13.4 %all_to_all.10.parts_ref = f32[16,4,192]{2,1,0:T(4,128)S(1)} all-to-all(f32[16,4,192]{2,1,0:T(4,128)S(1)} %contract.1), channel_id=1, replica_groups=mesh['sub'=48,'blk'=16] {'blk'}, dimensions={0} | all-to-all | bytes 98304 | tf_op jit(solution)/shard_map/sum_over_blk/all_to_all | solution.py:377
  113.2 0.7 sum_over_blk.1
  113.9 20.1 %all-to-all-start.1 = ((f32[48,4,192]{2,1,0:T(4,128)}), f32[48,4,192]{2,1,0:T(4,128)S(1)}, u32[]{:S(2)}, u32[]{:S(2)}) async-start(f32[48,4,192]{2,1,0:T(4,128)} %sum_over_blk.1), calls=%async_computation.1 | async-start | bytes 393216 | tf_op jit(solution)/shard_map/relay/all_to_all | solution.py:379
  134.0 16.6 %all-to-all-done.1.arrived_ref = f32[48,4,192]{2,1,0:T(4,128)S(1)} async-done(((f32[48,4,192]{2,1,0:T(4,128)}), f32[48,4,192]{2,1,0:T(4,128)S(1)}, u32[]{:S(2)}, u32[]{:S(2)}) %all-to-all-start.1) | async-done | bytes 147488 | tf_op jit(solution)/shard_map/relay/all_to_all | solution.py:379
  150.6 0.0 copy-done.3
  150.6 1.6 %slots.1 = f32[4,4,192]{2,1,0:T(4,128)} custom-call(s32[1]{0:T(128)} %bitcast.me_ref, s32[48]{0:T(128)S(1)} %copy-done.3, f32[48,4,192]{2,1,0:T(4,128)S(1)} %all-to-all-done.1.arrived_ref), custom_call_target="tpu_custom_call" | custom-call | tf_op jit(solution)/shard_map/slots/pallas_call | solution.py:324
  (2 shorter events, 0.0 us)
Async XLA Ops:
  0.0 0.9 copy-start
  1.0 6.3 %collective-permute-start = (bf16[512,128]{1,0:T(8,128)(2,1)S(1)}, bf16[512,128]{1,0:T(8,128)(2,1)S(1)}, u32[]{:S(2)}, u32[]{:S(2)}) collective-permute-start(bf16[512,128]{1,0:T(8,128)(2,1)S(1)} %pack.1), channel_id=1, source_target_pairs={{0,8},{1,9},{2,10},{3,11},{4,12},{5,13},{6,14},{7,15},{8,0},{9,1},... | collective-permute-start | bytes 393224 | tf_op jit(solution)/shard_map/gather_modes/ppermute | solution.py:335
  5.0 0.8 copy-start.1
  5.8 0.7 copy-start.2
  7.3 9.6 %collective-permute-start.1 = (bf16[1024,128]{1,0:T(8,128)(2,1)S(1)}, bf16[1024,128]{1,0:T(8,128)(2,1)S(1)}, u32[]{:S(2)}, u32[]{:S(2)}) collective-permute-start(bf16[1024,128]{1,0:T(8,128)(2,1)S(1)} %pad_maximum_fusion.refs_0_), channel_id=1, source_target_pairs={{0,1},{1,2},{2,3},{3,4},{4,5},{5,6},{6,7},{7,0},{8,9},{9,10},{10,1... | collective-permute-start | bytes 786440 | tf_op jit(solution)/shard_map/gather_modes/ppermute | solution.py:335
  11.3 7.6 %collective-permute-start.2 = (bf16[1024,128]{1,0:T(8,128)(2,1)S(1)}, bf16[1024,128]{1,0:T(8,128)(2,1)S(1)}, u32[]{:S(2)}, u32[]{:S(2)}) collective-permute-start(bf16[1024,128]{1,0:T(8,128)(2,1)S(1)} %pad_maximum_fusion.refs_0_), channel_id=1, source_target_pairs={{0,7},{1,0},{2,1},{3,2},{4,3},{5,4},{6,5},{7,6},{8,15},{9,8},{10,9... | collective-permute-start | bytes 786440 | tf_op jit(solution)/shard_map/gather_modes/ppermute | solution.py:335
  17.0 9.4 %collective-permute-start.3 = (bf16[1024,128]{1,0:T(8,128)(2,1)S(1)}, bf16[1024,128]{1,0:T(8,128)(2,1)S(1)}, u32[]{:S(2)}, u32[]{:S(2)}) collective-permute-start(bf16[1024,128]{1,0:T(8,128)(2,1)S(1)} %collective-permute-done.1.refs_1_), channel_id=1, source_target_pairs={{0,1},{1,2},{2,3},{3,4},{4,5},{5,6},{6,7},{7,0},{8,9},{9,10},{10,1... | collective-permute-start | bytes 786440 | tf_op jit(solution)/shard_map/gather_modes/ppermute | solution.py:335
  18.9 9.4 %collective-permute-start.4 = (bf16[1024,128]{1,0:T(8,128)(2,1)S(1)}, bf16[1024,128]{1,0:T(8,128)(2,1)S(1)}, u32[]{:S(2)}, u32[]{:S(2)}) collective-permute-start(bf16[1024,128]{1,0:T(8,128)(2,1)S(1)} %collective-permute-done.2.refs_2_), channel_id=1, source_target_pairs={{0,7},{1,0},{2,1},{3,2},{4,3},{5,4},{6,5},{7,6},{8,15},{9,8},{10,9... | collective-permute-start | bytes 786440 | tf_op jit(solution)/shard_map/gather_modes/ppermute | solution.py:335
  26.4 8.3 %collective-permute-start.5 = (bf16[1024,128]{1,0:T(8,128)(2,1)S(1)}, bf16[1024,128]{1,0:T(8,128)(2,1)S(1)}, u32[]{:S(2)}, u32[]{:S(2)}) collective-permute-start(bf16[1024,128]{1,0:T(8,128)(2,1)S(1)} %collective-permute-done.3.refs_3_), channel_id=1, source_target_pairs={{0,1},{1,2},{2,3},{3,4},{4,5},{5,6},{6,7},{7,0},{8,9},{9,10},{10,1... | collective-permute-start | bytes 786440 | tf_op jit(solution)/shard_map/gather_modes/ppermute | solution.py:335
  28.3 8.6 %collective-permute-start.6 = (bf16[1024,128]{1,0:T(8,128)(2,1)S(1)}, bf16[1024,128]{1,0:T(8,128)(2,1)S(1)}, u32[]{:S(2)}, u32[]{:S(2)}) collective-permute-start(bf16[1024,128]{1,0:T(8,128)(2,1)S(1)} %collective-permute-done.4.refs_4_), channel_id=1, source_target_pairs={{0,7},{1,0},{2,1},{3,2},{4,3},{5,4},{6,5},{7,6},{8,15},{9,8},{10,9... | collective-permute-start | bytes 786440 | tf_op jit(solution)/shard_map/gather_modes/ppermute | solution.py:335
  34.7 8.3 %collective-permute-start.7 = (bf16[1024,128]{1,0:T(8,128)(2,1)S(1)}, bf16[1024,128]{1,0:T(8,128)(2,1)S(1)}, u32[]{:S(2)}, u32[]{:S(2)}) collective-permute-start(bf16[1024,128]{1,0:T(8,128)(2,1)S(1)} %collective-permute-done.5.refs_5_), channel_id=1, source_target_pairs={{0,1},{1,2},{2,3},{3,4},{4,5},{5,6},{6,7},{7,0},{8,9},{9,10},{10,1... | collective-permute-start | bytes 786440 | tf_op jit(solution)/shard_map/gather_modes/ppermute | solution.py:335
  50.0 100.6 %copy-start.3 = (s32[48]{0:T(128)S(1)}, s32[48]{0:T(128)}, u32[]{:S(2)}) copy-start(s32[48]{0:T(128)} %owner_ref.1) | copy-start | bytes 580
  50.0 17.4 %collective-permute-start.8 = (bf16[1024,128]{1,0:T(8,128)(2,1)S(1)}, bf16[1024,128]{1,0:T(8,128)(2,1)S(1)}, u32[]{:S(2)}, u32[]{:S(2)}) collective-permute-start(bf16[1024,128]{1,0:T(8,128)(2,1)S(1)} %get-tuple-element.23), channel_id=1, source_target_pairs={{0,16},{16,32},{32,48},{48,64},{64,80},{80,96},{96,112},{112,128},... | collective-permute-start | bytes 786440 | tf_op jit(solution)/shard_map/rim/ppermute | solution.py:369
  60.6 9.2 %collective-permute-start.9 = (bf16[1024,128]{1,0:T(8,128)(2,1)S(1)}, bf16[1024,128]{1,0:T(8,128)(2,1)S(1)}, u32[]{:S(2)}, u32[]{:S(2)}) collective-permute-start(bf16[1024,128]{1,0:T(8,128)(2,1)S(1)} %get-tuple-element.24), channel_id=1, source_target_pairs={{16,0},{32,16},{48,32},{64,48},{80,64},{96,80},{112,96},{128,112},... | collective-permute-start | bytes 786440 | tf_op jit(solution)/shard_map/rim/ppermute | solution.py:370
  113.9 36.7 %all-to-all-start.1 = ((f32[48,4,192]{2,1,0:T(4,128)}), f32[48,4,192]{2,1,0:T(4,128)S(1)}, u32[]{:S(2)}, u32[]{:S(2)}) async-start(f32[48,4,192]{2,1,0:T(4,128)} %sum_over_blk.1), calls=%async_computation.1 | async-start | bytes 393216 | tf_op jit(solution)/shard_map/relay/all_to_all | solution.py:379

commit v6 on v5

--- a/solution.py
+++ b/solution.py
@@ -11,6 +11,7 @@
 CAP = 4
 LANES = 128
 CHUNK = 256
+SPARE = 8
 GROUP = 16
 TOGETHER = 16
 F32 = jnp.float32
@@ -130,7 +131,7 @@
         out_shape=(packed, packed),
         in_specs=[SMEM, SMEM] + [VMEM] * len(pieces),
         out_specs=(VMEM, VMEM),
-        scratch_shapes=[pltpu.VMEM((2 * total, LANES), F32), pltpu.VMEM((2 * count, LANES), F32)],
+        scratch_shapes=[pltpu.VMEM((2 * total + SPARE, LANES), F32), pltpu.VMEM((2 * count, LANES), F32)],
         compiler_params=pltpu.CompilerParams(vmem_limit_bytes=28 * 2**20),
     )(bases, rim, *pieces)
 
@@ -276,7 +277,7 @@
         in_specs=[SMEM] * 4 + [pl.BlockSpec(memory_space=pltpu.HBM)] + [VMEM] * (2 + len(pieces)),
         out_specs=VMEM,
         scratch_shapes=[
-            wide(2 * total), wide(count), wide(count), wide(2 * n_blocks * size),
+            wide(2 * total + SPARE), wide(count), wide(count), wide(2 * n_blocks * size + SPARE),
             pltpu.VMEM((2 * modes, 2 * LANES), F32), pltpu.VMEM((modes, LANES), F32),
             pltpu.VMEM(stiffness.shape, BF16), pltpu.SemaphoreType.DMA,
         ],

time: 153 us -> 154 us (level)
  no operation moved by 1% of the time
where the time goes in v6:
time: 154 us; the launch traced here: 153 us
  starting transfers between devices  64 us (42%)
  Pallas kernels  40.6 us (26%)
  waiting for transfers between devices  32 us (21%)
  blocking collectives  13.4 us (9%)
  local copies, waits for them, and re-layouts  2.55 us (2%)
    pallas_call x1, Pallas kernels, contract_blocks(): pl.pallas_call(functools.partial(main_kernel, slice_rows, len(pieces), sc...  30.8 us
    ppermute x8, starting transfers between devices, ring_pieces(): lax.ppermute(value, 'blk', [(i, (i // ring + dx) % 2 * ring + (i % ring +...  26.6 us
    all_to_all x1, starting transfers between devices, on_device(): arrived = lax.all_to_all(sent, 'sub', 0, 0, tiled=True)  20.1 us
    all_to_all x1, waiting for transfers between devices, on_device(): arrived = lax.all_to_all(sent, 'sub', 0, 0, tiled=True)  16.6 us
    all_to_all x1, blocking collectives, on_device(): lax.all_to_all(share, 'blk', 0, 0, tiled=True)  13.4 us
    ppermute x8, waiting for transfers between devices, ring_pieces(): lax.ppermute(value, 'blk', [(i, (i // ring + dx) % 2 * ring + (i % ring +...  13 us
    ppermute x1, starting transfers between devices, on_device(): lax.ppermute(right, 'sub', [(i, i + 1) for i in range(sub_count - 1)])  10.5 us
    pallas_call x1, Pallas kernels, take_rim(): pl.pallas_call(functools.partial(rim_kernel, slice_rows, len(pieces)), ou...  6.98 us
  transfers between devices with their start and end apart: 11, of which 7 were waited for; matrix products, arithmetic and copies ran while one was open for 0% of the time, Pallas kernels for 0%

profile of v6, /device:TPU:1, one launch (start us, length us, event | category | flops | bytes accessed | tf_op | source)
XLA Modules:
  0.0 153.0 jit_solution(6842657298365832842)
XLA Ops:
  0.0 0.0 copy-start
  0.0 0.9 copy-done
  0.9 0.1 pack.1
  1.0 3.9 %collective-permute-start = (bf16[512,128]{1,0:T(8,128)(2,1)S(1)}, bf16[512,128]{1,0:T(8,128)(2,1)S(1)}, u32[]{:S(2)}, u32[]{:S(2)}) collective-permute-start(bf16[512,128]{1,0:T(8,128)(2,1)S(1)} %pack.1), channel_id=1, source_target_pairs={{0,8},{1,9},{2,10},{3,11},{4,12},{5,13},{6,14},{7,15},{8,0},{9,1},... | collective-permute-start | bytes 393224 | tf_op jit(solution)/shard_map/gather_modes/ppermute | solution.py:336
  5.0 0.0 copy-start.1
  5.0 0.8 copy-done.1
  5.8 0.0 copy-start.2
  5.8 0.7 copy-done.2
  6.5 0.4 index_words.1
  6.9 0.4 collective-permute-done
  7.3 4.0 %collective-permute-start.1 = (bf16[1024,128]{1,0:T(8,128)(2,1)S(1)}, bf16[1024,128]{1,0:T(8,128)(2,1)S(1)}, u32[]{:S(2)}, u32[]{:S(2)}) collective-permute-start(bf16[1024,128]{1,0:T(8,128)(2,1)S(1)} %pad_maximum_fusion.refs_0_), channel_id=1, source_target_pairs={{0,1},{1,2},{2,3},{3,4},{4,5},{5,6},{6,7},{7,0},{8,9},{9,10},{10,1... | collective-permute-start | bytes 786440 | tf_op jit(solution)/shard_map/gather_modes/ppermute | solution.py:336
  11.3 3.8 %collective-permute-start.2 = (bf16[1024,128]{1,0:T(8,128)(2,1)S(1)}, bf16[1024,128]{1,0:T(8,128)(2,1)S(1)}, u32[]{:S(2)}, u32[]{:S(2)}) collective-permute-start(bf16[1024,128]{1,0:T(8,128)(2,1)S(1)} %pad_maximum_fusion.refs_0_), channel_id=1, source_target_pairs={{0,7},{1,0},{2,1},{3,2},{4,3},{5,4},{6,5},{7,6},{8,15},{9,8},{10,9... | collective-permute-start | bytes 786440 | tf_op jit(solution)/shard_map/gather_modes/ppermute | solution.py:336
  15.2 1.8 %collective-permute-done.1.refs_1_ = bf16[1024,128]{1,0:T(8,128)(2,1)S(1)} collective-permute-done((bf16[1024,128]{1,0:T(8,128)(2,1)S(1)}, bf16[1024,128]{1,0:T(8,128)(2,1)S(1)}, u32[]{:S(2)}, u32[]{:S(2)}) %collective-permute-start.1) | collective-permute-done | bytes 262176 | tf_op jit(solution)/shard_map/gather_modes/ppermute | solution.py:336
  17.0 1.9 %collective-permute-start.3 = (bf16[1024,128]{1,0:T(8,128)(2,1)S(1)}, bf16[1024,128]{1,0:T(8,128)(2,1)S(1)}, u32[]{:S(2)}, u32[]{:S(2)}) collective-permute-start(bf16[1024,128]{1,0:T(8,128)(2,1)S(1)} %collective-permute-done.1.refs_1_), channel_id=1, source_target_pairs={{0,1},{1,2},{2,3},{3,4},{4,5},{5,6},{6,7},{7,0},{8,9},{9,10},{10,1... | collective-permute-start | bytes 786440 | tf_op jit(solution)/shard_map/gather_modes/ppermute | solution.py:336
  18.9 0.0 collective-permute-done.2.refs_2_
  18.9 4.6 %collective-permute-start.4 = (bf16[1024,128]{1,0:T(8,128)(2,1)S(1)}, bf16[1024,128]{1,0:T(8,128)(2,1)S(1)}, u32[]{:S(2)}, u32[]{:S(2)}) collective-permute-start(bf16[1024,128]{1,0:T(8,128)(2,1)S(1)} %collective-permute-done.2.refs_2_), channel_id=1, source_target_pairs={{0,7},{1,0},{2,1},{3,2},{4,3},{5,4},{6,5},{7,6},{8,15},{9,8},{10,9... | collective-permute-start | bytes 786440 | tf_op jit(solution)/shard_map/gather_modes/ppermute | solution.py:336
  23.5 2.9 %collective-permute-done.3.refs_3_ = bf16[1024,128]{1,0:T(8,128)(2,1)S(1)} collective-permute-done((bf16[1024,128]{1,0:T(8,128)(2,1)S(1)}, bf16[1024,128]{1,0:T(8,128)(2,1)S(1)}, u32[]{:S(2)}, u32[]{:S(2)}) %collective-permute-start.3) | collective-permute-done | bytes 262176 | tf_op jit(solution)/shard_map/gather_modes/ppermute | solution.py:336
  26.4 1.9 %collective-permute-start.5 = (bf16[1024,128]{1,0:T(8,128)(2,1)S(1)}, bf16[1024,128]{1,0:T(8,128)(2,1)S(1)}, u32[]{:S(2)}, u32[]{:S(2)}) collective-permute-start(bf16[1024,128]{1,0:T(8,128)(2,1)S(1)} %collective-permute-done.3.refs_3_), channel_id=1, source_target_pairs={{0,1},{1,2},{2,3},{3,4},{4,5},{5,6},{6,7},{7,0},{8,9},{9,10},{10,1... | collective-permute-start | bytes 786440 | tf_op jit(solution)/shard_map/gather_modes/ppermute | solution.py:336
  28.3 0.0 collective-permute-done.4.refs_4_
  28.3 4.6 %collective-permute-start.6 = (bf16[1024,128]{1,0:T(8,128)(2,1)S(1)}, bf16[1024,128]{1,0:T(8,128)(2,1)S(1)}, u32[]{:S(2)}, u32[]{:S(2)}) collective-permute-start(bf16[1024,128]{1,0:T(8,128)(2,1)S(1)} %collective-permute-done.4.refs_4_), channel_id=1, source_target_pairs={{0,7},{1,0},{2,1},{3,2},{4,3},{5,4},{6,5},{7,6},{8,15},{9,8},{10,9... | collective-permute-start | bytes 786440 | tf_op jit(solution)/shard_map/gather_modes/ppermute | solution.py:336
  32.9 1.8 %collective-permute-done.5.refs_5_ = bf16[1024,128]{1,0:T(8,128)(2,1)S(1)} collective-permute-done((bf16[1024,128]{1,0:T(8,128)(2,1)S(1)}, bf16[1024,128]{1,0:T(8,128)(2,1)S(1)}, u32[]{:S(2)}, u32[]{:S(2)}) %collective-permute-start.5) | collective-permute-done | bytes 262176 | tf_op jit(solution)/shard_map/gather_modes/ppermute | solution.py:336
  34.7 1.9 %collective-permute-start.7 = (bf16[1024,128]{1,0:T(8,128)(2,1)S(1)}, bf16[1024,128]{1,0:T(8,128)(2,1)S(1)}, u32[]{:S(2)}, u32[]{:S(2)}) collective-permute-start(bf16[1024,128]{1,0:T(8,128)(2,1)S(1)} %collective-permute-done.5.refs_5_), channel_id=1, source_target_pairs={{0,1},{1,2},{2,3},{3,4},{4,5},{5,6},{6,7},{7,0},{8,9},{9,10},{10,1... | collective-permute-start | bytes 786440 | tf_op jit(solution)/shard_map/gather_modes/ppermute | solution.py:336
  36.8 0.1 stack.67
  37.0 0.0 collective-permute-done.6.refs_6_
  37.0 6.1 %collective-permute-done.7.refs_7_ = bf16[1024,128]{1,0:T(8,128)(2,1)S(1)} collective-permute-done((bf16[1024,128]{1,0:T(8,128)(2,1)S(1)}, bf16[1024,128]{1,0:T(8,128)(2,1)S(1)}, u32[]{:S(2)}, u32[]{:S(2)}) %collective-permute-start.7) | collective-permute-done | bytes 262176 | tf_op jit(solution)/shard_map/gather_modes/ppermute | solution.py:336
  43.0 7.0 %rim.1 = (bf16[1024,128]{1,0:T(8,128)(2,1)S(1)}, bf16[1024,128]{1,0:T(8,128)(2,1)S(1)}) custom-call(s32[16]{0:T(128)S(1)} %broadcast_multiply_fusion.base_ref, s32[16,128]{1,0:T(8,128)S(1)} %get-tuple-element.19.rim_ref, bf16[1024,128]{1,0:T(8,128)(2,1)S(1)} %pad_maximum_fusion.refs_0_, bf16[1024,128]{1,0:T(8,128)(2,1)S(1)} %collective-permute-done.1.refs_1_, ...), custom_call_target="tpu_custom_call" | custom-call | tf_op jit(solution)/shard_map/rim/pallas_call | solution.py:129
  50.0 0.0 copy-start.3
  50.0 10.5 %collective-permute-start.8 = (bf16[1024,128]{1,0:T(8,128)(2,1)S(1)}, bf16[1024,128]{1,0:T(8,128)(2,1)S(1)}, u32[]{:S(2)}, u32[]{:S(2)}) collective-permute-start(bf16[1024,128]{1,0:T(8,128)(2,1)S(1)} %get-tuple-element.23), channel_id=1, source_target_pairs={{0,16},{16,32},{32,48},{48,64},{64,80},{80,96},{96,112},{112,128},... | collective-permute-start | bytes 786440 | tf_op jit(solution)/shard_map/rim/ppermute | solution.py:370
  60.6 6.8 %collective-permute-start.9 = (bf16[1024,128]{1,0:T(8,128)(2,1)S(1)}, bf16[1024,128]{1,0:T(8,128)(2,1)S(1)}, u32[]{:S(2)}, u32[]{:S(2)}) collective-permute-start(bf16[1024,128]{1,0:T(8,128)(2,1)S(1)} %get-tuple-element.24), channel_id=1, source_target_pairs={{16,0},{32,16},{48,32},{64,48},{80,64},{96,80},{112,96},{128,112},... | collective-permute-start | bytes 786440 | tf_op jit(solution)/shard_map/rim/ppermute | solution.py:371
  67.4 0.0 collective-permute-done.8.from_left
  67.4 2.3 %collective-permute-done.9.from_right = bf16[1024,128]{1,0:T(8,128)(2,1)S(1)} collective-permute-done((bf16[1024,128]{1,0:T(8,128)(2,1)S(1)}, bf16[1024,128]{1,0:T(8,128)(2,1)S(1)}, u32[]{:S(2)}, u32[]{:S(2)}) %collective-permute-start.9) | collective-permute-done | bytes 262176 | tf_op jit(solution)/shard_map/rim/ppermute | solution.py:371
  69.8 30.8 %contract.1 = f32[16,4,192]{2,1,0:T(4,128)S(1)} custom-call(s32[16]{0:T(128)S(1)} %broadcast_multiply_fusion.base_ref, s32[16,128]{1,0:T(8,128)S(1)} %get-tuple-element.19.rim_ref, s32[16,128]{1,0:T(8,128)S(1)} %get-tuple-element.20.clash_ref, s32[128,128]{1,0:T(8,128)S(1)} %get-tuple-element.21.dof_ref, bf16[128,128,128]{2,1,0:T(8,128)(2,1)} %bitcast.24, ...), custom_call_target="tpu_custom_call" | custom-call | tf_op jit(solution)/shard_map/contract/pallas_call | solution.py:274
  100.6 13.4 %all_to_all.10.parts_ref = f32[16,4,192]{2,1,0:T(4,128)S(1)} all-to-all(f32[16,4,192]{2,1,0:T(4,128)S(1)} %contract.1), channel_id=1, replica_groups=mesh['sub'=48,'blk'=16] {'blk'}, dimensions={0} | all-to-all | bytes 98304 | tf_op jit(solution)/shard_map/sum_over_blk/all_to_all | solution.py:378
  114.0 0.7 sum_over_blk.1
  114.7 20.1 %all-to-all-start.1 = ((f32[48,4,192]{2,1,0:T(4,128)}), f32[48,4,192]{2,1,0:T(4,128)S(1)}, u32[]{:S(2)}, u32[]{:S(2)}) async-start(f32[48,4,192]{2,1,0:T(4,128)} %sum_over_blk.1), calls=%async_computation.1 | async-start | bytes 393216 | tf_op jit(solution)/shard_map/relay/all_to_all | solution.py:380
  134.8 16.6 %all-to-all-done.1.arrived_ref = f32[48,4,192]{2,1,0:T(4,128)S(1)} async-done(((f32[48,4,192]{2,1,0:T(4,128)}), f32[48,4,192]{2,1,0:T(4,128)S(1)}, u32[]{:S(2)}, u32[]{:S(2)}) %all-to-all-start.1) | async-done | bytes 147488 | tf_op jit(solution)/shard_map/relay/all_to_all | solution.py:380
  151.4 0.0 copy-done.3
  151.4 1.6 %slots.1 = f32[4,4,192]{2,1,0:T(4,128)} custom-call(s32[1]{0:T(128)} %bitcast.me_ref, s32[48]{0:T(128)S(1)} %copy-done.3, f32[48,4,192]{2,1,0:T(4,128)S(1)} %all-to-all-done.1.arrived_ref), custom_call_target="tpu_custom_call" | custom-call | tf_op jit(solution)/shard_map/slots/pallas_call | solution.py:325
  (2 shorter events, 0.0 us)
Async XLA Ops:
  0.0 0.9 copy-start
  1.0 6.3 %collective-permute-start = (bf16[512,128]{1,0:T(8,128)(2,1)S(1)}, bf16[512,128]{1,0:T(8,128)(2,1)S(1)}, u32[]{:S(2)}, u32[]{:S(2)}) collective-permute-start(bf16[512,128]{1,0:T(8,128)(2,1)S(1)} %pack.1), channel_id=1, source_target_pairs={{0,8},{1,9},{2,10},{3,11},{4,12},{5,13},{6,14},{7,15},{8,0},{9,1},... | collective-permute-start | bytes 393224 | tf_op jit(solution)/shard_map/gather_modes/ppermute | solution.py:336
  5.0 0.8 copy-start.1
  5.8 0.7 copy-start.2
  7.3 9.6 %collective-permute-start.1 = (bf16[1024,128]{1,0:T(8,128)(2,1)S(1)}, bf16[1024,128]{1,0:T(8,128)(2,1)S(1)}, u32[]{:S(2)}, u32[]{:S(2)}) collective-permute-start(bf16[1024,128]{1,0:T(8,128)(2,1)S(1)} %pad_maximum_fusion.refs_0_), channel_id=1, source_target_pairs={{0,1},{1,2},{2,3},{3,4},{4,5},{5,6},{6,7},{7,0},{8,9},{9,10},{10,1... | collective-permute-start | bytes 786440 | tf_op jit(solution)/shard_map/gather_modes/ppermute | solution.py:336
  11.3 7.6 %collective-permute-start.2 = (bf16[1024,128]{1,0:T(8,128)(2,1)S(1)}, bf16[1024,128]{1,0:T(8,128)(2,1)S(1)}, u32[]{:S(2)}, u32[]{:S(2)}) collective-permute-start(bf16[1024,128]{1,0:T(8,128)(2,1)S(1)} %pad_maximum_fusion.refs_0_), channel_id=1, source_target_pairs={{0,7},{1,0},{2,1},{3,2},{4,3},{5,4},{6,5},{7,6},{8,15},{9,8},{10,9... | collective-permute-start | bytes 786440 | tf_op jit(solution)/shard_map/gather_modes/ppermute | solution.py:336
  17.0 9.4 %collective-permute-start.3 = (bf16[1024,128]{1,0:T(8,128)(2,1)S(1)}, bf16[1024,128]{1,0:T(8,128)(2,1)S(1)}, u32[]{:S(2)}, u32[]{:S(2)}) collective-permute-start(bf16[1024,128]{1,0:T(8,128)(2,1)S(1)} %collective-permute-done.1.refs_1_), channel_id=1, source_target_pairs={{0,1},{1,2},{2,3},{3,4},{4,5},{5,6},{6,7},{7,0},{8,9},{9,10},{10,1... | collective-permute-start | bytes 786440 | tf_op jit(solution)/shard_map/gather_modes/ppermute | solution.py:336
  18.9 9.4 %collective-permute-start.4 = (bf16[1024,128]{1,0:T(8,128)(2,1)S(1)}, bf16[1024,128]{1,0:T(8,128)(2,1)S(1)}, u32[]{:S(2)}, u32[]{:S(2)}) collective-permute-start(bf16[1024,128]{1,0:T(8,128)(2,1)S(1)} %collective-permute-done.2.refs_2_), channel_id=1, source_target_pairs={{0,7},{1,0},{2,1},{3,2},{4,3},{5,4},{6,5},{7,6},{8,15},{9,8},{10,9... | collective-permute-start | bytes 786440 | tf_op jit(solution)/shard_map/gather_modes/ppermute | solution.py:336
  26.4 8.3 %collective-permute-start.5 = (bf16[1024,128]{1,0:T(8,128)(2,1)S(1)}, bf16[1024,128]{1,0:T(8,128)(2,1)S(1)}, u32[]{:S(2)}, u32[]{:S(2)}) collective-permute-start(bf16[1024,128]{1,0:T(8,128)(2,1)S(1)} %collective-permute-done.3.refs_3_), channel_id=1, source_target_pairs={{0,1},{1,2},{2,3},{3,4},{4,5},{5,6},{6,7},{7,0},{8,9},{9,10},{10,1... | collective-permute-start | bytes 786440 | tf_op jit(solution)/shard_map/gather_modes/ppermute | solution.py:336
  28.3 8.6 %collective-permute-start.6 = (bf16[1024,128]{1,0:T(8,128)(2,1)S(1)}, bf16[1024,128]{1,0:T(8,128)(2,1)S(1)}, u32[]{:S(2)}, u32[]{:S(2)}) collective-permute-start(bf16[1024,128]{1,0:T(8,128)(2,1)S(1)} %collective-permute-done.4.refs_4_), channel_id=1, source_target_pairs={{0,7},{1,0},{2,1},{3,2},{4,3},{5,4},{6,5},{7,6},{8,15},{9,8},{10,9... | collective-permute-start | bytes 786440 | tf_op jit(solution)/shard_map/gather_modes/ppermute | solution.py:336
  34.7 8.3 %collective-permute-start.7 = (bf16[1024,128]{1,0:T(8,128)(2,1)S(1)}, bf16[1024,128]{1,0:T(8,128)(2,1)S(1)}, u32[]{:S(2)}, u32[]{:S(2)}) collective-permute-start(bf16[1024,128]{1,0:T(8,128)(2,1)S(1)} %collective-permute-done.5.refs_5_), channel_id=1, source_target_pairs={{0,1},{1,2},{2,3},{3,4},{4,5},{5,6},{6,7},{7,0},{8,9},{9,10},{10,1... | collective-permute-start | bytes 786440 | tf_op jit(solution)/shard_map/gather_modes/ppermute | solution.py:336
  50.0 101.3 %copy-start.3 = (s32[48]{0:T(128)S(1)}, s32[48]{0:T(128)}, u32[]{:S(2)}) copy-start(s32[48]{0:T(128)} %owner_ref.1) | copy-start | bytes 580
  50.0 17.4 %collective-permute-start.8 = (bf16[1024,128]{1,0:T(8,128)(2,1)S(1)}, bf16[1024,128]{1,0:T(8,128)(2,1)S(1)}, u32[]{:S(2)}, u32[]{:S(2)}) collective-permute-start(bf16[1024,128]{1,0:T(8,128)(2,1)S(1)} %get-tuple-element.23), channel_id=1, source_target_pairs={{0,16},{16,32},{32,48},{48,64},{64,80},{80,96},{96,112},{112,128},... | collective-permute-start | bytes 786440 | tf_op jit(solution)/shard_map/rim/ppermute | solution.py:370
  60.6 9.2 %collective-permute-start.9 = (bf16[1024,128]{1,0:T(8,128)(2,1)S(1)}, bf16[1024,128]{1,0:T(8,128)(2,1)S(1)}, u32[]{:S(2)}, u32[]{:S(2)}) collective-permute-start(bf16[1024,128]{1,0:T(8,128)(2,1)S(1)} %get-tuple-element.24), channel_id=1, source_target_pairs={{16,0},{32,16},{48,32},{64,48},{80,64},{96,80},{112,96},{128,112},... | collective-permute-start | bytes 786440 | tf_op jit(solution)/shard_map/rim/ppermute | solution.py:371
  114.7 36.7 %all-to-all-start.1 = ((f32[48,4,192]{2,1,0:T(4,128)}), f32[48,4,192]{2,1,0:T(4,128)S(1)}, u32[]{:S(2)}, u32[]{:S(2)}) async-start(f32[48,4,192]{2,1,0:T(4,128)} %sum_over_blk.1), calls=%async_computation.1 | async-start | bytes 393216 | tf_op jit(solution)/shard_map/relay/all_to_all | solution.py:380
